TPU v7x, 32 devices: a whole 2x2x4 slice. The times are simulated.
32 devices in a mesh: replica: 8 (over z, core), tensor: 4 (over y, x).
Axes of the slice: x: 2, y: 2, z: 4, core: 2. Of those that a mesh axis runs over, the one named last changes fastest.
Arguments:
- tokens: bfloat16 [4096, 1024], P('replica'), may hold values from -6 to 6
- targets: bfloat16 [4096, 1024], P('replica'), may hold values from -6 to 6
- row_ids: int32 [8, 3, 512], P('replica'), may hold values from 0 to 511
- anchor: float32 [2, 1024, 4096], P(None, None, 'tensor'), may hold values from -0.1875 to 0.1875
- momentum: float32 [8, 2, 1024, 4096], P('replica', None, None, 'tensor'), may hold values from -4 to 4
- slow: float32 [2, 1024, 4096], P(None, None, 'tensor'), may hold values from -6 to 6
Outputs:
- anchor_new: float32 [2, 1024, 4096], P(None, None, 'tensor')
- slow_new: float32 [2, 1024, 4096], P(None, None, 'tensor')
- momentum_new: float32 [8, 2, 1024, 4096], P('replica', None, None, 'tensor')
Inputs may be any that keep to these rules, and one draw needn't show every extreme that they name: `row_ids`: each id names a row within its replica's own block of 512 rows; rows may repeat.
All inputs are finite; a program needn't handle non-finite values.
Results may differ from a plain program's by a relative error of at most 0.008.
Values may be sent and summed in bfloat16 or wider, within the bound.
No kernel may reach another device: no remote copies, remote signals or barrier semaphores. Data moves between devices by JAX's collectives and lax.ppermute only.
A program may use at most 128 MiB of HBM per device.

v0:
```python
import jax
import jax.numpy as jnp
from jax import lax
from jax.sharding import PartitionSpec as P

INNER = 3


learn_rate = 0.02
inner_beta = 0.9
slow_beta = 0.5


def passed_along(block, axis, distance):
    devices = range(lax.axis_size(axis))
    route = [((i - distance) % len(devices), i) for i in devices]
    return lax.ppermute(block, axis, route)


def gelu_pair(pre):
    coeff = 0.7978845608028654
    inner = coeff * (pre + 0.044715 * pre * pre * pre)
    tanh_val = jnp.tanh(inner)
    value = 0.5 * pre * (1.0 + tanh_val)
    slope = 0.5 * (1.0 + tanh_val) + 0.5 * pre * (1.0 - tanh_val * tanh_val) * coeff * (
        1.0 + 3.0 * 0.044715 * pre * pre
    )
    return (value, slope)


def body(tokens, targets, row_ids, anchor, momentum, slow):
    row_count = tokens.shape[0]
    scale = 1.0 / row_count
    weights = anchor
    moment = momentum[0]
    for step in range(INNER):
        if step > 0:
            incoming = passed_along(weights.astype(jnp.bfloat16), "replica", 2 ** (step - 1))
            weights = 0.5 * (weights + incoming.astype(jnp.float32))
        picks = row_ids[0, step]
        inputs = jnp.take(tokens, picks, axis=0)
        wanted = jnp.take(targets, picks, axis=0)
        weights_bf = weights.astype(jnp.bfloat16)
        pre = jnp.dot(inputs, weights_bf[0], preferred_element_type=jnp.float32)
        value, slope = gelu_pair(pre)
        hidden = value.astype(jnp.bfloat16)
        partial_out = lax.dot_general(
            hidden, weights_bf[1], (((1,), (1,)), ((), ())), preferred_element_type=jnp.float32
        )
        share = lax.psum_scatter(partial_out, "tensor", scatter_dimension=0, tiled=True)
        share_rows = share.shape[0]
        start = lax.axis_index("tensor") * share_rows
        wanted_share = lax.dynamic_slice_in_dim(wanted, start, share_rows, 0)
        error_share = ((share - wanted_share.astype(jnp.float32)) * scale).astype(jnp.bfloat16)
        error = lax.all_gather(error_share, "tensor", axis=0, tiled=True)
        back = (jnp.dot(error, weights_bf[1], preferred_element_type=jnp.float32) * slope).astype(
            jnp.bfloat16
        )
        grad_in = lax.dot_general(
            inputs, back, (((0,), (0,)), ((), ())), preferred_element_type=jnp.float32
        )
        grad_out = lax.dot_general(
            error, hidden, (((0,), (0,)), ((), ())), preferred_element_type=jnp.float32
        )
        moment = inner_beta * moment + jnp.stack([grad_in, grad_out])
        weights = weights - learn_rate * moment
    replicas = lax.axis_size("replica")
    total = lax.psum(weights, "replica")
    mean = total / replicas
    slow_new = slow_beta * slow + (anchor - mean) / learn_rate
    anchor_new = anchor - learn_rate * slow_new
    return (anchor_new, slow_new, moment[None])


def solution(mesh):
    return jax.shard_map(
        body,
        mesh=mesh,
        in_specs=(
            P("replica", None),
            P("replica", None),
            P("replica", None, None),
            P(None, None, "tensor"),
            P("replica", None, None, "tensor"),
            P(None, None, "tensor"),
        ),
        out_specs=(
            P(None, None, "tensor"),
            P(None, None, "tensor"),
            P("replica", None, None, "tensor"),
        ),
        check_vma=False,
    )
```

profile of v0, /device:TPU:0, one launch (start us, length us, event | category | flops | bytes accessed | tf_op | source)
XLA Modules:
  0.0 672.3 jit_solution(10556074730772822961)
XLA Ops:
  8.1 6.1 convert_element_type.57
  16.2 3.3 fusion.31
  26.9 34.8 %reduce-scatter.4.cloned.1.call-done = f32[128,1024]{1,0:T(8,128)} async-done(((f32[512,1024]{1,0:T(8,128)}), f32[128,1024]{1,0:T(8,128)}) %reduce-scatter.4.cloned.1.call-update) | async-done | bytes 524304 | tf_op jit(solution)/shard_map/reduce_scatter | solution.py:50
  63.7 27.3 %all-gather.4.cloned.1.call-done = bf16[512,1024]{1,0:T(8,128)(2,1)} async-done(((bf16[128,1024]{1,0:T(8,128)(2,1)}), bf16[512,1024]{1,0:T(8,128)(2,1)}) %all-gather.4.cloned.1.call-update) | async-done | bytes 1048592 | tf_op jit(solution)/shard_map/all_gather | solution.py:55
  90.9 8.1 %fusion.40 = f32[1024,1024]{1,0:T(8,128)} fusion(f32[512,1024]{1,0:T(8,128)} %copy-done.11, bf16[512,1024]{1,0:T(8,128)(2,1)} %all-gather.4.cloned.1.call-done, bf16[2,1024,1024]{2,1,0:T(8,128)(2,1)} %convert_element_type.57, bf16[512,1024]{1,0:T(8,128)(2,1)} %copy-done.15, pred[512]{0:T(512)(128)(4,1)S(1)} %compare_and_fusion.2), kind=kOutput, calls=%fused_computation.71 | convolution fusion | flops 2157969408 | bytes 10486272 | tf_op jit(solution)/shard_map/dot_general | solution.py:59
  99.1 3.2 fusion.78
  102.3 11.6 %fusion.62 = (bf16[2,1024,1024]{2,1,0:T(8,128)(2,1)}, f32[2,1024,1024]{2,1,0:T(8,128)}) fusion(f32[2,1024,1024]{2,1,0:T(8,128)} %param.11, f32[1,1024,1024]{2,1,0:T(8,128)S(1)} %bitcast.60, f32[1,1024,1024]{2,1,0:T(8,128)S(1)} %bitcast.68, f32[1,2,1024,1024]{3,2,1,0:T(8,128)} %param.12), kind=kLoop, calls=%fused_computation.111 | loop fusion | flops 12582912 | bytes 37748736 | tf_op jit(solution)/shard_map/convert_element_type | solution.py:38
  116.3 47.9 %collective-permute-done = bf16[2,1024,1024]{2,1,0:T(8,128)(2,1)} collective-permute-done((bf16[2,1024,1024]{2,1,0:T(8,128)(2,1)}, bf16[2,1024,1024]{2,1,0:T(8,128)(2,1)}, u32[]{:S(2)}, u32[]{:S(2)}) %collective-permute-start) | collective-permute-done | bytes 4194336 | tf_op jit(solution)/shard_map/ppermute | solution.py:17
  164.2 8.3 %fusion.6 = bf16[2,1024,1024]{2,1,0:T(8,128)(2,1)S(1)} fusion(bf16[2,1024,1024]{2,1,0:T(8,128)(2,1)} %collective-permute-done, f32[2,1024,1024]{2,1,0:T(8,128)} %param.11, f32[2,1024,1024]{2,1,0:T(8,128)} %get-tuple-element.9), kind=kLoop, calls=%fused_computation.22 | loop fusion | flops 12582912 | bytes 25165824 | tf_op jit(solution)/shard_map/convert_element_type | solution.py:43
  181.0 31.4 %reduce-scatter.6.cloned.1.call-done = f32[128,1024]{1,0:T(8,128)} async-done(((f32[512,1024]{1,0:T(8,128)}), f32[128,1024]{1,0:T(8,128)}) %reduce-scatter.6.cloned.1.call-update) | async-done | bytes 524304 | tf_op jit(solution)/shard_map/reduce_scatter | solution.py:50
  214.3 26.7 %all-gather.6.cloned.1.call-done = bf16[512,1024]{1,0:T(8,128)(2,1)} async-done(((bf16[128,1024]{1,0:T(8,128)(2,1)}), bf16[512,1024]{1,0:T(8,128)(2,1)}) %all-gather.6.cloned.1.call-update) | async-done | bytes 1048592 | tf_op jit(solution)/shard_map/all_gather | solution.py:55
  241.0 8.1 %fusion.39 = f32[1024,1024]{1,0:T(8,128)} fusion(f32[512,1024]{1,0:T(8,128)} %copy-done.14, bf16[512,1024]{1,0:T(8,128)(2,1)} %all-gather.6.cloned.1.call-done, bf16[2,1024,1024]{2,1,0:T(8,128)(2,1)} %copy-done.10, bf16[512,1024]{1,0:T(8,128)(2,1)} %copy-done.16, pred[512]{0:T(512)(128)(4,1)S(1)} %compare_and_fusion.1), kind=kOutput, calls=%fused_computation.70 | convolution fusion | flops 2157969408 | bytes 10486272 | tf_op jit(solution)/shard_map/dot_general | solution.py:59
  252.3 13.6 %fusion.81 = (bf16[2,1024,1024]{2,1,0:T(8,128)(2,1)}, f32[2,1024,1024]{2,1,0:T(8,128)}) fusion(f32[1,1024,1024]{2,1,0:T(8,128)S(1)} %bitcast.57, f32[1,1024,1024]{2,1,0:T(8,128)S(1)} %bitcast.64, f32[2,1024,1024]{2,1,0:T(8,128)} %get-tuple-element.9, bf16[2,1024,1024]{2,1,0:T(8,128)(2,1)} %collective-permute-done, f32[2,1024,1024]{2,1,0:T(8,128)} %param.11), kind=kLoop, calls=%fused_computation.130 | loop fusion | flops 23068672 | bytes 41943040 | tf_op jit(solution)/shard_map/convert_element_type | solution.py:38
  265.9 12.6 %collective-permute-start.1 = (bf16[2,1024,1024]{2,1,0:T(8,128)(2,1)}, bf16[2,1024,1024]{2,1,0:T(8,128)(2,1)}, u32[]{:S(2)}, u32[]{:S(2)}) collective-permute-start(bf16[2,1024,1024]{2,1,0:T(8,128)(2,1)} %get-tuple-element.6), channel_id=1, source_target_pairs={{24,0},{28,4},{0,8},{4,12},{8,16},{12,20},{16,24},{20,28},{25,1},{... | collective-permute-start | bytes 12582920 | tf_op jit(solution)/shard_map/ppermute | solution.py:17
  280.6 90.8 %collective-permute-done.1 = bf16[2,1024,1024]{2,1,0:T(8,128)(2,1)} collective-permute-done((bf16[2,1024,1024]{2,1,0:T(8,128)(2,1)}, bf16[2,1024,1024]{2,1,0:T(8,128)(2,1)}, u32[]{:S(2)}, u32[]{:S(2)}) %collective-permute-start.1) | collective-permute-done | bytes 4194336 | tf_op jit(solution)/shard_map/ppermute | solution.py:17
  371.4 6.2 fusion.7
  386.0 31.4 %reduce-scatter.8.cloned.1.call-done = f32[128,1024]{1,0:T(8,128)} async-done(((f32[512,1024]{1,0:T(8,128)}), f32[128,1024]{1,0:T(8,128)}) %reduce-scatter.8.cloned.1.call-update) | async-done | bytes 524304 | tf_op jit(solution)/shard_map/reduce_scatter | solution.py:50
  419.4 26.7 %all-gather.8.cloned.1.call-done = bf16[512,1024]{1,0:T(8,128)(2,1)} async-done(((bf16[128,1024]{1,0:T(8,128)(2,1)}), bf16[512,1024]{1,0:T(8,128)(2,1)}) %all-gather.8.cloned.1.call-update) | async-done | bytes 1048592 | tf_op jit(solution)/shard_map/all_gather | solution.py:55
  446.1 7.7 %fusion.38 = f32[1024,1024]{1,0:T(8,128)} fusion(f32[512,1024]{1,0:T(8,128)} %copy-done.12, bf16[512,1024]{1,0:T(8,128)(2,1)} %all-gather.8.cloned.1.call-done, bf16[2,1024,1024]{2,1,0:T(8,128)(2,1)} %copy-done.9, bf16[512,1024]{1,0:T(8,128)(2,1)S(1)} %gather_fusion.4, pred[512]{0:T(512)(128)(4,1)S(1)} %compare_and_fusion), kind=kOutput, calls=%fused_computation.69 | convolution fusion | flops 2157969408 | bytes 10486272 | tf_op jit(solution)/shard_map/dot_general | solution.py:59
  453.8 4.8 fusion.80
  458.6 16.6 %fusion.1 = f32[2,1024,1024]{2,1,0:T(8,128)} fusion(f32[1,1024,1024]{2,1,0:T(8,128)} %bitcast.65, f32[1,1024,1024]{2,1,0:T(8,128)} %bitcast.69, f32[2,1024,1024]{2,1,0:T(8,128)} %get-tuple-element.7, bf16[2,1024,1024]{2,1,0:T(8,128)(2,1)} %collective-permute-done.1, f32[1,1024,1024]{2,1,0:T(8,128)S(1)} %bitcast.59, f32[1,1024,1024]{2,1,0:T(8,128)} %bitcast.62, ...), kind=kLoop, calls=%fused_computation.10 | loop fusion | flops 23068672 | bytes 46137344 | tf_op jit(solution)/shard_map/sub | solution.py:66
  475.2 17.6 %fusion.5 = f32[1,2,1024,1024]{3,2,1,0:T(8,128)} fusion(f32[1,1,1024,1024]{3,2,1,0:T(8,128)} %bitcast.61, f32[1,1,1024,1024]{3,2,1,0:T(8,128)} %bitcast.67, f32[1,1,1024,1024]{3,2,1,0:T(8,128)} %bitcast.58, f32[1,1,1024,1024]{3,2,1,0:T(8,128)} %bitcast.63, f32[1,1,1024,1024]{3,2,1,0:T(8,128)} %bitcast.66, f32[1,1,1024,1024]{3,2,1,0:T(8,128)} %bitcast.70, ...), kind=kLoop, calls=%fused_computation.15 | loop fusion | flops 18874368 | bytes 41943040 | tf_op jit(solution)/shard_map/add | solution.py:65
  492.8 158.1 %all-reduce.2.cloned.1.call-done = f32[2,1024,1024]{2,1,0:T(8,128)} async-done(((f32[2,1024,1024]{2,1,0:T(8,128)}), f32[2,1024,1024]{2,1,0:T(8,128)}) %all-reduce.2.cloned.1.call-update) | async-done | bytes 8388624 | tf_op jit(solution)/shard_map/psum | solution.py:68
  650.9 14.3 %multiply_subtract_fusion = (f32[2,1024,1024]{2,1,0:T(8,128)}, f32[2,1024,1024]{2,1,0:T(8,128)}) fusion(f32[2,1024,1024]{2,1,0:T(8,128)} %param.11, f32[2,1024,1024]{2,1,0:T(8,128)} %all-reduce.2.cloned.1.call-done, f32[2,1024,1024]{2,1,0:T(8,128)} %param.13), kind=kLoop, calls=%fused_computation.16 | loop fusion | flops 14680064 | bytes 41943040 | tf_op jit(solution)/shard_map/sub | solution.py:71
  (81 shorter events, 40.5 us)
Async XLA Ops:
  7.2 7.0 %copy-start = (bf16[512,1024]{1,0:T(8,128)(2,1)S(1)}, bf16[512,1024]{1,0:T(8,128)(2,1)}, u32[]{:S(2)}) copy-start(bf16[512,1024]{1,0:T(8,128)(2,1)} %param.8) | copy-start | bytes 3145732
  7.2 54.5 %reduce-scatter.4.cloned.1.call-start = ((), (), s32[]{:S(2)}) async-start(), calls=%async_computation.3 | async-start | bytes 2621440 | tf_op jit(solution)/shard_map/reduce_scatter | solution.py:50
  16.2 3.4 copy-start.15
  16.2 4.7 copy-start.8
  23.7 67.3 %all-gather.4.cloned.1.call-start = ((), (), s32[]{:S(2)}) async-start(), calls=%async_computation.4 | async-start | bytes 1310720 | tf_op jit(solution)/shard_map/all_gather | solution.py:55
  63.6 148.7 %reduce-scatter.6.cloned.1.call-start = ((), (), s32[]{:S(2)}) async-start(), calls=%async_computation.5 | async-start | bytes 2621440 | tf_op jit(solution)/shard_map/reduce_scatter | solution.py:50
  90.9 8.1 %copy-start.17 = (bf16[512,1024]{1,0:T(8,128)(2,1)S(1)}, bf16[512,1024]{1,0:T(8,128)(2,1)}, u32[]{:S(2)}) copy-start(bf16[512,1024]{1,0:T(8,128)(2,1)} %all-gather.4.cloned.1.call-done) | copy-start | bytes 3145732
  99.1 3.2 copy-start.7
  102.2 11.7 %copy-start.5 = (f32[1024,1024]{1,0:T(8,128)}, f32[1024,1024]{1,0:T(8,128)S(1)}, u32[]{:S(2)}) copy-start(f32[1024,1024]{1,0:T(8,128)S(1)} %fusion.78) | copy-start | bytes 12582916
  113.9 50.3 %collective-permute-start = (bf16[2,1024,1024]{2,1,0:T(8,128)(2,1)}, bf16[2,1024,1024]{2,1,0:T(8,128)(2,1)}, u32[]{:S(2)}, u32[]{:S(2)}) collective-permute-start(bf16[2,1024,1024]{2,1,0:T(8,128)(2,1)} %get-tuple-element.8), channel_id=1, source_target_pairs={{28,0},{0,4},{4,8},{8,12},{12,16},{16,20},{20,24},{24,28},{29,1},{... | collective-permute-start | bytes 12582920 | tf_op jit(solution)/shard_map/ppermute | solution.py:17
  116.2 56.3 %copy-start.16 = (bf16[512,1024]{1,0:T(8,128)(2,1)}, bf16[512,1024]{1,0:T(8,128)(2,1)S(1)}, u32[]{:S(2)}) copy-start(bf16[512,1024]{1,0:T(8,128)(2,1)S(1)} %gather_fusion.2) | copy-start | bytes 3145732
  172.5 2.0 copy-start.10
  178.8 62.3 %all-gather.6.cloned.1.call-start = ((), (), s32[]{:S(2)}) async-start(), calls=%async_computation.6 | async-start | bytes 1310720 | tf_op jit(solution)/shard_map/all_gather | solution.py:55
  214.3 203.1 %reduce-scatter.8.cloned.1.call-start = ((), (), s32[]{:S(2)}) async-start(), calls=%async_computation.7 | async-start | bytes 2621440 | tf_op jit(solution)/shard_map/reduce_scatter | solution.py:50
  241.0 8.1 %copy-start.18 = (bf16[512,1024]{1,0:T(8,128)(2,1)S(1)}, bf16[512,1024]{1,0:T(8,128)(2,1)}, u32[]{:S(2)}) copy-start(bf16[512,1024]{1,0:T(8,128)(2,1)} %all-gather.6.cloned.1.call-done) | copy-start | bytes 3145732
  249.1 3.2 copy-start.6
  252.3 13.6 %copy-start.3 = (f32[1024,1024]{1,0:T(8,128)}, f32[1024,1024]{1,0:T(8,128)S(1)}, u32[]{:S(2)}) copy-start(f32[1024,1024]{1,0:T(8,128)S(1)} %fusion.79) | copy-start | bytes 12582916
  265.9 105.6 %collective-permute-start.1 = (bf16[2,1024,1024]{2,1,0:T(8,128)(2,1)}, bf16[2,1024,1024]{2,1,0:T(8,128)(2,1)}, u32[]{:S(2)}, u32[]{:S(2)}) collective-permute-start(bf16[2,1024,1024]{2,1,0:T(8,128)(2,1)} %get-tuple-element.6), channel_id=1, source_target_pairs={{24,0},{28,4},{0,8},{4,12},{8,16},{12,20},{16,24},{20,28},{25,1},{... | collective-permute-start | bytes 12582920 | tf_op jit(solution)/shard_map/ppermute | solution.py:17
  377.6 2.0 copy-start.9
  383.8 62.3 %all-gather.8.cloned.1.call-start = ((), (), s32[]{:S(2)}) async-start(), calls=%async_computation.8 | async-start | bytes 1310720 | tf_op jit(solution)/shard_map/all_gather | solution.py:55
  419.3 34.5 %copy-start.13 = (f32[512,1024]{1,0:T(8,128)S(1)}, f32[512,1024]{1,0:T(8,128)}, u32[]{:S(2)}) copy-start(f32[512,1024]{1,0:T(8,128)} %copy-done.12) | copy-start | bytes 6291460
  419.3 231.6 %all-reduce.2.cloned.1.call-start = ((), (), s32[]{:S(2)}) async-start(), calls=%async_computation.9 | async-start | bytes 16777216 | tf_op jit(solution)/shard_map/psum | solution.py:68
  453.8 4.8 copy-start.4
  650.9 14.3 %copy-start.1 = (bf16[512,1024]{1,0:T(8,128)(2,1)S(1)}, bf16[512,1024]{1,0:T(8,128)(2,1)}, u32[]{:S(2)}) copy-start(bf16[512,1024]{1,0:T(8,128)(2,1)} %param.8) | copy-start | bytes 3145732
  (4 other events, 5.3 us)
Sparse Core Ops, SparseCore 0:
  23.8 37.8 reduce-scatter.3
  64.3 26.6 all-gather.3
  178.9 33.3 reduce-scatter.5
  214.4 26.6 all-gather.5
  384.0 33.3 reduce-scatter.7
  419.4 26.6 all-gather.7
  475.4 175.5 all-reduce.1
where the time goes:
time: 675 us; the launch traced here: 672 us
  waiting for transfers between devices  475 us (70%)
  other arithmetic  100 us (15%)
  matrix products  49.3 us (7%)
  local copies, waits for them, and re-layouts  20 us (3%)
  between operations  14.6 us (2%)
  starting transfers between devices  13.1 us (2%)
    psum x1, waiting for transfers between devices, body(): total = lax.psum(weights, 'replica')  158 us
    ppermute x2, waiting for transfers between devices, passed_along(): return lax.ppermute(block, axis, route)  139 us
    reduce_scatter x3, waiting for transfers between devices, body(): lax.psum_scatter(partial_out, 'tensor', scatter_dimension=0, tiled=True)  97.5 us
    all_gather x3, waiting for transfers between devices, body(): error = lax.all_gather(error_share, 'tensor', axis=0, tiled=True)  80.7 us
    convert_element_type x2, other arithmetic, body(): weights.astype(jnp.bfloat16)  25.2 us
    dot_general x3, matrix products, body(): lax.dot_general(inputs, back, (((0,), (0,)), ((), ())), preferred_element...  23.9 us
    convert_element_type x3, other arithmetic, body(): weights_bf = weights.astype(jnp.bfloat16)  20.6 us
    add x1, other arithmetic, body(): moment = inner_beta * moment + jnp.stack([grad_in, grad_out])  17.6 us
  transfers between devices with their start and end apart: 9, of which 9 were waited for; matrix products, arithmetic and copies ran while one was open for 4% of the time, Pallas kernels for 0%

commit v1 on v0

--- a/solution.py
+++ b/solution.py
@@ -9,12 +9,17 @@
 learn_rate = 0.02
 inner_beta = 0.9
 slow_beta = 0.5
+chunks = 4
 
 
 def passed_along(block, axis, distance):
     devices = range(lax.axis_size(axis))
     route = [((i - distance) % len(devices), i) for i in devices]
     return lax.ppermute(block, axis, route)
+
+
+def swapped(block, axis, mask):
+    return lax.ppermute(block, axis, [(i, i ^ mask) for i in range(lax.axis_size(axis))])
 
 
 def gelu_pair(pre):
@@ -28,18 +33,65 @@
     return (value, slope)
 
 
+def rounded(value):
+    return lax.reduce_precision(value, 8, 7).astype(jnp.bfloat16)
+
+
+def added(left, right):
+    return rounded(left.astype(jnp.float32) + right.astype(jnp.float32))
+
+
+def line_sum(block, axis):
+    cores = 2
+    length = lax.axis_size(axis) // cores
+    chip = lax.axis_index(axis) // cores
+
+    def moved(part, hops):
+        return lax.ppermute(part, axis, [(cores * a + c, cores * b + c) for a, b in hops for c in range(cores)])
+
+    half = length // 2
+    for s in range(half - 1):
+        block = added(block, moved(block, [(s, s + 1), (length - 1 - s, length - 2 - s)]))
+    if half:
+        block = added(block, moved(block, [(half - 1, half), (half, half - 1)]))
+    for s in reversed(range(half - 1)):
+        arrived = moved(block, [(s + 1, s), (length - 2 - s, length - 1 - s)])
+        block = jnp.where((chip == s) | (chip == length - 1 - s), arrived, block)
+    return block
+
+
+def replica_sum(total):
+    core = lax.axis_index("replica") % 2
+    mine = lax.dynamic_index_in_dim(total, core, 0, keepdims=False)
+    other = lax.dynamic_index_in_dim(total, 1 - core, 0, keepdims=False)
+    size = mine.shape[0] // chunks
+    sums = []
+    for c in range(chunks):
+        part = slice(c * size, (c + 1) * size)
+        pair = added(mine[part], swapped(rounded(other[part]), "replica", 1))
+        own = line_sum(pair, "replica")
+        theirs = swapped(own, "replica", 1)
+        sums.append(jnp.stack([jnp.where(core == 0, own, theirs), jnp.where(core == 0, theirs, own)]))
+    return jnp.concatenate(sums, axis=1)
+
+
 def body(tokens, targets, row_ids, anchor, momentum, slow):
     row_count = tokens.shape[0]
     scale = 1.0 / row_count
+    tensors = lax.axis_size("tensor")
+    share_rows = row_count // tensors
+    order = lax.axis_index("tensor") ^ jnp.arange(tensors)
+    picks_all = row_ids[0].reshape(INNER, tensors, share_rows)[:, order].reshape(INNER, row_count)
     weights = anchor
     moment = momentum[0]
+    total = 0.0
     for step in range(INNER):
         if step > 0:
             incoming = passed_along(weights.astype(jnp.bfloat16), "replica", 2 ** (step - 1))
             weights = 0.5 * (weights + incoming.astype(jnp.float32))
-        picks = row_ids[0, step]
-        inputs = jnp.take(tokens, picks, axis=0)
-        wanted = jnp.take(targets, picks, axis=0)
+        picks = picks_all[step]
+        inputs = tokens.at[picks].get(mode="promise_in_bounds")
+        wanted = targets.at[picks[:share_rows]].get(mode="promise_in_bounds")
         weights_bf = weights.astype(jnp.bfloat16)
         pre = jnp.dot(inputs, weights_bf[0], preferred_element_type=jnp.float32)
         value, slope = gelu_pair(pre)
@@ -47,12 +99,12 @@
         partial_out = lax.dot_general(
             hidden, weights_bf[1], (((1,), (1,)), ((), ())), preferred_element_type=jnp.float32
         )
-        share = lax.psum_scatter(partial_out, "tensor", scatter_dimension=0, tiled=True)
-        share_rows = share.shape[0]
-        start = lax.axis_index("tensor") * share_rows
-        wanted_share = lax.dynamic_slice_in_dim(wanted, start, share_rows, 0)
-        error_share = ((share - wanted_share.astype(jnp.float32)) * scale).astype(jnp.bfloat16)
-        error = lax.all_gather(error_share, "tensor", axis=0, tiled=True)
+        share = partial_out[:share_rows]
+        for m in range(1, tensors):
+            piece = partial_out[m * share_rows : (m + 1) * share_rows].astype(jnp.bfloat16)
+            share = share + swapped(piece, "tensor", m).astype(jnp.float32)
+        error_share = ((share - wanted.astype(jnp.float32)) * scale).astype(jnp.bfloat16)
+        error = jnp.concatenate([error_share] + [swapped(error_share, "tensor", m) for m in range(1, tensors)])
         back = (jnp.dot(error, weights_bf[1], preferred_element_type=jnp.float32) * slope).astype(
             jnp.bfloat16
         )
@@ -64,10 +116,10 @@
         )
         moment = inner_beta * moment + jnp.stack([grad_in, grad_out])
         weights = weights - learn_rate * moment
+        total = total + moment
     replicas = lax.axis_size("replica")
-    total = lax.psum(weights, "replica")
-    mean = total / replicas
-    slow_new = slow_beta * slow + (anchor - mean) / learn_rate
+    mean_total = replica_sum(total).astype(jnp.float32) / replicas
+    slow_new = slow_beta * slow + mean_total
     anchor_new = anchor - learn_rate * slow_new
     return (anchor_new, slow_new, moment[None])
 

time: 675 us -> 469 us (0.69)
  waiting for transfers between devices: 475 us -> 257 us
  starting transfers between devices: 13.1 us -> 47.9 us
  between operations: 14.6 us -> 1.74 us
  other arithmetic: 100 us -> 87.5 us
    psum x1 -> x0, waiting for transfers between devices: 158 us -> none  [body(): total = lax.psum(weights, 'replica')]
    ppermute x0 -> x38, waiting for transfers between devices: none -> 125 us  [the longest x12 70.1 us: moved(): lax.ppermute(part, axis, [(cores * a + c, cores * b + c) for a, b in hops...]
    reduce_scatter x3 -> x0, waiting for transfers between devices: 97.5 us -> none  [body(): lax.psum_scatter(partial_out, 'tensor', scatter_dimension=0, tiled=True)]
    all_gather x3 -> x0, waiting for transfers between devices: 80.7 us -> none  [body(): error = lax.all_gather(error_share, 'tensor', axis=0, tiled=True)]
    ppermute x0 -> x38, starting transfers between devices: none -> 43.9 us  [the longest x26 24 us: swapped(): lax.ppermute(block, axis, [(i, i ^ mask) for i in range(lax.axis_size(axi...]
    sub x1 -> x0, other arithmetic: 16.6 us -> none  [body(): weights = weights - learn_rate * moment]
    ppermute x2, starting transfers between devices: 12.9 us -> 3.92 us  [passed_along(): return lax.ppermute(block, axis, route)]
    add x0 -> x1, other arithmetic: none -> 6.98 us  [body(): total = total + moment]
  transfers between devices with their start and end apart: 9 -> 40, of which waited for: 9 -> 25; matrix products, arithmetic and copies ran while one was open for 4% -> 5% of each run, Pallas kernels for 0% -> 0%
where the time goes in v1:
time: 469 us; the launch traced here: 461 us
  waiting for transfers between devices  257 us (55%)
  other arithmetic  87.5 us (19%)
  starting transfers between devices  47.9 us (10%)
  matrix products  46.9 us (10%)
  local copies, waits for them, and re-layouts  20.2 us (4%)
    ppermute x2, waiting for transfers between devices, passed_along(): return lax.ppermute(block, axis, route)  133 us
    ppermute x12, waiting for transfers between devices, moved(): lax.ppermute(part, axis, [(cores * a + c, cores * b + c) for a, b in hops...  70.1 us
    ppermute x26, waiting for transfers between devices, swapped(): lax.ppermute(block, axis, [(i, i ^ mask) for i in range(lax.axis_size(axi...  54.5 us
    convert_element_type x2, other arithmetic, body(): weights.astype(jnp.bfloat16)  25.1 us
    ppermute x26, starting transfers between devices, swapped(): lax.ppermute(block, axis, [(i, i ^ mask) for i in range(lax.axis_size(axi...  24 us
    dot_general x3, matrix products, body(): lax.dot_general(inputs, back, (((0,), (0,)), ((), ())), preferred_element...  23.1 us
    convert_element_type x3, other arithmetic, body(): weights_bf = weights.astype(jnp.bfloat16)  20.6 us
    ppermute x12, starting transfers between devices, moved(): lax.ppermute(part, axis, [(cores * a + c, cores * b + c) for a, b in hops...  19.9 us
  transfers between devices with their start and end apart: 40, of which 25 were waited for; matrix products, arithmetic and copies ran while one was open for 5% of the time, Pallas kernels for 0%

profile of v1, /device:TPU:0, one launch (start us, length us, event | category | flops | bytes accessed | tf_op | source)
XLA Modules:
  0.0 461.3 jit_solution(17364277043529936507)
XLA Ops:
  2.1 6.1 %convert_element_type.216 = bf16[2,1024,1024]{2,1,0:T(8,128)(2,1)} convert(f32[2,1024,1024]{2,1,0:T(8,128)} %param.9) | non-fusion elementwise | flops 2097152 | bytes 12582912 | tf_op jit(solution)/shard_map/convert_element_type | solution.py:95
  22.2 5.0 %collective-permute-done = bf16[128,1024]{1,0:T(8,128)(2,1)} collective-permute-done((bf16[128,1024]{1,0:T(8,128)(2,1)}, bf16[128,1024]{1,0:T(8,128)(2,1)}, u32[]{:S(2)}, u32[]{:S(2)}) %collective-permute-start) | collective-permute-done | bytes 262176 | tf_op jit(solution)/shard_map/ppermute | solution.py:22
  27.2 6.3 %collective-permute-done.1 = bf16[128,1024]{1,0:T(8,128)(2,1)} collective-permute-done((bf16[128,1024]{1,0:T(8,128)(2,1)}, bf16[128,1024]{1,0:T(8,128)(2,1)}, u32[]{:S(2)}, u32[]{:S(2)}) %collective-permute-start.1) | collective-permute-done | bytes 262176 | tf_op jit(solution)/shard_map/ppermute | solution.py:22
  38.6 5.7 %collective-permute-done.3 = bf16[128,1024]{1,0:T(8,128)(2,1)S(1)} collective-permute-done((bf16[128,1024]{1,0:T(8,128)(2,1)S(1)}, bf16[128,1024]{1,0:T(8,128)(2,1)S(1)}, u32[]{:S(2)}, u32[]{:S(2)}) %collective-permute-start.3) | collective-permute-done | bytes 262176 | tf_op jit(solution)/shard_map/ppermute | solution.py:22
  49.5 7.8 %fusion.39 = f32[1024,1024]{1,0:T(8,128)} fusion(bf16[512,1024]{1,0:T(8,128)(2,1)S(1)} %gather_fusion.1, f32[512,1024]{1,0:T(8,128)} %copy-done.25, bf16[2,1024,1024]{2,1,0:T(8,128)(2,1)} %convert_element_type.216, bf16[128,1024]{1,0:T(8,128)(2,1)} %collective-permute-done.5, bf16[128,1024]{1,0:T(8,128)(2,1)} %copy-done.22, ...), kind=kOutput, calls=%fused_computation.71 | convolution fusion | flops 2161639424 | bytes 10485760 | tf_op jit(solution)/shard_map/dot_general | solution.py:111
  60.7 11.6 %fusion.6 = (bf16[2,1024,1024]{2,1,0:T(8,128)(2,1)}, f32[2,1024,1024]{2,1,0:T(8,128)}) fusion(f32[2,1024,1024]{2,1,0:T(8,128)} %param.9, f32[1,1024,1024]{2,1,0:T(8,128)S(1)} %bitcast.163, f32[1,1024,1024]{2,1,0:T(8,128)S(1)} %bitcast.162, f32[1,2,1024,1024]{3,2,1,0:T(8,128)} %param.10), kind=kLoop, calls=%fused_computation.29 | loop fusion | flops 12582912 | bytes 37748736 | tf_op jit(solution)/shard_map/convert_element_type | solution.py:90
  74.6 47.9 %collective-permute-done.6 = bf16[2,1024,1024]{2,1,0:T(8,128)(2,1)} collective-permute-done((bf16[2,1024,1024]{2,1,0:T(8,128)(2,1)}, bf16[2,1024,1024]{2,1,0:T(8,128)(2,1)}, u32[]{:S(2)}, u32[]{:S(2)}) %collective-permute-start.6) | collective-permute-done | bytes 4194336 | tf_op jit(solution)/shard_map/ppermute | solution.py:18
  122.5 8.3 %fusion.5 = bf16[2,1024,1024]{2,1,0:T(8,128)(2,1)S(1)} fusion(bf16[2,1024,1024]{2,1,0:T(8,128)(2,1)} %collective-permute-done.6, f32[2,1024,1024]{2,1,0:T(8,128)} %param.9, f32[2,1024,1024]{2,1,0:T(8,128)} %get-tuple-element.8), kind=kLoop, calls=%fused_computation.22 | loop fusion | flops 12582912 | bytes 25165824 | tf_op jit(solution)/shard_map/convert_element_type | solution.py:95
  161.8 7.9 %fusion.38 = f32[1024,1024]{1,0:T(8,128)} fusion(bf16[512,1024]{1,0:T(8,128)(2,1)S(1)} %gather_fusion.3, f32[512,1024]{1,0:T(8,128)} %copy-done.26, bf16[2,1024,1024]{2,1,0:T(8,128)(2,1)} %copy-done.15, bf16[128,1024]{1,0:T(8,128)(2,1)} %collective-permute-done.12, bf16[128,1024]{1,0:T(8,128)(2,1)} %copy-done.23, bf16[128,1024]{1,0:T(8,128)(2,1)} %copy-done.21, ...), kind=kOutput, calls=%fused_computation.70 | convolution fusion | flops 2161639424 | bytes 10485760 | tf_op jit(solution)/shard_map/dot_general | solution.py:111
  173.1 13.5 %fusion.121 = (bf16[2,1024,1024]{2,1,0:T(8,128)(2,1)}, f32[2,1024,1024]{2,1,0:T(8,128)}) fusion(f32[1,1024,1024]{2,1,0:T(8,128)S(1)} %bitcast.158, f32[1,1024,1024]{2,1,0:T(8,128)S(1)} %bitcast.155, f32[2,1024,1024]{2,1,0:T(8,128)} %get-tuple-element.8, bf16[2,1024,1024]{2,1,0:T(8,128)(2,1)} %collective-permute-done.6, f32[2,1024,1024]{2,1,0:T(8,128)} %param.9), kind=kLoop, calls=%fused_computation.204 | loop fusion | flops 23068672 | bytes 41943040 | tf_op jit(solution)/shard_map/convert_element_type | solution.py:90
  192.4 84.6 %collective-permute-done.13 = bf16[2,1024,1024]{2,1,0:T(8,128)(2,1)} collective-permute-done((bf16[2,1024,1024]{2,1,0:T(8,128)(2,1)}, bf16[2,1024,1024]{2,1,0:T(8,128)(2,1)}, u32[]{:S(2)}, u32[]{:S(2)}) %collective-permute-start.13) | collective-permute-done | bytes 4194336 | tf_op jit(solution)/shard_map/ppermute | solution.py:18
  277.0 6.2 %multiply_convert_fusion = bf16[2,1024,1024]{2,1,0:T(8,128)(2,1)S(1)} fusion(f32[2,1024,1024]{2,1,0:T(8,128)} %get-tuple-element.6, bf16[2,1024,1024]{2,1,0:T(8,128)(2,1)} %collective-permute-done.13), kind=kLoop, calls=%fused_computation.18 | loop fusion | flops 8388608 | bytes 16777216 | tf_op jit(solution)/shard_map/convert_element_type | solution.py:95
  311.8 7.5 %fusion.37 = f32[1024,1024]{1,0:T(8,128)} fusion(bf16[512,1024]{1,0:T(8,128)(2,1)S(1)} %gather_fusion.5, f32[512,1024]{1,0:T(8,128)} %copy-done.24, bf16[2,1024,1024]{2,1,0:T(8,128)(2,1)} %copy-done.14, bf16[128,1024]{1,0:T(8,128)(2,1)S(1)} %collective-permute-done.19, bf16[128,1024]{1,0:T(8,128)(2,1)S(1)} %collective-permute-done.18, ...), kind=kOutput, calls=%fused_computation.69 | convolution fusion | flops 2161639424 | bytes 10485760 | tf_op jit(solution)/shard_map/dot_general | solution.py:111
  323.4 7.0 %fusion = f32[2,1024,1024]{2,1,0:T(8,128)S(1)} fusion(f32[1,1024,1024]{2,1,0:T(8,128)S(1)} %bitcast.167, f32[1,1024,1024]{2,1,0:T(8,128)} %bitcast.165, f32[2,1024,1024]{2,1,0:T(8,128)} %get-tuple-element.8, f32[1,1024,1024]{2,1,0:T(8,128)S(1)} %bitcast.159, f32[1,1024,1024]{2,1,0:T(8,128)S(1)} %bitcast.156), kind=kLoop, calls=%fused_computation.10 | loop fusion | flops 16777216 | bytes 33554432 | tf_op jit(solution)/shard_map/add | solution.py:119
  342.3 7.8 %collective-permute-start.21 = (bf16[256,1024]{1,0:T(8,128)(2,1)S(1)}, bf16[256,1024]{1,0:T(8,128)(2,1)S(1)}, u32[]{:S(2)}, u32[]{:S(2)}) collective-permute-start(bf16[256,1024]{1,0:T(8,128)(2,1)S(1)} %get-tuple-element.9), channel_id=1, source_target_pairs={{0,8},{4,12},{24,16},{28,20},{1,9},{5,13},{25,17},{29,21},{2,10},{... | collective-permute-start | bytes 1572872 | tf_op jit(solution)/shard_map/ppermute | solution.py:50
  351.5 13.3 %fusion.4 = f32[1,2,1024,1024]{3,2,1,0:T(8,128)} fusion(f32[1,1,1024,1024]{3,2,1,0:T(8,128)} %bitcast.164, f32[1,1,1024,1024]{3,2,1,0:T(8,128)} %bitcast.161, f32[1,1,1024,1024]{3,2,1,0:T(8,128)S(1)} %bitcast.160, f32[1,1,1024,1024]{3,2,1,0:T(8,128)S(1)} %bitcast.157, f32[1,1,1024,1024]{3,2,1,0:T(8,128)} %bitcast.168, f32[1,1,1024,1024]{3,2,1,0:T(8,128)} %bitcast.166, ...), kind=kLoop, calls=%fused_computation.15 | loop fusion | flops 18874368 | bytes 41943040 | tf_op jit(solution)/shard_map/add | solution.py:117
  368.3 5.3 %collective-permute-done.26 = bf16[256,1024]{1,0:T(8,128)(2,1)S(1)} collective-permute-done((bf16[256,1024]{1,0:T(8,128)(2,1)S(1)}, bf16[256,1024]{1,0:T(8,128)(2,1)S(1)}, u32[]{:S(2)}, u32[]{:S(2)}) %collective-permute-start.26) | collective-permute-done | bytes 524320 | tf_op jit(solution)/shard_map/ppermute | solution.py:50
  374.5 10.3 %collective-permute-done.31 = bf16[256,1024]{1,0:T(8,128)(2,1)S(1)} collective-permute-done((bf16[256,1024]{1,0:T(8,128)(2,1)S(1)}, bf16[256,1024]{1,0:T(8,128)(2,1)S(1)}, u32[]{:S(2)}, u32[]{:S(2)}) %collective-permute-start.31) | collective-permute-done | bytes 524320 | tf_op jit(solution)/shard_map/ppermute | solution.py:50
  385.7 9.5 %collective-permute-done.36 = bf16[256,1024]{1,0:T(8,128)(2,1)S(1)} collective-permute-done((bf16[256,1024]{1,0:T(8,128)(2,1)S(1)}, bf16[256,1024]{1,0:T(8,128)(2,1)S(1)}, u32[]{:S(2)}, u32[]{:S(2)}) %collective-permute-start.36) | collective-permute-done | bytes 524320 | tf_op jit(solution)/shard_map/ppermute | solution.py:50
  402.5 13.4 %collective-permute-done.23 = bf16[256,1024]{1,0:T(8,128)(2,1)S(1)} collective-permute-done((bf16[256,1024]{1,0:T(8,128)(2,1)S(1)}, bf16[256,1024]{1,0:T(8,128)(2,1)S(1)}, u32[]{:S(2)}, u32[]{:S(2)}) %collective-permute-start.23) | collective-permute-done | bytes 524320 | tf_op jit(solution)/shard_map/ppermute | solution.py:50
  416.0 11.1 %collective-permute-done.28 = bf16[256,1024]{1,0:T(8,128)(2,1)S(1)} collective-permute-done((bf16[256,1024]{1,0:T(8,128)(2,1)S(1)}, bf16[256,1024]{1,0:T(8,128)(2,1)S(1)}, u32[]{:S(2)}, u32[]{:S(2)}) %collective-permute-start.28) | collective-permute-done | bytes 524320 | tf_op jit(solution)/shard_map/ppermute | solution.py:50
  427.2 11.1 %collective-permute-done.33 = bf16[256,1024]{1,0:T(8,128)(2,1)S(1)} collective-permute-done((bf16[256,1024]{1,0:T(8,128)(2,1)S(1)}, bf16[256,1024]{1,0:T(8,128)(2,1)S(1)}, u32[]{:S(2)}, u32[]{:S(2)}) %collective-permute-start.33) | collective-permute-done | bytes 524320 | tf_op jit(solution)/shard_map/ppermute | solution.py:50
  438.5 9.4 %collective-permute-done.38 = bf16[256,1024]{1,0:T(8,128)(2,1)S(1)} collective-permute-done((bf16[256,1024]{1,0:T(8,128)(2,1)S(1)}, bf16[256,1024]{1,0:T(8,128)(2,1)S(1)}, u32[]{:S(2)}, u32[]{:S(2)}) %collective-permute-start.38) | collective-permute-done | bytes 524320 | tf_op jit(solution)/shard_map/ppermute | solution.py:50
  450.9 9.9 %multiply_subtract_fusion = (f32[2,1024,1024]{2,1,0:T(8,128)}, f32[2,1024,1024]{2,1,0:T(8,128)}) fusion(f32[2,1024,1024]{2,1,0:T(8,128)S(1)} %bitcast.154, bf16[1,256,1024]{2,1,0:T(8,128)(2,1)} %get-tuple-element.24, bf16[1,256,1024]{2,1,0:T(8,128)(2,1)} %get-tuple-element.23, bf16[1,256,1024]{2,1,0:T(8,128)(2,1)S(1)} %get-tuple-element.22, ...), kind=kLoop, calls=%fused_computation.16 | loop fusion | flops 44040192 | bytes 37748736 | tf_op jit(solution)/shard_map/sub | solution.py:123
  (177 shorter events, 133.1 us)
Async XLA Ops:
  16.9 10.4 %collective-permute-start = (bf16[128,1024]{1,0:T(8,128)(2,1)}, bf16[128,1024]{1,0:T(8,128)(2,1)}, u32[]{:S(2)}, u32[]{:S(2)}) collective-permute-start(bf16[128,1024]{1,0:T(8,128)(2,1)} %get-tuple-element.31), channel_id=1, source_target_pairs={{0,1},{1,0},{2,3},{3,2},{4,5},{5,4},{6,7},{7,6},{8,9},{9,8},{10,11... | collective-permute-start | bytes 786440 | tf_op jit(solution)/shard_map/ppermute | solution.py:22
  19.8 13.7 %collective-permute-start.1 = (bf16[128,1024]{1,0:T(8,128)(2,1)}, bf16[128,1024]{1,0:T(8,128)(2,1)}, u32[]{:S(2)}, u32[]{:S(2)}) collective-permute-start(bf16[128,1024]{1,0:T(8,128)(2,1)} %get-tuple-element.33), channel_id=1, source_target_pairs={{0,2},{1,3},{2,0},{3,1},{4,6},{5,7},{6,4},{7,5},{8,10},{9,11},{10,... | collective-permute-start | bytes 786440 | tf_op jit(solution)/shard_map/ppermute | solution.py:22
  21.3 12.2 %collective-permute-start.2 = (bf16[128,1024]{1,0:T(8,128)(2,1)}, bf16[128,1024]{1,0:T(8,128)(2,1)}, u32[]{:S(2)}, u32[]{:S(2)}) collective-permute-start(bf16[128,1024]{1,0:T(8,128)(2,1)} %get-tuple-element.32), channel_id=1, source_target_pairs={{0,3},{1,2},{2,1},{3,0},{4,7},{5,6},{6,5},{7,4},{8,11},{9,10},{10,... | collective-permute-start | bytes 786440 | tf_op jit(solution)/shard_map/ppermute | solution.py:22
  36.3 12.5 %collective-permute-start.4 = (bf16[128,1024]{1,0:T(8,128)(2,1)S(1)}, bf16[128,1024]{1,0:T(8,128)(2,1)S(1)}, u32[]{:S(2)}, u32[]{:S(2)}) collective-permute-start(bf16[128,1024]{1,0:T(8,128)(2,1)S(1)} %fusion.89), channel_id=1, source_target_pairs={{0,2},{1,3},{2,0},{3,1},{4,6},{5,7},{6,4},{7,5},{8,10},{9,11},{10,... | collective-permute-start | bytes 786440 | tf_op jit(solution)/shard_map/ppermute | solution.py:22
  37.1 12.4 %collective-permute-start.5 = (bf16[128,1024]{1,0:T(8,128)(2,1)S(1)}, bf16[128,1024]{1,0:T(8,128)(2,1)}, u32[]{:S(2)}, u32[]{:S(2)}) collective-permute-start(bf16[128,1024]{1,0:T(8,128)(2,1)S(1)} %fusion.89), channel_id=1, source_target_pairs={{0,3},{1,2},{2,1},{3,0},{4,7},{5,6},{6,5},{7,4},{8,11},{9,10},{10,... | collective-permute-start | bytes 786440 | tf_op jit(solution)/shard_map/ppermute | solution.py:22
  72.4 50.2 %collective-permute-start.6 = (bf16[2,1024,1024]{2,1,0:T(8,128)(2,1)}, bf16[2,1024,1024]{2,1,0:T(8,128)(2,1)}, u32[]{:S(2)}, u32[]{:S(2)}) collective-permute-start(bf16[2,1024,1024]{2,1,0:T(8,128)(2,1)} %get-tuple-element.7), channel_id=1, source_target_pairs={{28,0},{0,4},{4,8},{8,12},{12,16},{16,20},{20,24},{24,28},{29,1},{... | collective-permute-start | bytes 12582920 | tf_op jit(solution)/shard_map/ppermute | solution.py:18
  137.2 11.3 %collective-permute-start.8 = (bf16[128,1024]{1,0:T(8,128)(2,1)}, bf16[128,1024]{1,0:T(8,128)(2,1)}, u32[]{:S(2)}, u32[]{:S(2)}) collective-permute-start(bf16[128,1024]{1,0:T(8,128)(2,1)} %get-tuple-element.30), channel_id=1, source_target_pairs={{0,2},{1,3},{2,0},{3,1},{4,6},{5,7},{6,4},{7,5},{8,10},{9,11},{10,... | collective-permute-start | bytes 786440 | tf_op jit(solution)/shard_map/ppermute | solution.py:22
  137.8 10.6 %collective-permute-start.9 = (bf16[128,1024]{1,0:T(8,128)(2,1)}, bf16[128,1024]{1,0:T(8,128)(2,1)}, u32[]{:S(2)}, u32[]{:S(2)}) collective-permute-start(bf16[128,1024]{1,0:T(8,128)(2,1)} %get-tuple-element.29), channel_id=1, source_target_pairs={{0,3},{1,2},{2,1},{3,0},{4,7},{5,6},{6,5},{7,4},{8,11},{9,10},{10,... | collective-permute-start | bytes 786440 | tf_op jit(solution)/shard_map/ppermute | solution.py:22
  152.0 9.8 %collective-permute-start.12 = (bf16[128,1024]{1,0:T(8,128)(2,1)S(1)}, bf16[128,1024]{1,0:T(8,128)(2,1)}, u32[]{:S(2)}, u32[]{:S(2)}) collective-permute-start(bf16[128,1024]{1,0:T(8,128)(2,1)S(1)} %fusion.84), channel_id=1, source_target_pairs={{0,3},{1,2},{2,1},{3,0},{4,7},{5,6},{6,5},{7,4},{8,11},{9,10},{10,... | collective-permute-start | bytes 786440 | tf_op jit(solution)/shard_map/ppermute | solution.py:22
  186.6 90.4 %collective-permute-start.13 = (bf16[2,1024,1024]{2,1,0:T(8,128)(2,1)}, bf16[2,1024,1024]{2,1,0:T(8,128)(2,1)}, u32[]{:S(2)}, u32[]{:S(2)}) collective-permute-start(bf16[2,1024,1024]{2,1,0:T(8,128)(2,1)} %get-tuple-element.5), channel_id=1, source_target_pairs={{24,0},{28,4},{0,8},{4,12},{8,16},{12,20},{16,24},{20,28},{25,1},{... | collective-permute-start | bytes 12582920 | tf_op jit(solution)/shard_map/ppermute | solution.py:18
  342.3 25.1 %collective-permute-start.21 = (bf16[256,1024]{1,0:T(8,128)(2,1)S(1)}, bf16[256,1024]{1,0:T(8,128)(2,1)S(1)}, u32[]{:S(2)}, u32[]{:S(2)}) collective-permute-start(bf16[256,1024]{1,0:T(8,128)(2,1)S(1)} %get-tuple-element.9), channel_id=1, source_target_pairs={{0,8},{4,12},{24,16},{28,20},{1,9},{5,13},{25,17},{29,21},{2,10},{... | collective-permute-start | bytes 1572872 | tf_op jit(solution)/shard_map/ppermute | solution.py:50
  350.1 23.5 %collective-permute-start.26 = (bf16[256,1024]{1,0:T(8,128)(2,1)S(1)}, bf16[256,1024]{1,0:T(8,128)(2,1)S(1)}, u32[]{:S(2)}, u32[]{:S(2)}) collective-permute-start(bf16[256,1024]{1,0:T(8,128)(2,1)S(1)} %get-tuple-element.11), channel_id=1, source_target_pairs={{0,8},{4,12},{24,16},{28,20},{1,9},{5,13},{25,17},{29,21},{2,10},{... | collective-permute-start | bytes 1572872 | tf_op jit(solution)/shard_map/ppermute | solution.py:50
  364.8 20.1 %collective-permute-start.31 = (bf16[256,1024]{1,0:T(8,128)(2,1)S(1)}, bf16[256,1024]{1,0:T(8,128)(2,1)S(1)}, u32[]{:S(2)}, u32[]{:S(2)}) collective-permute-start(bf16[256,1024]{1,0:T(8,128)(2,1)S(1)} %get-tuple-element.10), channel_id=1, source_target_pairs={{0,8},{4,12},{24,16},{28,20},{1,9},{5,13},{25,17},{29,21},{2,10},{... | collective-permute-start | bytes 1572872 | tf_op jit(solution)/shard_map/ppermute | solution.py:50
  366.1 29.2 %collective-permute-start.36 = (bf16[256,1024]{1,0:T(8,128)(2,1)S(1)}, bf16[256,1024]{1,0:T(8,128)(2,1)S(1)}, u32[]{:S(2)}, u32[]{:S(2)}) collective-permute-start(bf16[256,1024]{1,0:T(8,128)(2,1)S(1)} %get-tuple-element.12), channel_id=1, source_target_pairs={{0,8},{4,12},{24,16},{28,20},{1,9},{5,13},{25,17},{29,21},{2,10},{... | collective-permute-start | bytes 1572872 | tf_op jit(solution)/shard_map/ppermute | solution.py:50
  367.6 28.5 %collective-permute-start.22 = (bf16[256,1024]{1,0:T(8,128)(2,1)S(1)}, bf16[256,1024]{1,0:T(8,128)(2,1)S(1)}, u32[]{:S(2)}, u32[]{:S(2)}) collective-permute-start(bf16[256,1024]{1,0:T(8,128)(2,1)S(1)} %reduce-precision_convert_fusion.7), channel_id=1, source_target_pairs={{8,16},{12,20},{16,8},{20,12},{9,17},{13,21},{17,9},{21,13},{10,18... | collective-permute-start | bytes 1572872 | tf_op jit(solution)/shard_map/ppermute | solution.py:50
  373.8 23.9 %collective-permute-start.27 = (bf16[256,1024]{1,0:T(8,128)(2,1)S(1)}, bf16[256,1024]{1,0:T(8,128)(2,1)S(1)}, u32[]{:S(2)}, u32[]{:S(2)}) collective-permute-start(bf16[256,1024]{1,0:T(8,128)(2,1)S(1)} %reduce-precision_convert_fusion.5), channel_id=1, source_target_pairs={{8,16},{12,20},{16,8},{20,12},{9,17},{13,21},{17,9},{21,13},{10,18... | collective-permute-start | bytes 1572872 | tf_op jit(solution)/shard_map/ppermute | solution.py:50
  385.0 14.2 %collective-permute-start.32 = (bf16[256,1024]{1,0:T(8,128)(2,1)S(1)}, bf16[256,1024]{1,0:T(8,128)(2,1)S(1)}, u32[]{:S(2)}, u32[]{:S(2)}) collective-permute-start(bf16[256,1024]{1,0:T(8,128)(2,1)S(1)} %reduce-precision_convert_fusion.3), channel_id=1, source_target_pairs={{8,16},{12,20},{16,8},{20,12},{9,17},{13,21},{17,9},{21,13},{10,18... | collective-permute-start | bytes 1572872 | tf_op jit(solution)/shard_map/ppermute | solution.py:50
  396.4 19.5 %collective-permute-start.23 = (bf16[256,1024]{1,0:T(8,128)(2,1)S(1)}, bf16[256,1024]{1,0:T(8,128)(2,1)S(1)}, u32[]{:S(2)}, u32[]{:S(2)}) collective-permute-start(bf16[256,1024]{1,0:T(8,128)(2,1)S(1)} %reduce-precision_convert_fusion.6), channel_id=1, source_target_pairs={{8,0},{12,4},{16,24},{20,28},{9,1},{13,5},{17,25},{21,29},{10,2},{... | collective-permute-start | bytes 1572872 | tf_op jit(solution)/shard_map/ppermute | solution.py:50
  397.9 29.2 %collective-permute-start.28 = (bf16[256,1024]{1,0:T(8,128)(2,1)S(1)}, bf16[256,1024]{1,0:T(8,128)(2,1)S(1)}, u32[]{:S(2)}, u32[]{:S(2)}) collective-permute-start(bf16[256,1024]{1,0:T(8,128)(2,1)S(1)} %reduce-precision_convert_fusion.4), channel_id=1, source_target_pairs={{8,0},{12,4},{16,24},{20,28},{9,1},{13,5},{17,25},{21,29},{10,2},{... | collective-permute-start | bytes 1572872 | tf_op jit(solution)/shard_map/ppermute | solution.py:50
  399.4 38.9 %collective-permute-start.33 = (bf16[256,1024]{1,0:T(8,128)(2,1)S(1)}, bf16[256,1024]{1,0:T(8,128)(2,1)S(1)}, u32[]{:S(2)}, u32[]{:S(2)}) collective-permute-start(bf16[256,1024]{1,0:T(8,128)(2,1)S(1)} %reduce-precision_convert_fusion.2), channel_id=1, source_target_pairs={{8,0},{12,4},{16,24},{20,28},{9,1},{13,5},{17,25},{21,29},{10,2},{... | collective-permute-start | bytes 1572872 | tf_op jit(solution)/shard_map/ppermute | solution.py:50
  401.2 46.7 %collective-permute-start.38 = (bf16[256,1024]{1,0:T(8,128)(2,1)S(1)}, bf16[256,1024]{1,0:T(8,128)(2,1)S(1)}, u32[]{:S(2)}, u32[]{:S(2)}) collective-permute-start(bf16[256,1024]{1,0:T(8,128)(2,1)S(1)} %reduce-precision_convert_fusion), channel_id=1, source_target_pairs={{8,0},{12,4},{16,24},{20,28},{9,1},{13,5},{17,25},{21,29},{10,2},{... | collective-permute-start | bytes 1572872 | tf_op jit(solution)/shard_map/ppermute | solution.py:50
  415.9 32.1 %collective-permute-start.24 = (bf16[256,1024]{1,0:T(8,128)(2,1)S(1)}, bf16[256,1024]{1,0:T(8,128)(2,1)S(1)}, u32[]{:S(2)}, u32[]{:S(2)}) collective-permute-start(bf16[256,1024]{1,0:T(8,128)(2,1)S(1)} %broadcast_select_fusion.3), channel_id=1, source_target_pairs={{0,4},{4,0},{8,12},{12,8},{16,20},{20,16},{24,28},{28,24},{1,5},{5... | collective-permute-start | bytes 1572872 | tf_op jit(solution)/shard_map/ppermute | solution.py:22
  427.2 20.9 %collective-permute-start.29 = (bf16[256,1024]{1,0:T(8,128)(2,1)S(1)}, bf16[256,1024]{1,0:T(8,128)(2,1)S(1)}, u32[]{:S(2)}, u32[]{:S(2)}) collective-permute-start(bf16[256,1024]{1,0:T(8,128)(2,1)S(1)} %broadcast_select_fusion.2), channel_id=1, source_target_pairs={{0,4},{4,0},{8,12},{12,8},{16,20},{20,16},{24,28},{28,24},{1,5},{5... | collective-permute-start | bytes 1572872 | tf_op jit(solution)/shard_map/ppermute | solution.py:22
  438.4 9.8 %collective-permute-start.34 = (bf16[256,1024]{1,0:T(8,128)(2,1)S(1)}, bf16[256,1024]{1,0:T(8,128)(2,1)S(1)}, u32[]{:S(2)}, u32[]{:S(2)}) collective-permute-start(bf16[256,1024]{1,0:T(8,128)(2,1)S(1)} %broadcast_select_fusion.1), channel_id=1, source_target_pairs={{0,4},{4,0},{8,12},{12,8},{16,20},{20,16},{24,28},{28,24},{1,5},{5... | collective-permute-start | bytes 1572872 | tf_op jit(solution)/shard_map/ppermute | solution.py:22
  (45 other events, 331.4 us)

commit v2 on v0

v2 whole, which is shorter than its diff:
```python
import functools

import jax
import jax.numpy as jnp
from jax import lax
from jax.experimental import pallas as pl
from jax.experimental.pallas import tpu as pltpu
from jax.sharding import PartitionSpec as P

INNER = 3


learn_rate = 0.02
inner_beta = 0.9
slow_beta = 0.5
chunks = 8
bf16, f32 = jnp.bfloat16, jnp.float32


def passed_along(block, axis, distance):
    devices = range(lax.axis_size(axis))
    route = [((i - distance) % len(devices), i) for i in devices]
    return lax.ppermute(block, axis, route)


def swapped(block, axis, mask):
    return lax.ppermute(block, axis, [(i, i ^ mask) for i in range(lax.axis_size(axis))])


def gelu_pair(pre):
    coeff = 0.7978845608028654
    square = pre * pre
    tanh_val = jnp.tanh(coeff * (pre + 0.044715 * square * pre))
    half = 0.5 * (1.0 + tanh_val)
    slope = half + 0.5 * pre * (1.0 - tanh_val * tanh_val) * coeff * (1.0 + 3.0 * 0.044715 * square)
    return (pre * half, slope)


def whole(shape):
    return pl.BlockSpec(shape, lambda j: (0,) * len(shape))


def forward_kernel(mixes, inputs, weights, *refs):
    if mixes:
        incoming, hidden, slope, partial, mixed, total = refs
        block = (0.5 * (weights[...].astype(f32) + incoming[...].astype(f32))).astype(bf16)
        mixed[...] = block
    else:
        hidden, slope, partial, total = refs
        block = weights[...].astype(bf16)
    j = pl.program_id(0)
    value, slope_val = gelu_pair(jnp.dot(inputs[...], block[0], preferred_element_type=f32))
    value = value.astype(bf16)
    hidden[...] = value
    slope[...] = slope_val.astype(bf16)
    out = lax.dot_general(value, block[1], (((1,), (1,)), ((), ())), preferred_element_type=f32)

    @pl.when(j == 0)
    def _():
        total[...] = out

    @pl.when(j > 0)
    def _():
        total[...] += out

    @pl.when(j == pl.num_programs(0) - 1)
    def _():
        partial[...] = total[...].astype(bf16)


def forward(inputs, weights, incoming=None):
    rows, width = inputs.shape
    units = weights.shape[2]
    block = min(units, 512)
    mixes = incoming is not None
    weight_spec = pl.BlockSpec((2, width, block), lambda j: (0, 0, j))
    unit_spec = pl.BlockSpec((rows, block), lambda j: (0, j))
    shapes = [((rows, units), unit_spec), ((rows, units), unit_spec), ((rows, width), whole((rows, width)))]
    if mixes:
        shapes.append((weights.shape, weight_spec))
    return pl.pallas_call(
        functools.partial(forward_kernel, mixes),
        grid=(units // block,),
        in_specs=[whole((rows, width)), weight_spec] + [weight_spec] * mixes,
        out_specs=[spec for _, spec in shapes],
        out_shape=[jax.ShapeDtypeStruct(shape, bf16) for shape, _ in shapes],
        scratch_shapes=[pltpu.VMEM((rows, width), f32)],
        compiler_params=pltpu.CompilerParams(vmem_limit_bytes=40 << 20),
        cost_estimate=pl.CostEstimate(
            flops=4 * rows * width * units, bytes_accessed=8 * width * units, transcendentals=rows * units
        ),
    )(inputs, weights, *([incoming] if mixes else []))


def backward_kernel(update, taken, error, weights, slope, hidden, inputs_t, *refs):
    states, results, error_t = refs[:taken], refs[taken:-1], refs[-1]

    @pl.when(pl.program_id(0) == 0)
    def _():
        error_t[...] = error[...].T

    back = jnp.dot(error[...], weights[0].astype(bf16), preferred_element_type=f32) * slope[...].astype(f32)
    for k, (left, right) in enumerate(((inputs_t[...], back.astype(bf16)), (error_t[...], hidden[...]))):
        grad = jnp.dot(left, right, preferred_element_type=f32)
        values = update(grad, *[state[k].astype(f32) for state in states])
        for result, value in zip(results, values):
            result[k] = value.astype(result.dtype)


def backward(error, weights, slope, hidden, inputs_t, states, update, kinds):
    rows, width = error.shape
    units = weights.shape[2]
    block = min(units, 512)
    both = pl.BlockSpec((2, width, block), lambda j: (0, 0, j))
    out_only = pl.BlockSpec((1, width, block), lambda j: (1, 0, j))
    unit_spec = pl.BlockSpec((rows, block), lambda j: (0, j))
    return pl.pallas_call(
        functools.partial(backward_kernel, update, len(states)),
        grid=(units // block,),
        in_specs=[whole((rows, width)), out_only, unit_spec, unit_spec, whole((width, rows))] + [both] * len(states),
        out_specs=[both] * len(kinds),
        out_shape=[jax.ShapeDtypeStruct(weights.shape, kind) for kind in kinds],
        scratch_shapes=[pltpu.VMEM((width, rows), bf16)],
        compiler_params=pltpu.CompilerParams(vmem_limit_bytes=56 << 20),
        cost_estimate=pl.CostEstimate(
            flops=6 * rows * width * units, bytes_accessed=28 * width * units, transcendentals=0
        ),
    )(error, weights, slope, hidden, inputs_t, *states)


def first_update(grad, moment, weights):
    moment = inner_beta * moment + grad
    return (moment, weights - learn_rate * moment)


def second_update(grad, moment, weights):
    moment_new = inner_beta * moment + grad
    return (moment_new, weights - learn_rate * moment_new, moment + (1.0 + inner_beta) * moment_new)


def third_update(grad, moment, known):
    return (inner_beta * moment + grad, known + grad)


def rounded(value):
    return lax.reduce_precision(value, 8, 7).astype(bf16)


def added(left, right):
    return rounded(left.astype(f32) + right.astype(f32))


def tied(early, late):
    return lax.optimization_barrier((early, late))[1]


def replica_sum(total):
    axis, cores = "replica", 2
    index = lax.axis_index(axis)
    core, chip = index % cores, index // cores
    length = lax.axis_size(axis) // cores
    half = length // 2
    mine = lax.dynamic_index_in_dim(total, core, 0, keepdims=False)
    other = lax.dynamic_index_in_dim(total, 1 - core, 0, keepdims=False)
    size = mine.shape[0] // chunks

    def moved(part, hops):
        return lax.ppermute(part, axis, [(cores * a + c, cores * b + c) for a, b in hops for c in range(cores)])

    stages = [("add", [(s, s + 1), (length - 1 - s, length - 2 - s)]) for s in range(half - 1)]
    if half:
        stages.append(("add", [(half - 1, half), (half, half - 1)]))
    stages += [("take", [(s + 1, s), (length - 2 - s, length - 1 - s)]) for s in reversed(range(half - 1))]

    blocks = []
    for c in range(chunks):
        part = slice(c * size, (c + 1) * size)
        blocks.append(added(mine[part], swapped(other[part], axis, 1)))
    ticks = []
    for tick in range(chunks + 2 * (len(stages) - 1)):
        work = [(tick - 2 * s, s) for s in range(len(stages)) if 0 <= tick - 2 * s < chunks]
        if tick >= 2:
            held = tied(ticks[tick - 2], [blocks[c] for c, _ in work])
            for (c, _), block in zip(work, held):
                blocks[c] = block
        arrivals = [moved(blocks[c], stages[s][1]) for c, s in work]
        ticks.append(arrivals)
        for (c, s), arrived in zip(work, arrivals):
            kind, hops = stages[s]
            if kind == "add":
                blocks[c] = added(blocks[c], arrived)
            else:
                landed = functools.reduce(jnp.logical_or, [chip == b for _, b in hops])
                blocks[c] = jnp.where(landed, arrived, blocks[c])
    sums = []
    for own in blocks:
        theirs = swapped(own, axis, 1)
        sums.append(jnp.stack([jnp.where(core == 0, own, theirs), jnp.where(core == 0, theirs, own)]))
    return jnp.concatenate(sums, axis=1)


def body(tokens, targets, row_ids, anchor, momentum, slow):
    row_count = tokens.shape[0]
    scale = 1.0 / row_count
    tensors = lax.axis_size("tensor")
    share_rows = row_count // tensors
    order = lax.axis_index("tensor") ^ jnp.arange(tensors)
    picks_all = row_ids[0].reshape(INNER, tensors, share_rows)[:, order].reshape(INNER, row_count)

    def error_of(partial, step):
        wanted = targets.at[picks_all[step, :share_rows]].get(mode="promise_in_bounds")
        share = partial[:share_rows].astype(f32)
        for m in range(1, tensors):
            share = share + swapped(partial[m * share_rows : (m + 1) * share_rows], "tensor", m).astype(f32)
        own = ((share - wanted.astype(f32)) * scale).astype(bf16)
        return jnp.concatenate([own] + [swapped(own, "tensor", m) for m in range(1, tensors)])

    inputs = [tokens.at[picks_all[step]].get(mode="promise_in_bounds") for step in range(INNER)]
    inputs_t = [block.T for block in inputs]

    hidden, slope, partial = forward(inputs[0], anchor)
    error = error_of(partial, 0)
    moment, weights = backward(
        error, anchor, slope, hidden, inputs_t[0], [momentum[0], anchor], first_update, [f32, bf16]
    )
    incoming = passed_along(weights, "replica", 1)
    hidden, slope, partial, weights = forward(inputs[1], weights, incoming)
    error = error_of(partial, 1)
    moment, weights, known = backward(
        error, weights, slope, hidden, inputs_t[1], [moment, weights], second_update, [f32, bf16, bf16]
    )
    incoming = passed_along(weights, "replica", 2)
    hidden, slope, partial, weights = forward(inputs[2], weights, incoming)
    error = error_of(partial, 2)
    moment, total = backward(
        error, weights, slope, hidden, inputs_t[2], [moment, known], third_update, [f32, bf16]
    )
    mean_total = replica_sum(total).astype(f32) / lax.axis_size("replica")
    slow_new = slow_beta * slow + mean_total
    anchor_new = anchor - learn_rate * slow_new
    return (anchor_new, slow_new, moment[None])


def solution(mesh):
    return jax.shard_map(
        body,
        mesh=mesh,
        in_specs=(
            P("replica", None),
            P("replica", None),
            P("replica", None, None),
            P(None, None, "tensor"),
            P("replica", None, None, "tensor"),
            P(None, None, "tensor"),
        ),
        out_specs=(
            P(None, None, "tensor"),
            P(None, None, "tensor"),
            P("replica", None, None, "tensor"),
        ),
        check_vma=False,
    )
```

time: 675 us -> 421 us (0.62)
  waiting for transfers between devices: 475 us -> 201 us
  starting transfers between devices: 13.1 us -> 89.3 us
  other arithmetic: 100 us -> 30.6 us
  Pallas kernels: 0 us -> 57.8 us
  matrix products: 49.3 us -> 0 us
  local copies, waits for them, and re-layouts: 20 us -> 39.9 us
  between operations: 14.6 us -> 1.56 us
    psum x1 -> x0, waiting for transfers between devices: 158 us -> none  [body(): total = lax.psum(weights, 'replica')]
    reduce_scatter x3 -> x0, waiting for transfers between devices: 97.5 us -> none  [body(): lax.psum_scatter(partial_out, 'tensor', scatter_dimension=0, tiled=True)]
    ppermute x0 -> x58, starting transfers between devices: none -> 85.6 us  [the longest x24 60 us: moved(): lax.ppermute(part, axis, [(cores * a + c, cores * b + c) for a, b in hops...]
    all_gather x3 -> x0, waiting for transfers between devices: 80.7 us -> none  [body(): error = lax.all_gather(error_share, 'tensor', axis=0, tiled=True)]
    ppermute x0 -> x58, waiting for transfers between devices: none -> 68.2 us  [the longest x34 45.8 us: swapped(): lax.ppermute(block, axis, [(i, i ^ mask) for i in range(lax.axis_size(axi...]
    pallas_call x0 -> x6, Pallas kernels: none -> 57.8 us  [the longest x3 40.1 us: backward(): pl.pallas_call(functools.partial(backward_kernel, update, len(states)), g...]
    dot_general x12 -> x0, matrix products: 49.3 us -> none  [the longest x3 23.9 us: body(): lax.dot_general(inputs, back, (((0,), (0,)), ((), ())), preferred_element...]
    convert_element_type x8 -> x20, other arithmetic: 51.5 us -> 9.15 us  [the longest x3 5.43 us: error_of(): own = ((share - wanted.astype(f32)) * scale).astype(bf16)]
  transfers between devices with their start and end apart: 9 -> 60, of which waited for: 9 -> 28; matrix products, arithmetic and copies ran while one was open for 4% -> 5% of each run, Pallas kernels for 0% -> 0%
where the time goes in v2:
time: 421 us; the launch traced here: 420 us
  waiting for transfers between devices  201 us (48%)
  starting transfers between devices  89.3 us (21%)
  Pallas kernels  57.8 us (14%)
  local copies, waits for them, and re-layouts  39.9 us (9%)
  other arithmetic  30.6 us (7%)
    ppermute x2, waiting for transfers between devices, passed_along(): return lax.ppermute(block, axis, route)  133 us
    ppermute x24, starting transfers between devices, moved(): lax.ppermute(part, axis, [(cores * a + c, cores * b + c) for a, b in hops...  60 us
    ppermute x34, waiting for transfers between devices, swapped(): lax.ppermute(block, axis, [(i, i ^ mask) for i in range(lax.axis_size(axi...  45.8 us
    pallas_call x3, Pallas kernels, backward(): pl.pallas_call(functools.partial(backward_kernel, update, len(states)), g...  40.1 us
    ppermute x34, starting transfers between devices, swapped(): lax.ppermute(block, axis, [(i, i ^ mask) for i in range(lax.axis_size(axi...  25.6 us
    ppermute x24, waiting for transfers between devices, moved(): lax.ppermute(part, axis, [(cores * a + c, cores * b + c) for a, b in hops...  22.5 us
    unnamed x38, local copies, waits for them, and re-layouts  18.4 us
    pallas_call x3, Pallas kernels, forward(): pl.pallas_call(functools.partial(forward_kernel, mixes), grid=(units // b...  17.7 us
  transfers between devices with their start and end apart: 60, of which 28 were waited for; matrix products, arithmetic and copies ran while one was open for 5% of the time, Pallas kernels for 0%

profile of v2, /device:TPU:0, one launch (start us, length us, event | category | flops | bytes accessed | tf_op | source)
XLA Modules:
  0.0 420.2 jit_solution(11417392863612429357)
XLA Ops:
  7.5 4.6 %shard_map.85 = (bf16[512,1024]{1,0:T(8,128)(2,1)S(1)}, bf16[512,1024]{1,0:T(8,128)(2,1)S(1)}, bf16[512,1024]{1,0:T(8,128)(2,1)S(1)}) custom-call(bf16[512,1024]{1,0:T(8,128)(2,1)S(1)} %gather_fusion.3, f32[2,1024,1024]{2,1,0:T(8,128)S(1)} %copy-done.2), custom_call_target="tpu_custom_call" | custom-call | flops 2147483648 | bytes 8388608 | tf_op jit(solution)/shard_map/pallas_call | solution.py:81
  25.3 6.3 %collective-permute-done.1 = bf16[128,1024]{1,0:T(8,128)(2,1)} collective-permute-done((bf16[128,1024]{1,0:T(8,128)(2,1)}, bf16[128,1024]{1,0:T(8,128)(2,1)}, u32[]{:S(2)}, u32[]{:S(2)}) %collective-permute-start.1) | collective-permute-done | bytes 262176 | tf_op jit(solution)/shard_map/ppermute | solution.py:27
  38.4 4.6 %collective-permute-done.3 = bf16[128,1024]{1,0:T(8,128)(2,1)S(1)} collective-permute-done((bf16[128,1024]{1,0:T(8,128)(2,1)}, bf16[128,1024]{1,0:T(8,128)(2,1)S(1)}, u32[]{:S(2)}, u32[]{:S(2)}) %collective-permute-start.3) | collective-permute-done | bytes 262176 | tf_op jit(solution)/shard_map/ppermute | solution.py:27
  43.1 4.5 %collective-permute-done.4 = bf16[128,1024]{1,0:T(8,128)(2,1)S(1)} collective-permute-done((bf16[128,1024]{1,0:T(8,128)(2,1)}, bf16[128,1024]{1,0:T(8,128)(2,1)S(1)}, u32[]{:S(2)}, u32[]{:S(2)}) %collective-permute-start.4) | collective-permute-done | bytes 262176 | tf_op jit(solution)/shard_map/ppermute | solution.py:27
  49.6 13.5 %shard_map.86 = (f32[2,1024,1024]{2,1,0:T(8,128)}, bf16[2,1024,1024]{2,1,0:T(8,128)(2,1)}) custom-call(bf16[512,1024]{1,0:T(8,128)(2,1)} %pad_maximum_fusion.error, f32[2,1024,1024]{2,1,0:T(8,128)} %refs_1_.1, bf16[512,1024]{1,0:T(8,128)(2,1)} %copy-done.12, bf16[512,1024]{1,0:T(8,128)(2,1)} %copy-done.11, bf16[1024,512]{1,0:T(8,128)(2,1)} %bitcast.139, ...), custom_call_target="tpu_custom_call" | custom-call | flops 3221225472 | bytes 29360128 | tf_op jit(solution)/shard_map/pallas_call | solution.py:117
  65.1 48.0 %collective-permute-done.6.refs_0_ = bf16[2,1024,1024]{2,1,0:T(8,128)(2,1)} collective-permute-done((bf16[2,1024,1024]{2,1,0:T(8,128)(2,1)}, bf16[2,1024,1024]{2,1,0:T(8,128)(2,1)}, u32[]{:S(2)}, u32[]{:S(2)}) %collective-permute-start.6) | collective-permute-done | bytes 4194336 | tf_op jit(solution)/shard_map/ppermute | solution.py:23
  115.3 6.5 %shard_map.87 = (bf16[512,1024]{1,0:T(8,128)(2,1)S(1)}, bf16[512,1024]{1,0:T(8,128)(2,1)S(1)}, bf16[512,1024]{1,0:T(8,128)(2,1)S(1)}, bf16[2,1024,1024]{2,1,0:T(8,128)(2,1)S(1)}) custom-call(bf16[512,1024]{1,0:T(8,128)(2,1)S(1)} %gather_fusion.2, bf16[2,1024,1024]{2,1,0:T(8,128)(2,1)S(1)} %copy-done.6, bf16[2,1024,1024]{2,1,0:T(8,128)(2,1)} %collective-permute-done.6.refs_0_), custom_call_target="tpu_custom_call" | custom-call | flops 2147483648 | bytes 8388608 | tf_op jit(solution)/shard_map/pallas_call | solution.py:81
  147.7 4.0 collective-permute-done.11
  153.7 14.0 %shard_map.88 = (f32[2,1024,1024]{2,1,0:T(8,128)}, bf16[2,1024,1024]{2,1,0:T(8,128)(2,1)}, bf16[2,1024,1024]{2,1,0:T(8,128)(2,1)}) custom-call(bf16[512,1024]{1,0:T(8,128)(2,1)} %pad_maximum_fusion.1.error, bf16[2,1024,1024]{2,1,0:T(8,128)(2,1)} %copy-done.3, bf16[512,1024]{1,0:T(8,128)(2,1)} %copy-done.10, bf16[512,1024]{1,0:T(8,128)(2,1)} %copy-done.9, ...), custom_call_target="tpu_custom_call" | custom-call | flops 3221225472 | bytes 29360128 | tf_op jit(solution)/shard_map/pallas_call | solution.py:117
  173.5 84.9 %collective-permute-done.13.refs_0_ = bf16[2,1024,1024]{2,1,0:T(8,128)(2,1)} collective-permute-done((bf16[2,1024,1024]{2,1,0:T(8,128)(2,1)}, bf16[2,1024,1024]{2,1,0:T(8,128)(2,1)}, u32[]{:S(2)}, u32[]{:S(2)}) %collective-permute-start.13) | collective-permute-done | bytes 4194336 | tf_op jit(solution)/shard_map/ppermute | solution.py:23
  260.6 6.6 %shard_map.89 = (bf16[512,1024]{1,0:T(8,128)(2,1)S(1)}, bf16[512,1024]{1,0:T(8,128)(2,1)S(1)}, bf16[512,1024]{1,0:T(8,128)(2,1)S(1)}, bf16[2,1024,1024]{2,1,0:T(8,128)(2,1)S(1)}) custom-call(bf16[512,1024]{1,0:T(8,128)(2,1)S(1)} %gather_fusion.1, bf16[2,1024,1024]{2,1,0:T(8,128)(2,1)S(1)} %copy-done.5, bf16[2,1024,1024]{2,1,0:T(8,128)(2,1)} %collective-permute-done.13.refs_0_), custom_call_target="tpu_custom_call" | custom-call | flops 2147483648 | bytes 8388608 | tf_op jit(solution)/shard_map/pallas_call | solution.py:81
  290.3 4.8 %collective-permute-done.18 = bf16[128,1024]{1,0:T(8,128)(2,1)S(1)} collective-permute-done((bf16[128,1024]{1,0:T(8,128)(2,1)S(1)}, bf16[128,1024]{1,0:T(8,128)(2,1)S(1)}, u32[]{:S(2)}, u32[]{:S(2)}) %collective-permute-start.18) | collective-permute-done | bytes 262176 | tf_op jit(solution)/shard_map/ppermute | solution.py:27
  296.2 12.6 %shard_map.90 = (f32[2,1024,1024]{2,1,0:T(8,128)}, bf16[2,1024,1024]{2,1,0:T(8,128)(2,1)}) custom-call(bf16[512,1024]{1,0:T(8,128)(2,1)} %pad_maximum_fusion.2.error, bf16[2,1024,1024]{2,1,0:T(8,128)(2,1)} %copy-done.4, bf16[512,1024]{1,0:T(8,128)(2,1)} %copy-done.8, bf16[512,1024]{1,0:T(8,128)(2,1)} %copy-done.7, bf16[1024,512]{1,0:T(8,128)(2,1)} %bitcast.137, ...), custom_call_target="tpu_custom_call" | custom-call | flops 3221225472 | bytes 29360128 | tf_op jit(solution)/shard_map/pallas_call | solution.py:117
  317.7 4.4 %collective-permute-start.29 = (bf16[128,1024]{1,0:T(8,128)(2,1)S(1)}, bf16[128,1024]{1,0:T(8,128)(2,1)S(1)}, u32[]{:S(2)}, u32[]{:S(2)}) collective-permute-start(bf16[128,1024]{1,0:T(8,128)(2,1)S(1)} %get-tuple-element.89), channel_id=1, source_target_pairs={{0,8},{4,12},{24,16},{28,20},{1,9},{5,13},{25,17},{29,21},{2,10},{... | collective-permute-start | bytes 786440 | tf_op jit(solution)/shard_map/ppermute | solution.py:168
  323.4 5.3 %collective-permute-done.29 = bf16[128,1024]{1,0:T(8,128)(2,1)S(1)} collective-permute-done((bf16[128,1024]{1,0:T(8,128)(2,1)S(1)}, bf16[128,1024]{1,0:T(8,128)(2,1)S(1)}, u32[]{:S(2)}, u32[]{:S(2)}) %collective-permute-start.29) | collective-permute-done | bytes 262176 | tf_op jit(solution)/shard_map/ppermute | solution.py:168
  329.5 8.0 %collective-permute-start.31 = (bf16[128,1024]{1,0:T(8,128)(2,1)S(1)}, bf16[128,1024]{1,0:T(8,128)(2,1)S(1)}, u32[]{:S(2)}, u32[]{:S(2)}) collective-permute-start(bf16[128,1024]{1,0:T(8,128)(2,1)S(1)} %get-tuple-element.63), channel_id=1, source_target_pairs={{0,8},{4,12},{24,16},{28,20},{1,9},{5,13},{25,17},{29,21},{2,10},{... | collective-permute-start | bytes 786440 | tf_op jit(solution)/shard_map/ppermute | solution.py:168
  338.2 4.0 collective-permute-start.23
  343.2 5.1 %collective-permute-start.41 = (bf16[128,1024]{1,0:T(8,128)(2,1)S(1)}, bf16[128,1024]{1,0:T(8,128)(2,1)S(1)}, u32[]{:S(2)}, u32[]{:S(2)}) collective-permute-start(bf16[128,1024]{1,0:T(8,128)(2,1)S(1)} %get-tuple-element.69), channel_id=1, source_target_pairs={{0,8},{4,12},{24,16},{28,20},{1,9},{5,13},{25,17},{29,21},{2,10},{... | collective-permute-start | bytes 786440 | tf_op jit(solution)/shard_map/ppermute | solution.py:168
  350.5 7.5 %collective-permute-start.36 = (bf16[128,1024]{1,0:T(8,128)(2,1)S(1)}, bf16[128,1024]{1,0:T(8,128)(2,1)S(1)}, u32[]{:S(2)}, u32[]{:S(2)}) collective-permute-start(bf16[128,1024]{1,0:T(8,128)(2,1)S(1)} %get-tuple-element.66), channel_id=1, source_target_pairs={{0,8},{4,12},{24,16},{28,20},{1,9},{5,13},{25,17},{29,21},{2,10},{... | collective-permute-start | bytes 786440 | tf_op jit(solution)/shard_map/ppermute | solution.py:168
  360.2 6.1 %collective-permute-start.50 = (bf16[128,1024]{1,0:T(8,128)(2,1)S(1)}, bf16[128,1024]{1,0:T(8,128)(2,1)S(1)}, u32[]{:S(2)}, u32[]{:S(2)}) collective-permute-start(bf16[128,1024]{1,0:T(8,128)(2,1)S(1)} %get-tuple-element.75), channel_id=1, source_target_pairs={{0,8},{4,12},{24,16},{28,20},{1,9},{5,13},{25,17},{29,21},{2,10},{... | collective-permute-start | bytes 786440 | tf_op jit(solution)/shard_map/ppermute | solution.py:168
  368.5 7.5 %collective-permute-start.46 = (bf16[128,1024]{1,0:T(8,128)(2,1)S(1)}, bf16[128,1024]{1,0:T(8,128)(2,1)S(1)}, u32[]{:S(2)}, u32[]{:S(2)}) collective-permute-start(bf16[128,1024]{1,0:T(8,128)(2,1)S(1)} %get-tuple-element.72), channel_id=1, source_target_pairs={{0,8},{4,12},{24,16},{28,20},{1,9},{5,13},{25,17},{29,21},{2,10},{... | collective-permute-start | bytes 786440 | tf_op jit(solution)/shard_map/ppermute | solution.py:168
  392.5 4.5 %collective-permute-done.48 = bf16[128,1024]{1,0:T(8,128)(2,1)S(1)} collective-permute-done((bf16[128,1024]{1,0:T(8,128)(2,1)S(1)}, bf16[128,1024]{1,0:T(8,128)(2,1)S(1)}, u32[]{:S(2)}, u32[]{:S(2)}) %collective-permute-start.48) | collective-permute-done | bytes 262176 | tf_op jit(solution)/shard_map/ppermute | solution.py:168
  402.7 4.8 %collective-permute-done.55 = bf16[128,1024]{1,0:T(8,128)(2,1)S(1)} collective-permute-done((bf16[128,1024]{1,0:T(8,128)(2,1)S(1)}, bf16[128,1024]{1,0:T(8,128)(2,1)S(1)}, u32[]{:S(2)}, u32[]{:S(2)}) %collective-permute-start.55) | collective-permute-done | bytes 262176 | tf_op jit(solution)/shard_map/ppermute | solution.py:168
  411.3 9.0 %multiply_subtract_fusion = (f32[2,1024,1024]{2,1,0:T(8,128)}, f32[2,1024,1024]{2,1,0:T(8,128)}) fusion(f32[2,1024,1024]{2,1,0:T(8,128)S(1)} %bitcast.133, bf16[2,1024,1024]{2,1,0:T(8,128)(2,1)} %maximum_dynamic-update-slice_fusion, f32[2,1024,1024]{2,1,0:T(8,128)S(1)} %bitcast.136), kind=kLoop, calls=%fused_computation.7 | loop fusion | flops 12582912 | bytes 37748736 | tf_op jit(solution)/shard_map/sub | solution.py:240
  (215 shorter events, 137.7 us)
Async XLA Ops:
  17.9 13.7 %collective-permute-start.1 = (bf16[128,1024]{1,0:T(8,128)(2,1)}, bf16[128,1024]{1,0:T(8,128)(2,1)}, u32[]{:S(2)}, u32[]{:S(2)}) collective-permute-start(bf16[128,1024]{1,0:T(8,128)(2,1)} %get-tuple-element.109), channel_id=1, source_target_pairs={{0,2},{1,3},{2,0},{3,1},{4,6},{5,7},{6,4},{7,5},{8,10},{9,11},{10,... | collective-permute-start | bytes 786440 | tf_op jit(solution)/shard_map/ppermute | solution.py:27
  19.4 12.2 %collective-permute-start.2 = (bf16[128,1024]{1,0:T(8,128)(2,1)}, bf16[128,1024]{1,0:T(8,128)(2,1)}, u32[]{:S(2)}, u32[]{:S(2)}) collective-permute-start(bf16[128,1024]{1,0:T(8,128)(2,1)} %get-tuple-element.108), channel_id=1, source_target_pairs={{0,3},{1,2},{2,1},{3,0},{4,7},{5,6},{6,5},{7,4},{8,11},{9,10},{10,... | collective-permute-start | bytes 786440 | tf_op jit(solution)/shard_map/ppermute | solution.py:27
  34.8 12.7 %collective-permute-start.4 = (bf16[128,1024]{1,0:T(8,128)(2,1)}, bf16[128,1024]{1,0:T(8,128)(2,1)S(1)}, u32[]{:S(2)}, u32[]{:S(2)}) collective-permute-start(bf16[128,1024]{1,0:T(8,128)(2,1)} %multiply_convert_fusion.2), channel_id=1, source_target_pairs={{0,2},{1,3},{2,0},{3,1},{4,6},{5,7},{6,4},{7,5},{8,10},{9,11},{10,... | collective-permute-start | bytes 786440 | tf_op jit(solution)/shard_map/ppermute | solution.py:27
  35.7 11.9 %collective-permute-start.5 = (bf16[128,1024]{1,0:T(8,128)(2,1)}, bf16[128,1024]{1,0:T(8,128)(2,1)S(1)}, u32[]{:S(2)}, u32[]{:S(2)}) collective-permute-start(bf16[128,1024]{1,0:T(8,128)(2,1)} %multiply_convert_fusion.2), channel_id=1, source_target_pairs={{0,3},{1,2},{2,1},{3,0},{4,7},{5,6},{6,5},{7,4},{8,11},{9,10},{10,... | collective-permute-start | bytes 786440 | tf_op jit(solution)/shard_map/ppermute | solution.py:27
  63.0 50.0 %collective-permute-start.6 = (bf16[2,1024,1024]{2,1,0:T(8,128)(2,1)}, bf16[2,1024,1024]{2,1,0:T(8,128)(2,1)}, u32[]{:S(2)}, u32[]{:S(2)}) collective-permute-start(bf16[2,1024,1024]{2,1,0:T(8,128)(2,1)} %get-tuple-element.46.weights), channel_id=1, source_target_pairs={{28,0},{0,4},{4,8},{8,12},{12,16},{16,20},{20,24},{24,28},{29,1},{... | collective-permute-start | bytes 12582920 | tf_op jit(solution)/shard_map/ppermute | solution.py:23
  127.2 11.3 %collective-permute-start.8 = (bf16[128,1024]{1,0:T(8,128)(2,1)}, bf16[128,1024]{1,0:T(8,128)(2,1)}, u32[]{:S(2)}, u32[]{:S(2)}) collective-permute-start(bf16[128,1024]{1,0:T(8,128)(2,1)} %get-tuple-element.106), channel_id=1, source_target_pairs={{0,2},{1,3},{2,0},{3,1},{4,6},{5,7},{6,4},{7,5},{8,10},{9,11},{10,... | collective-permute-start | bytes 786440 | tf_op jit(solution)/shard_map/ppermute | solution.py:27
  167.8 90.6 %collective-permute-start.13 = (bf16[2,1024,1024]{2,1,0:T(8,128)(2,1)}, bf16[2,1024,1024]{2,1,0:T(8,128)(2,1)}, u32[]{:S(2)}, u32[]{:S(2)}) collective-permute-start(bf16[2,1024,1024]{2,1,0:T(8,128)(2,1)} %get-tuple-element.52.weights), channel_id=1, source_target_pairs={{24,0},{28,4},{0,8},{4,12},{8,16},{12,20},{16,24},{20,28},{25,1},{... | collective-permute-start | bytes 12582920 | tf_op jit(solution)/shard_map/ppermute | solution.py:23
  322.1 15.4 %collective-permute-start.21 = (bf16[128,1024]{1,0:T(8,128)(2,1)S(1)}, bf16[128,1024]{1,0:T(8,128)(2,1)S(1)}, u32[]{:S(2)}, u32[]{:S(2)}) collective-permute-start(bf16[128,1024]{1,0:T(8,128)(2,1)S(1)} %get-tuple-element.92), channel_id=1, source_target_pairs={{0,8},{4,12},{24,16},{28,20},{1,9},{5,13},{25,17},{29,21},{2,10},{... | collective-permute-start | bytes 786440 | tf_op jit(solution)/shard_map/ppermute | solution.py:168
  328.8 13.5 %collective-permute-start.32 = (bf16[128,1024]{1,0:T(8,128)(2,1)S(1)}, bf16[128,1024]{1,0:T(8,128)(2,1)S(1)}, u32[]{:S(2)}, u32[]{:S(2)}) collective-permute-start(bf16[128,1024]{1,0:T(8,128)(2,1)S(1)} %reduce-precision_convert_fusion.12), channel_id=1, source_target_pairs={{8,16},{12,20},{16,8},{20,12},{9,17},{13,21},{17,9},{21,13},{10,18... | collective-permute-start | bytes 786440 | tf_op jit(solution)/shard_map/ppermute | solution.py:168
  329.5 12.8 %collective-permute-start.31 = (bf16[128,1024]{1,0:T(8,128)(2,1)S(1)}, bf16[128,1024]{1,0:T(8,128)(2,1)S(1)}, u32[]{:S(2)}, u32[]{:S(2)}) collective-permute-start(bf16[128,1024]{1,0:T(8,128)(2,1)S(1)} %get-tuple-element.63), channel_id=1, source_target_pairs={{0,8},{4,12},{24,16},{28,20},{1,9},{5,13},{25,17},{29,21},{2,10},{... | collective-permute-start | bytes 786440 | tf_op jit(solution)/shard_map/ppermute | solution.py:168
  337.5 12.1 %collective-permute-start.24 = (bf16[128,1024]{1,0:T(8,128)(2,1)S(1)}, bf16[128,1024]{1,0:T(8,128)(2,1)S(1)}, u32[]{:S(2)}, u32[]{:S(2)}) collective-permute-start(bf16[128,1024]{1,0:T(8,128)(2,1)S(1)} %reduce-precision_convert_fusion.15), channel_id=1, source_target_pairs={{8,16},{12,20},{16,8},{20,12},{9,17},{13,21},{17,9},{21,13},{10,18... | collective-permute-start | bytes 786440 | tf_op jit(solution)/shard_map/ppermute | solution.py:168
  338.2 11.5 %collective-permute-start.23 = (bf16[128,1024]{1,0:T(8,128)(2,1)S(1)}, bf16[128,1024]{1,0:T(8,128)(2,1)S(1)}, u32[]{:S(2)}, u32[]{:S(2)}) collective-permute-start(bf16[128,1024]{1,0:T(8,128)(2,1)S(1)} %get-tuple-element.60), channel_id=1, source_target_pairs={{0,8},{4,12},{24,16},{28,20},{1,9},{5,13},{25,17},{29,21},{2,10},{... | collective-permute-start | bytes 786440 | tf_op jit(solution)/shard_map/ppermute | solution.py:168
  342.4 15.6 %collective-permute-start.42 = (bf16[128,1024]{1,0:T(8,128)(2,1)S(1)}, bf16[128,1024]{1,0:T(8,128)(2,1)S(1)}, u32[]{:S(2)}, u32[]{:S(2)}) collective-permute-start(bf16[128,1024]{1,0:T(8,128)(2,1)S(1)} %reduce-precision_convert_fusion.11), channel_id=1, source_target_pairs={{8,16},{12,20},{16,8},{20,12},{9,17},{13,21},{17,9},{21,13},{10,18... | collective-permute-start | bytes 786440 | tf_op jit(solution)/shard_map/ppermute | solution.py:168
  343.2 16.2 %collective-permute-start.41 = (bf16[128,1024]{1,0:T(8,128)(2,1)S(1)}, bf16[128,1024]{1,0:T(8,128)(2,1)S(1)}, u32[]{:S(2)}, u32[]{:S(2)}) collective-permute-start(bf16[128,1024]{1,0:T(8,128)(2,1)S(1)} %get-tuple-element.69), channel_id=1, source_target_pairs={{0,8},{4,12},{24,16},{28,20},{1,9},{5,13},{25,17},{29,21},{2,10},{... | collective-permute-start | bytes 786440 | tf_op jit(solution)/shard_map/ppermute | solution.py:168
  349.8 16.5 %collective-permute-start.37 = (bf16[128,1024]{1,0:T(8,128)(2,1)S(1)}, bf16[128,1024]{1,0:T(8,128)(2,1)S(1)}, u32[]{:S(2)}, u32[]{:S(2)}) collective-permute-start(bf16[128,1024]{1,0:T(8,128)(2,1)S(1)} %reduce-precision_convert_fusion.14), channel_id=1, source_target_pairs={{8,16},{12,20},{16,8},{20,12},{9,17},{13,21},{17,9},{21,13},{10,18... | collective-permute-start | bytes 786440 | tf_op jit(solution)/shard_map/ppermute | solution.py:168
  350.5 17.2 %collective-permute-start.36 = (bf16[128,1024]{1,0:T(8,128)(2,1)S(1)}, bf16[128,1024]{1,0:T(8,128)(2,1)S(1)}, u32[]{:S(2)}, u32[]{:S(2)}) collective-permute-start(bf16[128,1024]{1,0:T(8,128)(2,1)S(1)} %get-tuple-element.66), channel_id=1, source_target_pairs={{0,8},{4,12},{24,16},{28,20},{1,9},{5,13},{25,17},{29,21},{2,10},{... | collective-permute-start | bytes 786440 | tf_op jit(solution)/shard_map/ppermute | solution.py:168
  359.5 16.6 %collective-permute-start.51 = (bf16[128,1024]{1,0:T(8,128)(2,1)S(1)}, bf16[128,1024]{1,0:T(8,128)(2,1)S(1)}, u32[]{:S(2)}, u32[]{:S(2)}) collective-permute-start(bf16[128,1024]{1,0:T(8,128)(2,1)S(1)} %reduce-precision_convert_fusion.7), channel_id=1, source_target_pairs={{8,16},{12,20},{16,8},{20,12},{9,17},{13,21},{17,9},{21,13},{10,18... | collective-permute-start | bytes 786440 | tf_op jit(solution)/shard_map/ppermute | solution.py:168
  360.2 17.3 %collective-permute-start.50 = (bf16[128,1024]{1,0:T(8,128)(2,1)S(1)}, bf16[128,1024]{1,0:T(8,128)(2,1)S(1)}, u32[]{:S(2)}, u32[]{:S(2)}) collective-permute-start(bf16[128,1024]{1,0:T(8,128)(2,1)S(1)} %get-tuple-element.75), channel_id=1, source_target_pairs={{0,8},{4,12},{24,16},{28,20},{1,9},{5,13},{25,17},{29,21},{2,10},{... | collective-permute-start | bytes 786440 | tf_op jit(solution)/shard_map/ppermute | solution.py:168
  366.3 11.3 %collective-permute-start.44 = (bf16[128,1024]{1,0:T(8,128)(2,1)S(1)}, bf16[128,1024]{1,0:T(8,128)(2,1)S(1)}, u32[]{:S(2)}, u32[]{:S(2)}) collective-permute-start(bf16[128,1024]{1,0:T(8,128)(2,1)S(1)} %reduce-precision_convert_fusion.6), channel_id=1, source_target_pairs={{8,0},{12,4},{16,24},{20,28},{9,1},{13,5},{17,25},{21,29},{10,2},{... | collective-permute-start | bytes 786440 | tf_op jit(solution)/shard_map/ppermute | solution.py:168
  368.5 11.4 %collective-permute-start.46 = (bf16[128,1024]{1,0:T(8,128)(2,1)S(1)}, bf16[128,1024]{1,0:T(8,128)(2,1)S(1)}, u32[]{:S(2)}, u32[]{:S(2)}) collective-permute-start(bf16[128,1024]{1,0:T(8,128)(2,1)S(1)} %get-tuple-element.72), channel_id=1, source_target_pairs={{0,8},{4,12},{24,16},{28,20},{1,9},{5,13},{25,17},{29,21},{2,10},{... | collective-permute-start | bytes 786440 | tf_op jit(solution)/shard_map/ppermute | solution.py:168
  379.9 11.3 %collective-permute-start.52 = (bf16[128,1024]{1,0:T(8,128)(2,1)S(1)}, bf16[128,1024]{1,0:T(8,128)(2,1)S(1)}, u32[]{:S(2)}, u32[]{:S(2)}) collective-permute-start(bf16[128,1024]{1,0:T(8,128)(2,1)S(1)} %reduce-precision_convert_fusion.2), channel_id=1, source_target_pairs={{8,0},{12,4},{16,24},{20,28},{9,1},{13,5},{17,25},{21,29},{10,2},{... | collective-permute-start | bytes 786440 | tf_op jit(solution)/shard_map/ppermute | solution.py:168
  385.3 11.6 %collective-permute-start.48 = (bf16[128,1024]{1,0:T(8,128)(2,1)S(1)}, bf16[128,1024]{1,0:T(8,128)(2,1)S(1)}, u32[]{:S(2)}, u32[]{:S(2)}) collective-permute-start(bf16[128,1024]{1,0:T(8,128)(2,1)S(1)} %reduce-precision_convert_fusion.4), channel_id=1, source_target_pairs={{8,0},{12,4},{16,24},{20,28},{9,1},{13,5},{17,25},{21,29},{10,2},{... | collective-permute-start | bytes 786440 | tf_op jit(solution)/shard_map/ppermute | solution.py:168
  386.7 11.7 %collective-permute-start.45 = (bf16[128,1024]{1,0:T(8,128)(2,1)S(1)}, bf16[128,1024]{1,0:T(8,128)(2,1)S(1)}, u32[]{:S(2)}, u32[]{:S(2)}) collective-permute-start(bf16[128,1024]{1,0:T(8,128)(2,1)S(1)} %broadcast_select_fusion.4), channel_id=1, source_target_pairs={{0,4},{4,0},{8,12},{12,8},{16,20},{20,16},{24,28},{28,24},{1,5},{5... | collective-permute-start | bytes 786440 | tf_op jit(solution)/shard_map/ppermute | solution.py:27
  391.1 11.5 %collective-permute-start.58 = (bf16[128,1024]{1,0:T(8,128)(2,1)S(1)}, bf16[128,1024]{1,0:T(8,128)(2,1)S(1)}, u32[]{:S(2)}, u32[]{:S(2)}) collective-permute-start(bf16[128,1024]{1,0:T(8,128)(2,1)S(1)} %reduce-precision_convert_fusion), channel_id=1, source_target_pairs={{8,0},{12,4},{16,24},{20,28},{9,1},{13,5},{17,25},{21,29},{10,2},{... | collective-permute-start | bytes 786440 | tf_op jit(solution)/shard_map/ppermute | solution.py:168
  (55 other events, 417.6 us)

commit v3 on v2

--- a/solution.py
+++ b/solution.py
@@ -15,12 +15,6 @@
 slow_beta = 0.5
 chunks = 8
 bf16, f32 = jnp.bfloat16, jnp.float32
-
-
-def passed_along(block, axis, distance):
-    devices = range(lax.axis_size(axis))
-    route = [((i - distance) % len(devices), i) for i in devices]
-    return lax.ppermute(block, axis, route)
 
 
 def swapped(block, axis, mask):
@@ -40,56 +34,69 @@
     return pl.BlockSpec(shape, lambda j: (0,) * len(shape))
 
 
-def forward_kernel(mixes, inputs, weights, *refs):
-    if mixes:
-        incoming, hidden, slope, partial, mixed, total = refs
-        block = (0.5 * (weights[...].astype(f32) + incoming[...].astype(f32))).astype(bf16)
-        mixed[...] = block
-    else:
-        hidden, slope, partial, total = refs
-        block = weights[...].astype(bf16)
+def forward_kernel(mix, taken, sums, emits, flag, inputs, *refs):
+    sources, refs = refs[:taken], list(refs[taken:])
+    hidden, slope = refs[:2]
+    block = mix(flag[0], *[source[...].astype(f32) for source in sources]).astype(bf16)
+    if emits:
+        refs[2 + sums][...] = block
     j = pl.program_id(0)
     value, slope_val = gelu_pair(jnp.dot(inputs[...], block[0], preferred_element_type=f32))
     value = value.astype(bf16)
     hidden[...] = value
     slope[...] = slope_val.astype(bf16)
-    out = lax.dot_general(value, block[1], (((1,), (1,)), ((), ())), preferred_element_type=f32)
-
-    @pl.when(j == 0)
-    def _():
-        total[...] = out
-
-    @pl.when(j > 0)
-    def _():
-        total[...] += out
-
-    @pl.when(j == pl.num_programs(0) - 1)
-    def _():
-        partial[...] = total[...].astype(bf16)
-
-
-def forward(inputs, weights, incoming=None):
+    if sums:
+        partial, total = refs[2], refs[-1]
+        out = lax.dot_general(value, block[1], (((1,), (1,)), ((), ())), preferred_element_type=f32)
+
+        @pl.when(j == 0)
+        def _():
+            total[...] = out
+
+        @pl.when(j > 0)
+        def _():
+            total[...] += out
+
+        @pl.when(j == pl.num_programs(0) - 1)
+        def _():
+            partial[...] = total[...].astype(bf16)
+
+
+def forward(flag, inputs, sources, mix, sums=True, emits=True):
     rows, width = inputs.shape
-    units = weights.shape[2]
+    units = sources[0].shape[2]
     block = min(units, 512)
-    mixes = incoming is not None
-    weight_spec = pl.BlockSpec((2, width, block), lambda j: (0, 0, j))
+    parts = 2 if sums or emits else 1
+    weight_spec = pl.BlockSpec((parts, width, block), lambda j: (0, 0, j))
     unit_spec = pl.BlockSpec((rows, block), lambda j: (0, j))
-    shapes = [((rows, units), unit_spec), ((rows, units), unit_spec), ((rows, width), whole((rows, width)))]
-    if mixes:
-        shapes.append((weights.shape, weight_spec))
+    shapes = [((rows, units), unit_spec), ((rows, units), unit_spec)]
+    shapes += [((rows, width), whole((rows, width)))] * sums + [(sources[0].shape, weight_spec)] * emits
     return pl.pallas_call(
-        functools.partial(forward_kernel, mixes),
+        functools.partial(forward_kernel, mix, len(sources), sums, emits),
         grid=(units // block,),
-        in_specs=[whole((rows, width)), weight_spec] + [weight_spec] * mixes,
+        in_specs=[pl.BlockSpec(memory_space=pltpu.SMEM), whole((rows, width))] + [weight_spec] * len(sources),
         out_specs=[spec for _, spec in shapes],
         out_shape=[jax.ShapeDtypeStruct(shape, bf16) for shape, _ in shapes],
-        scratch_shapes=[pltpu.VMEM((rows, width), f32)],
-        compiler_params=pltpu.CompilerParams(vmem_limit_bytes=40 << 20),
+        scratch_shapes=[pltpu.VMEM((rows, width), f32)] * sums,
+        compiler_params=pltpu.CompilerParams(vmem_limit_bytes=48 << 20),
         cost_estimate=pl.CostEstimate(
-            flops=4 * rows * width * units, bytes_accessed=8 * width * units, transcendentals=rows * units
+            flops=(2 + 2 * sums) * rows * width * units,
+            bytes_accessed=16 * width * units,
+            transcendentals=rows * units,
         ),
-    )(inputs, weights, *([incoming] if mixes else []))
+    )(flag, inputs, *sources)
+
+
+def only(flag, weights):
+    return weights
+
+
+def pushed(flag, weights, first, second):
+    return weights - 0.5 * learn_rate * (first + second)
+
+
+def halved(flag, weights, sent, found):
+    return 0.5 * (weights + jnp.where(flag == 0, sent, found))
 
 
 def backward_kernel(update, taken, error, weights, slope, hidden, inputs_t, *refs):
@@ -128,14 +135,23 @@
     )(error, weights, slope, hidden, inputs_t, *states)
 
 
-def first_update(grad, moment, weights):
+def first_update(grad, moment):
     moment = inner_beta * moment + grad
-    return (moment, weights - learn_rate * moment)
+    return (moment, moment)
+
+
+def first_beside(grad, moment, own_moment, weights):
+    moment = inner_beta * moment + grad
+    return (moment, weights - 0.5 * learn_rate * (own_moment + moment))
 
 
 def second_update(grad, moment, weights):
     moment_new = inner_beta * moment + grad
     return (moment_new, weights - learn_rate * moment_new, moment + (1.0 + inner_beta) * moment_new)
+
+
+def second_beside(grad, moment, weights):
+    return (weights - learn_rate * (inner_beta * moment + grad),)
 
 
 def third_update(grad, moment, known):
@@ -215,27 +231,50 @@
         own = ((share - wanted.astype(f32)) * scale).astype(bf16)
         return jnp.concatenate([own] + [swapped(own, "tensor", m) for m in range(1, tensors)])
 
+    replicas = lax.axis_size("replica")
+    flag = (lax.axis_index("replica") % 2).astype(jnp.int32).reshape(1)
+
+    def sent(block, distance, which=(0, 1)):
+        route = [((i - distance) % replicas, i) for i in range(replicas) if i % 2 in which]
+        return lax.ppermute(block, "replica", route)
+
     inputs = [tokens.at[picks_all[step]].get(mode="promise_in_bounds") for step in range(INNER)]
     inputs_t = [block.T for block in inputs]
 
-    hidden, slope, partial = forward(inputs[0], anchor)
+    inputs_near = sent(inputs[0], 1)
+    moment_near = sent(momentum[0].astype(bf16), 1)
+    hidden, slope, partial = forward(flag, inputs[0], [anchor], only, emits=False)
     error = error_of(partial, 0)
-    moment, weights = backward(
-        error, anchor, slope, hidden, inputs_t[0], [momentum[0], anchor], first_update, [f32, bf16]
-    )
-    incoming = passed_along(weights, "replica", 1)
-    hidden, slope, partial, weights = forward(inputs[1], weights, incoming)
+    error_near = sent(error, 1)
+    moment, moment_bf = backward(error, anchor, slope, hidden, inputs_t[0], [momentum[0]], first_update, [f32, bf16])
+    moment_far = sent(moment_bf, 2, (0,))
+    hidden, slope = forward(flag, inputs_near, [anchor], only, sums=False, emits=False)
+    moment_near, weights = backward(
+        error_near, anchor, slope, hidden, inputs_near.T, [moment_near, moment, anchor], first_beside, [bf16, bf16]
+    )
+
+    inputs_far = sent(tied(error_near, inputs[1]), 2, (1,))
+    hidden, slope, partial = forward(flag, inputs[1], [weights], only, emits=False)
     error = error_of(partial, 1)
+    error_far = sent(error, 2, (1,))
     moment, weights, known = backward(
         error, weights, slope, hidden, inputs_t[1], [moment, weights], second_update, [f32, bf16, bf16]
     )
-    incoming = passed_along(weights, "replica", 2)
-    hidden, slope, partial, weights = forward(inputs[2], weights, incoming)
+    weights_sent = sent(weights, 2, (0,))
+    moment_two = sent(moment_near, 1, (1,))
+    moment_three = sent(moment_far, 1, (1,))
+    inputs_far = tied(weights, inputs_far)
+    hidden, slope, weights_far = forward(flag, inputs_far, [anchor, moment_two, moment_three], pushed, sums=False)
+    (weights_found,) = backward(
+        error_far, weights_far, slope, hidden, inputs_far.T, [moment_two, weights_far], second_beside, [bf16]
+    )
+
+    hidden, slope, partial, weights = forward(flag, inputs[2], [weights, weights_sent, weights_found], halved)
     error = error_of(partial, 2)
     moment, total = backward(
         error, weights, slope, hidden, inputs_t[2], [moment, known], third_update, [f32, bf16]
     )
-    mean_total = replica_sum(total).astype(f32) / lax.axis_size("replica")
+    mean_total = replica_sum(total).astype(f32) / replicas
     slow_new = slow_beta * slow + mean_total
     anchor_new = anchor - learn_rate * slow_new
     return (anchor_new, slow_new, moment[None])

time: 421 us -> 428 us (1.017); the launches traced: 420 us -> 421 us
  waiting for transfers between devices: 201 us -> 152 us
  Pallas kernels: 57.8 us -> 95.8 us
  starting transfers between devices: 89.3 us -> 99.4 us
  other arithmetic: 30.6 us -> 36.8 us
  local copies, waits for them, and re-layouts: 39.9 us -> 35.5 us
    ppermute x2 -> x9, waiting for transfers between devices: 133 us -> 80.3 us  [sent(): return lax.ppermute(block, 'replica', route)]
    pallas_call x3 -> x5, Pallas kernels: 40.1 us -> 61.5 us  [backward(): pl.pallas_call(functools.partial(backward_kernel, update, len(states)), g...]
    pallas_call x3 -> x5, Pallas kernels: 17.7 us -> 34.3 us  [forward(): pl.pallas_call(functools.partial(forward_kernel, mix, len(sources), sums,...]
    ppermute x2 -> x9, starting transfers between devices: 3.69 us -> 17.8 us  [sent(): return lax.ppermute(block, 'replica', route)]
    unnamed x38 -> x42, local copies, waits for them, and re-layouts: 18.4 us -> 10.4 us
    convert_element_type x0 -> x1, other arithmetic: none -> 6.15 us  [body(): moment_near = sent(momentum[0].astype(bf16), 1)]
  transfers between devices with their start and end apart: 60 -> 67, of which waited for: 28 -> 29; matrix products, arithmetic and copies ran while one was open for 5% -> 9% of each run, Pallas kernels for 0% -> 18%
where the time goes in v3:
time: 428 us; the launch traced here: 421 us
  waiting for transfers between devices  152 us (36%)
  starting transfers between devices  99.4 us (23%)
  Pallas kernels  95.8 us (22%)
  other arithmetic  36.8 us (9%)
  local copies, waits for them, and re-layouts  35.5 us (8%)
    ppermute x9, waiting for transfers between devices, sent(): return lax.ppermute(block, 'replica', route)  80.3 us
    pallas_call x5, Pallas kernels, backward(): pl.pallas_call(functools.partial(backward_kernel, update, len(states)), g...  61.5 us
    ppermute x24, starting transfers between devices, moved(): lax.ppermute(part, axis, [(cores * a + c, cores * b + c) for a, b in hops...  55.7 us
    ppermute x34, waiting for transfers between devices, swapped(): lax.ppermute(block, axis, [(i, i ^ mask) for i in range(lax.axis_size(axi...  47.6 us
    pallas_call x5, Pallas kernels, forward(): pl.pallas_call(functools.partial(forward_kernel, mix, len(sources), sums,...  34.3 us
    ppermute x34, starting transfers between devices, swapped(): lax.ppermute(block, axis, [(i, i ^ mask) for i in range(lax.axis_size(axi...  25.9 us
    ppermute x24, waiting for transfers between devices, moved(): lax.ppermute(part, axis, [(cores * a + c, cores * b + c) for a, b in hops...  23.7 us
    ppermute x9, starting transfers between devices, sent(): return lax.ppermute(block, 'replica', route)  17.8 us
  transfers between devices with their start and end apart: 67, of which 29 were waited for; matrix products, arithmetic and copies ran while one was open for 9% of the time, Pallas kernels for 18%

profile of v3, /device:TPU:0, one launch (start us, length us, event | category | flops | bytes accessed | tf_op | source)
XLA Modules:
  0.0 421.2 jit_solution(156820089541170138)
XLA Ops:
  0.7 6.2 %bitcast_convert_fusion = bf16[2,1024,1024]{2,1,0:T(8,128)(2,1)} fusion(f32[1,2,1024,1024]{3,2,1,0:T(8,128)} %param.10), kind=kLoop, calls=%fused_computation.127 | loop fusion | flops 2097152 | bytes 12582912 | tf_op jit(solution)/shard_map/convert_element_type | solution.py:245
  10.0 6.2 %shard_map.85 = (bf16[512,1024]{1,0:T(8,128)(2,1)S(1)}, bf16[512,1024]{1,0:T(8,128)(2,1)S(1)}, bf16[512,1024]{1,0:T(8,128)(2,1)S(1)}) custom-call(s32[1]{0:T(128)} %bitcast.flag, bf16[512,1024]{1,0:T(8,128)(2,1)S(1)} %gather_fusion.3, f32[2,1024,1024]{2,1,0:T(8,128)} %refs_0_.5), custom_call_target="tpu_custom_call" | custom-call | flops 2147483648 | bytes 16777216 | tf_op jit(solution)/shard_map/pallas_call | solution.py:74
  27.9 8.4 %collective-permute-done.1 = bf16[128,1024]{1,0:T(8,128)(2,1)} collective-permute-done((bf16[128,1024]{1,0:T(8,128)(2,1)}, bf16[128,1024]{1,0:T(8,128)(2,1)}, u32[]{:S(2)}, u32[]{:S(2)}) %collective-permute-start.1) | collective-permute-done | bytes 262176 | tf_op jit(solution)/shard_map/ppermute | solution.py:21
  47.7 4.6 %collective-permute-done.4 = bf16[128,1024]{1,0:T(8,128)(2,1)S(1)} collective-permute-done((bf16[128,1024]{1,0:T(8,128)(2,1)}, bf16[128,1024]{1,0:T(8,128)(2,1)S(1)}, u32[]{:S(2)}, u32[]{:S(2)}) %collective-permute-start.4) | collective-permute-done | bytes 262176 | tf_op jit(solution)/shard_map/ppermute | solution.py:21
  55.8 10.7 %shard_map.87 = (f32[2,1024,1024]{2,1,0:T(8,128)}, bf16[2,1024,1024]{2,1,0:T(8,128)(2,1)}) custom-call(bf16[512,1024]{1,0:T(8,128)(2,1)} %pad_maximum_fusion.error, f32[2,1024,1024]{2,1,0:T(8,128)} %refs_0_.5, bf16[512,1024]{1,0:T(8,128)(2,1)} %copy-done.7, bf16[512,1024]{1,0:T(8,128)(2,1)} %copy-done.6, bf16[1024,512]{1,0:T(8,128)(2,1)} %bitcast.142, ...), custom_call_target="tpu_custom_call" | custom-call | flops 3221225472 | bytes 29360128 | tf_op jit(solution)/shard_map/pallas_call | solution.py:124
  73.9 23.4 %collective-permute-done.7 = bf16[512,1024]{0,1:T(8,128)(2,1)} collective-permute-done((bf16[512,1024]{0,1:T(8,128)(2,1)S(1)}, bf16[512,1024]{0,1:T(8,128)(2,1)}, u32[]{:S(2)}, u32[]{:S(2)}) %collective-permute-start.7) | collective-permute-done | bytes 1048608 | tf_op jit(solution)/shard_map/ppermute | solution.py:239
  105.1 14.8 %collective-permute-done.6.error = bf16[512,1024]{1,0:T(8,128)(2,1)} collective-permute-done((bf16[512,1024]{1,0:T(8,128)(2,1)}, bf16[512,1024]{1,0:T(8,128)(2,1)}, u32[]{:S(2)}, u32[]{:S(2)}) %collective-permute-start.6) | collective-permute-done | bytes 1048608 | tf_op jit(solution)/shard_map/ppermute | solution.py:239
  119.9 13.8 %shard_map.88 = (bf16[2,1024,1024]{2,1,0:T(8,128)(2,1)}, bf16[2,1024,1024]{2,1,0:T(8,128)(2,1)}) custom-call(bf16[512,1024]{1,0:T(8,128)(2,1)} %collective-permute-done.6.error, f32[2,1024,1024]{2,1,0:T(8,128)} %refs_0_.5, bf16[512,1024]{1,0:T(8,128)(2,1)} %copy-done.9, bf16[512,1024]{1,0:T(8,128)(2,1)} %copy-done.8, bf16[1024,512]{1,0:T(8,128)(2,1)} %bitcast.13.inputs_t, ...), custom_call_target="tpu_custom_call" | custom-call | flops 3221225472 | bytes 29360128 | tf_op jit(solution)/shard_map/pallas_call | solution.py:124
  133.6 5.6 %shard_map.89 = (bf16[512,1024]{1,0:T(8,128)(2,1)S(1)}, bf16[512,1024]{1,0:T(8,128)(2,1)S(1)}, bf16[512,1024]{1,0:T(8,128)(2,1)S(1)}) custom-call(s32[1]{0:T(128)} %bitcast.flag, bf16[512,1024]{1,0:T(8,128)(2,1)S(1)} %gather_fusion.2, bf16[2,1024,1024]{2,1,0:T(8,128)(2,1)} %get-tuple-element.57.refs_0_.weights.refs_1_), custom_call_target="tpu_custom_call" | custom-call | flops 2147483648 | bytes 16777216 | tf_op jit(solution)/shard_map/pallas_call | solution.py:74
  147.9 5.7 %collective-permute-done.10 = bf16[128,1024]{1,0:T(8,128)(2,1)} collective-permute-done((bf16[128,1024]{1,0:T(8,128)(2,1)}, bf16[128,1024]{1,0:T(8,128)(2,1)}, u32[]{:S(2)}, u32[]{:S(2)}) %collective-permute-start.10) | collective-permute-done | bytes 262176 | tf_op jit(solution)/shard_map/ppermute | solution.py:21
  170.8 14.2 %shard_map.90 = (f32[2,1024,1024]{2,1,0:T(8,128)}, bf16[2,1024,1024]{2,1,0:T(8,128)(2,1)}, bf16[2,1024,1024]{2,1,0:T(8,128)(2,1)}) custom-call(bf16[512,1024]{1,0:T(8,128)(2,1)} %pad_maximum_fusion.1.error, bf16[2,1024,1024]{2,1,0:T(8,128)(2,1)} %get-tuple-element.57.refs_0_.weights.refs_1_, bf16[512,1024]{1,0:T(8,128)(2,1)} %copy-done.5, ...), custom_call_target="tpu_custom_call" | custom-call | flops 3221225472 | bytes 29360128 | tf_op jit(solution)/shard_map/pallas_call | solution.py:124
  195.3 9.4 %shard_map.91 = (bf16[512,1024]{1,0:T(8,128)(2,1)S(1)}, bf16[512,1024]{1,0:T(8,128)(2,1)S(1)}, bf16[2,1024,1024]{2,1,0:T(8,128)(2,1)}) custom-call(s32[1]{0:T(128)} %bitcast.flag, bf16[512,1024]{1,0:T(8,128)(2,1)S(1)} %copy.29.inputs, f32[2,1024,1024]{2,1,0:T(8,128)} %refs_0_.5, bf16[2,1024,1024]{2,1,0:T(8,128)(2,1)} %collective-permute-done.18.refs_1_.refs_0_, ...), custom_call_target="tpu_custom_call" | custom-call | flops 1073741824 | bytes 16777216 | tf_op jit(solution)/shard_map/pallas_call | solution.py:74
  206.6 10.1 %shard_map.92.refs_2_ = bf16[2,1024,1024]{2,1,0:T(8,128)(2,1)} custom-call(bf16[512,1024]{1,0:T(8,128)(2,1)} %collective-permute-done.16.error, bf16[2,1024,1024]{2,1,0:T(8,128)(2,1)} %get-tuple-element.66.weights.refs_1_, bf16[512,1024]{1,0:T(8,128)(2,1)} %copy-done.11, bf16[512,1024]{1,0:T(8,128)(2,1)} %copy-done.10, bf16[1024,512]{1,0:T(8,128)(2,1)} %bitcast.20.inputs_t, ...), custom_call_target="tpu_custom_call" | custom-call | flops 3221225472 | bytes 29360128 | tf_op jit(solution)/shard_map/pallas_call | solution.py:124
  216.7 42.1 %collective-permute-done.15.refs_1_ = bf16[2,1024,1024]{2,1,0:T(8,128)(2,1)} collective-permute-done((bf16[2,1024,1024]{2,1,0:T(8,128)(2,1)}, bf16[2,1024,1024]{2,1,0:T(8,128)(2,1)}, u32[]{:S(2)}, u32[]{:S(2)}) %collective-permute-start.15) | collective-permute-done | bytes 4194336 | tf_op jit(solution)/shard_map/ppermute | solution.py:239
  258.8 8.8 %shard_map.93 = (bf16[512,1024]{1,0:T(8,128)(2,1)S(1)}, bf16[512,1024]{1,0:T(8,128)(2,1)S(1)}, bf16[512,1024]{1,0:T(8,128)(2,1)S(1)}, bf16[2,1024,1024]{2,1,0:T(8,128)(2,1)}) custom-call(s32[1]{0:T(128)} %bitcast.flag, bf16[512,1024]{1,0:T(8,128)(2,1)S(1)} %gather_fusion.1, bf16[2,1024,1024]{2,1,0:T(8,128)(2,1)} %get-tuple-element.61.refs_0_, ...), custom_call_target="tpu_custom_call" | custom-call | flops 2147483648 | bytes 16777216 | tf_op jit(solution)/shard_map/pallas_call | solution.py:74
  279.6 6.7 %collective-permute-done.22 = bf16[128,1024]{1,0:T(8,128)(2,1)} collective-permute-done((bf16[128,1024]{1,0:T(8,128)(2,1)}, bf16[128,1024]{1,0:T(8,128)(2,1)}, u32[]{:S(2)}, u32[]{:S(2)}) %collective-permute-start.22) | collective-permute-done | bytes 262176 | tf_op jit(solution)/shard_map/ppermute | solution.py:21
  299.5 12.8 %shard_map.94 = (f32[2,1024,1024]{2,1,0:T(8,128)}, bf16[2,1024,1024]{2,1,0:T(8,128)(2,1)}) custom-call(bf16[512,1024]{1,0:T(8,128)(2,1)} %pad_maximum_fusion.2.error, bf16[2,1024,1024]{2,1,0:T(8,128)(2,1)} %get-tuple-element.70.weights, bf16[512,1024]{1,0:T(8,128)(2,1)} %copy-done.3, bf16[512,1024]{1,0:T(8,128)(2,1)} %copy-done.2, ...), custom_call_target="tpu_custom_call" | custom-call | flops 3221225472 | bytes 29360128 | tf_op jit(solution)/shard_map/pallas_call | solution.py:124
  323.8 5.3 %collective-permute-done.36 = bf16[128,1024]{1,0:T(8,128)(2,1)S(1)} collective-permute-done((bf16[128,1024]{1,0:T(8,128)(2,1)S(1)}, bf16[128,1024]{1,0:T(8,128)(2,1)S(1)}, u32[]{:S(2)}, u32[]{:S(2)}) %collective-permute-start.36) | collective-permute-done | bytes 262176 | tf_op jit(solution)/shard_map/ppermute | solution.py:184
  329.9 7.0 %collective-permute-start.38 = (bf16[128,1024]{1,0:T(8,128)(2,1)S(1)}, bf16[128,1024]{1,0:T(8,128)(2,1)S(1)}, u32[]{:S(2)}, u32[]{:S(2)}) collective-permute-start(bf16[128,1024]{1,0:T(8,128)(2,1)S(1)} %get-tuple-element.79), channel_id=1, source_target_pairs={{0,8},{4,12},{24,16},{28,20},{1,9},{5,13},{25,17},{29,21},{2,10},{... | collective-permute-start | bytes 786440 | tf_op jit(solution)/shard_map/ppermute | solution.py:184
  342.5 5.9 %collective-permute-start.48 = (bf16[128,1024]{1,0:T(8,128)(2,1)S(1)}, bf16[128,1024]{1,0:T(8,128)(2,1)S(1)}, u32[]{:S(2)}, u32[]{:S(2)}) collective-permute-start(bf16[128,1024]{1,0:T(8,128)(2,1)S(1)} %get-tuple-element.85), channel_id=1, source_target_pairs={{0,8},{4,12},{24,16},{28,20},{1,9},{5,13},{25,17},{29,21},{2,10},{... | collective-permute-start | bytes 786440 | tf_op jit(solution)/shard_map/ppermute | solution.py:184
  350.8 6.7 %collective-permute-start.43 = (bf16[128,1024]{1,0:T(8,128)(2,1)S(1)}, bf16[128,1024]{1,0:T(8,128)(2,1)S(1)}, u32[]{:S(2)}, u32[]{:S(2)}) collective-permute-start(bf16[128,1024]{1,0:T(8,128)(2,1)S(1)} %get-tuple-element.82), channel_id=1, source_target_pairs={{0,8},{4,12},{24,16},{28,20},{1,9},{5,13},{25,17},{29,21},{2,10},{... | collective-permute-start | bytes 786440 | tf_op jit(solution)/shard_map/ppermute | solution.py:184
  359.7 7.1 %collective-permute-start.57 = (bf16[128,1024]{1,0:T(8,128)(2,1)S(1)}, bf16[128,1024]{1,0:T(8,128)(2,1)S(1)}, u32[]{:S(2)}, u32[]{:S(2)}) collective-permute-start(bf16[128,1024]{1,0:T(8,128)(2,1)S(1)} %get-tuple-element.91), channel_id=1, source_target_pairs={{0,8},{4,12},{24,16},{28,20},{1,9},{5,13},{25,17},{29,21},{2,10},{... | collective-permute-start | bytes 786440 | tf_op jit(solution)/shard_map/ppermute | solution.py:184
  368.9 6.5 %collective-permute-start.53 = (bf16[128,1024]{1,0:T(8,128)(2,1)S(1)}, bf16[128,1024]{1,0:T(8,128)(2,1)S(1)}, u32[]{:S(2)}, u32[]{:S(2)}) collective-permute-start(bf16[128,1024]{1,0:T(8,128)(2,1)S(1)} %get-tuple-element.88), channel_id=1, source_target_pairs={{0,8},{4,12},{24,16},{28,20},{1,9},{5,13},{25,17},{29,21},{2,10},{... | collective-permute-start | bytes 786440 | tf_op jit(solution)/shard_map/ppermute | solution.py:184
  411.8 9.0 %multiply_subtract_fusion = (f32[2,1024,1024]{2,1,0:T(8,128)}, f32[2,1024,1024]{2,1,0:T(8,128)}) fusion(f32[2,1024,1024]{2,1,0:T(8,128)S(1)} %bitcast.137, bf16[2,1024,1024]{2,1,0:T(8,128)(2,1)} %maximum_dynamic-update-slice_fusion, f32[2,1024,1024]{2,1,0:T(8,128)S(1)} %bitcast.140), kind=kLoop, calls=%fused_computation.7 | loop fusion | flops 12582912 | bytes 37748736 | tf_op jit(solution)/shard_map/sub | solution.py:279
  (241 shorter events, 168.1 us)
Async XLA Ops:
  6.8 113.0 %collective-permute-start.8 = (bf16[2,1024,1024]{2,1,0:T(8,128)(2,1)}, bf16[2,1024,1024]{2,1,0:T(8,128)(2,1)}, u32[]{:S(2)}, u32[]{:S(2)}) collective-permute-start(bf16[2,1024,1024]{2,1,0:T(8,128)(2,1)} %bitcast_convert_fusion), channel_id=1, source_target_pairs={{28,0},{0,4},{4,8},{8,12},{12,16},{16,20},{20,24},{24,28},{29,1},{... | collective-permute-start | bytes 12582920 | tf_op jit(solution)/shard_map/ppermute | solution.py:239
  21.5 14.8 %collective-permute-start.1 = (bf16[128,1024]{1,0:T(8,128)(2,1)}, bf16[128,1024]{1,0:T(8,128)(2,1)}, u32[]{:S(2)}, u32[]{:S(2)}) collective-permute-start(bf16[128,1024]{1,0:T(8,128)(2,1)} %get-tuple-element.125), channel_id=1, source_target_pairs={{0,2},{1,3},{2,0},{3,1},{4,6},{5,7},{6,4},{7,5},{8,10},{9,11},{10,... | collective-permute-start | bytes 786440 | tf_op jit(solution)/shard_map/ppermute | solution.py:21
  23.1 13.2 %collective-permute-start.2 = (bf16[128,1024]{1,0:T(8,128)(2,1)}, bf16[128,1024]{1,0:T(8,128)(2,1)}, u32[]{:S(2)}, u32[]{:S(2)}) collective-permute-start(bf16[128,1024]{1,0:T(8,128)(2,1)} %get-tuple-element.124), channel_id=1, source_target_pairs={{0,3},{1,2},{2,1},{3,0},{4,7},{5,6},{6,5},{7,4},{8,11},{9,10},{10,... | collective-permute-start | bytes 786440 | tf_op jit(solution)/shard_map/ppermute | solution.py:21
  39.0 13.3 %collective-permute-start.4 = (bf16[128,1024]{1,0:T(8,128)(2,1)}, bf16[128,1024]{1,0:T(8,128)(2,1)S(1)}, u32[]{:S(2)}, u32[]{:S(2)}) collective-permute-start(bf16[128,1024]{1,0:T(8,128)(2,1)} %multiply_convert_fusion.2), channel_id=1, source_target_pairs={{0,2},{1,3},{2,0},{3,1},{4,6},{5,7},{6,4},{7,5},{8,10},{9,11},{10,... | collective-permute-start | bytes 786440 | tf_op jit(solution)/shard_map/ppermute | solution.py:21
  40.4 13.4 %collective-permute-start.5 = (bf16[128,1024]{1,0:T(8,128)(2,1)}, bf16[128,1024]{1,0:T(8,128)(2,1)S(1)}, u32[]{:S(2)}, u32[]{:S(2)}) collective-permute-start(bf16[128,1024]{1,0:T(8,128)(2,1)} %multiply_convert_fusion.2), channel_id=1, source_target_pairs={{0,3},{1,2},{2,1},{3,0},{4,7},{5,6},{6,5},{7,4},{8,11},{9,10},{10,... | collective-permute-start | bytes 786440 | tf_op jit(solution)/shard_map/ppermute | solution.py:21
  66.5 98.5 %collective-permute-start.19 = (bf16[2,1024,1024]{2,1,0:T(8,128)(2,1)}, bf16[2,1024,1024]{2,1,0:T(8,128)(2,1)}, u32[]{:S(2)}, u32[]{:S(2)}) collective-permute-start(bf16[2,1024,1024]{2,1,0:T(8,128)(2,1)} %get-tuple-element.65), channel_id=1, source_target_pairs={{24,0},{0,8},{8,16},{16,24},{25,1},{1,9},{9,17},{17,25},{26,2},{2,... | collective-permute-start | bytes 12582920 | tf_op jit(solution)/shard_map/ppermute | solution.py:239
  70.0 27.4 %collective-permute-start.7 = (bf16[512,1024]{0,1:T(8,128)(2,1)S(1)}, bf16[512,1024]{0,1:T(8,128)(2,1)}, u32[]{:S(2)}, u32[]{:S(2)}) collective-permute-start(bf16[512,1024]{0,1:T(8,128)(2,1)S(1)} %copy-done.14), channel_id=1, source_target_pairs={{28,0},{0,4},{4,8},{8,12},{12,16},{16,20},{20,24},{24,28},{29,1},{... | collective-permute-start | bytes 3145736 | tf_op jit(solution)/shard_map/ppermute | solution.py:239
  70.1 49.8 %collective-permute-start.6 = (bf16[512,1024]{1,0:T(8,128)(2,1)}, bf16[512,1024]{1,0:T(8,128)(2,1)}, u32[]{:S(2)}, u32[]{:S(2)}) collective-permute-start(bf16[512,1024]{1,0:T(8,128)(2,1)} %pad_maximum_fusion.error), channel_id=1, source_target_pairs={{28,0},{0,4},{4,8},{8,12},{12,16},{16,20},{20,24},{24,28},{29,1},{... | collective-permute-start | bytes 3145736 | tf_op jit(solution)/shard_map/ppermute | solution.py:239
  161.7 33.6 %collective-permute-start.18 = (bf16[2,1024,1024]{2,1,0:T(8,128)(2,1)}, bf16[2,1024,1024]{2,1,0:T(8,128)(2,1)}, u32[]{:S(2)}, u32[]{:S(2)}) collective-permute-start(bf16[2,1024,1024]{2,1,0:T(8,128)(2,1)} %get-tuple-element.64), channel_id=1, source_target_pairs={{0,4},{8,12},{16,20},{24,28},{1,5},{9,13},{17,21},{25,29},{2,6},{1... | collective-permute-start | bytes 12582920 | tf_op jit(solution)/shard_map/ppermute | solution.py:239
  165.0 30.3 %collective-permute-start.20 = (bf16[2,1024,1024]{2,1,0:T(8,128)(2,1)}, bf16[2,1024,1024]{2,1,0:T(8,128)(2,1)}, u32[]{:S(2)}, u32[]{:S(2)}) collective-permute-start(bf16[2,1024,1024]{2,1,0:T(8,128)(2,1)} %collective-permute-done.19), channel_id=1, source_target_pairs={{0,4},{8,12},{16,20},{24,28},{1,5},{9,13},{17,21},{25,29},{2,6},{1... | collective-permute-start | bytes 12582920 | tf_op jit(solution)/shard_map/ppermute | solution.py:239
  185.0 73.8 %collective-permute-start.15 = (bf16[2,1024,1024]{2,1,0:T(8,128)(2,1)}, bf16[2,1024,1024]{2,1,0:T(8,128)(2,1)}, u32[]{:S(2)}, u32[]{:S(2)}) collective-permute-start(bf16[2,1024,1024]{2,1,0:T(8,128)(2,1)} %get-tuple-element.61.refs_0_), channel_id=1, source_target_pairs={{24,0},{0,8},{8,16},{16,24},{25,1},{1,9},{9,17},{17,25},{26,2},{2,... | collective-permute-start | bytes 12582920 | tf_op jit(solution)/shard_map/ppermute | solution.py:239
  189.9 16.8 %collective-permute-start.16 = (bf16[512,1024]{1,0:T(8,128)(2,1)S(1)}, bf16[512,1024]{1,0:T(8,128)(2,1)}, u32[]{:S(2)}, u32[]{:S(2)}) collective-permute-start(bf16[512,1024]{1,0:T(8,128)(2,1)S(1)} %copy-done.13), channel_id=1, source_target_pairs={{28,4},{4,12},{12,20},{20,28},{29,5},{5,13},{13,21},{21,29},{30,6}... | collective-permute-start | bytes 3145736 | tf_op jit(solution)/shard_map/ppermute | solution.py:239
  272.4 13.9 %collective-permute-start.22 = (bf16[128,1024]{1,0:T(8,128)(2,1)}, bf16[128,1024]{1,0:T(8,128)(2,1)}, u32[]{:S(2)}, u32[]{:S(2)}) collective-permute-start(bf16[128,1024]{1,0:T(8,128)(2,1)} %get-tuple-element.119), channel_id=1, source_target_pairs={{0,2},{1,3},{2,0},{3,1},{4,6},{5,7},{6,4},{7,5},{8,10},{9,11},{10,... | collective-permute-start | bytes 786440 | tf_op jit(solution)/shard_map/ppermute | solution.py:21
  273.4 13.0 %collective-permute-start.23 = (bf16[128,1024]{1,0:T(8,128)(2,1)}, bf16[128,1024]{1,0:T(8,128)(2,1)}, u32[]{:S(2)}, u32[]{:S(2)}) collective-permute-start(bf16[128,1024]{1,0:T(8,128)(2,1)} %get-tuple-element.118), channel_id=1, source_target_pairs={{0,3},{1,2},{2,1},{3,0},{4,7},{5,6},{6,5},{7,4},{8,11},{9,10},{10,... | collective-permute-start | bytes 786440 | tf_op jit(solution)/shard_map/ppermute | solution.py:21
  322.5 14.4 %collective-permute-start.28 = (bf16[128,1024]{1,0:T(8,128)(2,1)S(1)}, bf16[128,1024]{1,0:T(8,128)(2,1)S(1)}, u32[]{:S(2)}, u32[]{:S(2)}) collective-permute-start(bf16[128,1024]{1,0:T(8,128)(2,1)S(1)} %get-tuple-element.108), channel_id=1, source_target_pairs={{0,8},{4,12},{24,16},{28,20},{1,9},{5,13},{25,17},{29,21},{2,10},{... | collective-permute-start | bytes 786440 | tf_op jit(solution)/shard_map/ppermute | solution.py:184
  337.0 12.8 %collective-permute-start.31 = (bf16[128,1024]{1,0:T(8,128)(2,1)S(1)}, bf16[128,1024]{1,0:T(8,128)(2,1)S(1)}, u32[]{:S(2)}, u32[]{:S(2)}) collective-permute-start(bf16[128,1024]{1,0:T(8,128)(2,1)S(1)} %reduce-precision_convert_fusion.15), channel_id=1, source_target_pairs={{8,16},{12,20},{16,8},{20,12},{9,17},{13,21},{17,9},{21,13},{10,18... | collective-permute-start | bytes 786440 | tf_op jit(solution)/shard_map/ppermute | solution.py:184
  341.9 15.6 %collective-permute-start.49 = (bf16[128,1024]{1,0:T(8,128)(2,1)S(1)}, bf16[128,1024]{1,0:T(8,128)(2,1)S(1)}, u32[]{:S(2)}, u32[]{:S(2)}) collective-permute-start(bf16[128,1024]{1,0:T(8,128)(2,1)S(1)} %reduce-precision_convert_fusion.11), channel_id=1, source_target_pairs={{8,16},{12,20},{16,8},{20,12},{9,17},{13,21},{17,9},{21,13},{10,18... | collective-permute-start | bytes 786440 | tf_op jit(solution)/shard_map/ppermute | solution.py:184
  342.5 16.3 %collective-permute-start.48 = (bf16[128,1024]{1,0:T(8,128)(2,1)S(1)}, bf16[128,1024]{1,0:T(8,128)(2,1)S(1)}, u32[]{:S(2)}, u32[]{:S(2)}) collective-permute-start(bf16[128,1024]{1,0:T(8,128)(2,1)S(1)} %get-tuple-element.85), channel_id=1, source_target_pairs={{0,8},{4,12},{24,16},{28,20},{1,9},{5,13},{25,17},{29,21},{2,10},{... | collective-permute-start | bytes 786440 | tf_op jit(solution)/shard_map/ppermute | solution.py:184
  350.0 16.8 %collective-permute-start.44 = (bf16[128,1024]{1,0:T(8,128)(2,1)S(1)}, bf16[128,1024]{1,0:T(8,128)(2,1)S(1)}, u32[]{:S(2)}, u32[]{:S(2)}) collective-permute-start(bf16[128,1024]{1,0:T(8,128)(2,1)S(1)} %reduce-precision_convert_fusion.14), channel_id=1, source_target_pairs={{8,16},{12,20},{16,8},{20,12},{9,17},{13,21},{17,9},{21,13},{10,18... | collective-permute-start | bytes 786440 | tf_op jit(solution)/shard_map/ppermute | solution.py:184
  350.8 17.3 %collective-permute-start.43 = (bf16[128,1024]{1,0:T(8,128)(2,1)S(1)}, bf16[128,1024]{1,0:T(8,128)(2,1)S(1)}, u32[]{:S(2)}, u32[]{:S(2)}) collective-permute-start(bf16[128,1024]{1,0:T(8,128)(2,1)S(1)} %get-tuple-element.82), channel_id=1, source_target_pairs={{0,8},{4,12},{24,16},{28,20},{1,9},{5,13},{25,17},{29,21},{2,10},{... | collective-permute-start | bytes 786440 | tf_op jit(solution)/shard_map/ppermute | solution.py:184
  359.0 16.6 %collective-permute-start.58 = (bf16[128,1024]{1,0:T(8,128)(2,1)S(1)}, bf16[128,1024]{1,0:T(8,128)(2,1)S(1)}, u32[]{:S(2)}, u32[]{:S(2)}) collective-permute-start(bf16[128,1024]{1,0:T(8,128)(2,1)S(1)} %reduce-precision_convert_fusion.7), channel_id=1, source_target_pairs={{8,16},{12,20},{16,8},{20,12},{9,17},{13,21},{17,9},{21,13},{10,18... | collective-permute-start | bytes 786440 | tf_op jit(solution)/shard_map/ppermute | solution.py:184
  359.7 17.3 %collective-permute-start.57 = (bf16[128,1024]{1,0:T(8,128)(2,1)S(1)}, bf16[128,1024]{1,0:T(8,128)(2,1)S(1)}, u32[]{:S(2)}, u32[]{:S(2)}) collective-permute-start(bf16[128,1024]{1,0:T(8,128)(2,1)S(1)} %get-tuple-element.91), channel_id=1, source_target_pairs={{0,8},{4,12},{24,16},{28,20},{1,9},{5,13},{25,17},{29,21},{2,10},{... | collective-permute-start | bytes 786440 | tf_op jit(solution)/shard_map/ppermute | solution.py:184
  384.6 13.1 %collective-permute-start.55 = (bf16[128,1024]{1,0:T(8,128)(2,1)S(1)}, bf16[128,1024]{1,0:T(8,128)(2,1)S(1)}, u32[]{:S(2)}, u32[]{:S(2)}) collective-permute-start(bf16[128,1024]{1,0:T(8,128)(2,1)S(1)} %reduce-precision_convert_fusion.4), channel_id=1, source_target_pairs={{8,0},{12,4},{16,24},{20,28},{9,1},{13,5},{17,25},{21,29},{10,2},{... | collective-permute-start | bytes 786440 | tf_op jit(solution)/shard_map/ppermute | solution.py:184
  385.9 13.2 %collective-permute-start.52 = (bf16[128,1024]{1,0:T(8,128)(2,1)S(1)}, bf16[128,1024]{1,0:T(8,128)(2,1)S(1)}, u32[]{:S(2)}, u32[]{:S(2)}) collective-permute-start(bf16[128,1024]{1,0:T(8,128)(2,1)S(1)} %broadcast_select_fusion.4), channel_id=1, source_target_pairs={{0,4},{4,0},{8,12},{12,8},{16,20},{20,16},{24,28},{28,24},{1,5},{5... | collective-permute-start | bytes 786440 | tf_op jit(solution)/shard_map/ppermute | solution.py:21
  (64 other events, 577.7 us)

commit v4 on v3

v4 whole, which is shorter than its diff:
```python
import functools

import jax
import jax.numpy as jnp
from jax import lax
from jax.experimental import pallas as pl
from jax.experimental.pallas import tpu as pltpu
from jax.sharding import PartitionSpec as P

INNER = 3


learn_rate = 0.02
inner_beta = 0.9
slow_beta = 0.5
chunks = 8
bf16, f32 = jnp.bfloat16, jnp.float32


def swapped(block, axis, mask):
    return lax.ppermute(block, axis, [(i, i ^ mask) for i in range(lax.axis_size(axis))])


def gelu_pair(pre):
    coeff = 0.7978845608028654
    square = pre * pre
    tanh_val = jnp.tanh(coeff * (pre + 0.044715 * square * pre))
    half = 0.5 * (1.0 + tanh_val)
    slope = half + 0.5 * pre * (1.0 - tanh_val * tanh_val) * coeff * (1.0 + 3.0 * 0.044715 * square)
    return (pre * half, slope)


def whole(shape):
    return pl.BlockSpec(shape, lambda j: (0,) * len(shape))


def forward_kernel(mix, taken, sums, emits, flag, inputs, *refs):
    sources, refs = refs[:taken], list(refs[taken:])
    hidden, slope = refs[:2]
    block = mix(flag[0], *[source[...].astype(f32) for source in sources]).astype(bf16)
    if emits:
        refs[2 + sums][...] = block
    j = pl.program_id(0)
    value, slope_val = gelu_pair(jnp.dot(inputs[...], block[0], preferred_element_type=f32))
    value = value.astype(bf16)
    hidden[...] = value
    slope[...] = slope_val.astype(bf16)
    if sums:
        partials, total = refs[2 : 2 + sums], refs[-1]
        out = lax.dot_general(value, block[1], (((1,), (1,)), ((), ())), preferred_element_type=f32)

        @pl.when(j == 0)
        def _():
            total[...] = out

        @pl.when(j > 0)
        def _():
            total[...] += out

        @pl.when(j == pl.num_programs(0) - 1)
        def _():
            size = partials[0].shape[0]
            for b, partial in enumerate(partials):
                partial[...] = total[b * size : (b + 1) * size].astype(bf16)


def forward(flag, inputs, sources, mix, sums, emits=True):
    rows, width = inputs.shape
    units = sources[0].shape[2]
    block = min(units, 512)
    parts = 2 if sums or emits else 1
    weight_spec = pl.BlockSpec((parts, width, block), lambda j: (0, 0, j))
    unit_spec = pl.BlockSpec((rows, block), lambda j: (0, j))
    shapes = [((rows, units), unit_spec), ((rows, units), unit_spec)]
    if sums:
        shapes += [((rows // sums, width), whole((rows // sums, width)))] * sums
    shapes += [(sources[0].shape, weight_spec)] * emits
    return pl.pallas_call(
        functools.partial(forward_kernel, mix, len(sources), sums, emits),
        grid=(units // block,),
        in_specs=[pl.BlockSpec(memory_space=pltpu.SMEM), whole((rows, width))] + [weight_spec] * len(sources),
        out_specs=[spec for _, spec in shapes],
        out_shape=[jax.ShapeDtypeStruct(shape, bf16) for shape, _ in shapes],
        scratch_shapes=[pltpu.VMEM((rows, width), f32)] * bool(sums),
        compiler_params=pltpu.CompilerParams(vmem_limit_bytes=48 << 20),
        cost_estimate=pl.CostEstimate(
            flops=(2 + 2 * bool(sums)) * rows * width * units,
            bytes_accessed=16 * width * units,
            transcendentals=rows * units,
        ),
    )(flag, inputs, *sources)


def only(flag, weights):
    return weights


def pushed(flag, weights, first, second):
    return weights - 0.5 * learn_rate * (first + second)


def halved(flag, weights, sent, found):
    return 0.5 * (weights + jnp.where(flag == 0, sent, found))


def backward_kernel(update, taken, pieces, weights, slope, hidden, inputs_t, *refs):
    states, refs = refs[:taken], refs[taken:]
    errors, results, error, error_t = refs[:pieces], refs[pieces:-2], refs[-2], refs[-1]

    @pl.when(pl.program_id(0) == 0)
    def _():
        size = errors[0].shape[0]
        for b, piece in enumerate(errors):
            error[b * size : (b + 1) * size] = piece[...]
        error_t[...] = error[...].T

    back = jnp.dot(error[...], weights[0].astype(bf16), preferred_element_type=f32) * slope[...].astype(f32)
    for k, (left, right) in enumerate(((inputs_t[...], back.astype(bf16)), (error_t[...], hidden[...]))):
        grad = jnp.dot(left, right, preferred_element_type=f32)
        values = update(grad, *[state[k].astype(f32) for state in states])
        for result, value in zip(results, values):
            result[k] = value.astype(result.dtype)


def backward(errors, weights, slope, hidden, inputs_t, states, update, kinds):
    width, rows = inputs_t.shape
    units = weights.shape[2]
    block = min(units, 512)
    both = pl.BlockSpec((2, width, block), lambda j: (0, 0, j))
    out_only = pl.BlockSpec((1, width, block), lambda j: (1, 0, j))
    unit_spec = pl.BlockSpec((rows, block), lambda j: (0, j))
    return pl.pallas_call(
        functools.partial(backward_kernel, update, len(states), len(errors)),
        grid=(units // block,),
        in_specs=[out_only, unit_spec, unit_spec, whole((width, rows))]
        + [both] * len(states)
        + [whole(piece.shape) for piece in errors],
        out_specs=[both] * len(kinds),
        out_shape=[jax.ShapeDtypeStruct(weights.shape, kind) for kind in kinds],
        scratch_shapes=[pltpu.VMEM((rows, width), bf16), pltpu.VMEM((width, rows), bf16)],
        compiler_params=pltpu.CompilerParams(vmem_limit_bytes=56 << 20),
        cost_estimate=pl.CostEstimate(
            flops=6 * rows * width * units, bytes_accessed=28 * width * units, transcendentals=0
        ),
    )(weights, slope, hidden, inputs_t, *states, *errors)


def first_update(grad, moment):
    moment = inner_beta * moment + grad
    return (moment, moment)


def first_beside(grad, moment, own_moment, weights):
    moment = inner_beta * moment + grad
    return (moment, weights - 0.5 * learn_rate * (own_moment + moment))


def second_update(grad, moment, weights):
    moment_new = inner_beta * moment + grad
    return (moment_new, weights - learn_rate * moment_new, moment + (1.0 + inner_beta) * moment_new)


def second_beside(grad, moment, weights):
    return (weights - learn_rate * (inner_beta * moment + grad),)


def third_update(grad, moment, known):
    return (inner_beta * moment + grad, known + grad)


def rounded(value):
    return lax.reduce_precision(value, 8, 7).astype(bf16)


def added(left, right):
    return rounded(left.astype(f32) + right.astype(f32))


def tied(early, late):
    return lax.optimization_barrier((early, late))[1]


def finish_kernel(replicas, flag, slow, anchor, own, theirs, *refs):
    anchor_new, slow_new = refs[-2:]
    for k in range(2):
        total = jnp.where(flag[0] == k, own[...].astype(f32), theirs[...].astype(f32))
        value = slow_beta * slow[k] + total / replicas
        slow_new[k] = value
        anchor_new[k] = anchor[k] - learn_rate * value


def finish(flag, replicas, slow, anchor, own, theirs, position, before):
    size, units = own.shape
    rows = pl.BlockSpec((2, size, units), lambda j: (0, position, 0))
    shape = jax.ShapeDtypeStruct(slow.shape, f32)
    return pl.pallas_call(
        functools.partial(finish_kernel, replicas),
        grid=(1,),
        in_specs=[pl.BlockSpec(memory_space=pltpu.SMEM), rows, rows, whole(own.shape), whole(own.shape)]
        + [pl.BlockSpec(memory_space=pl.ANY)] * len(before),
        out_specs=[rows, rows],
        out_shape=[shape, shape],
        input_output_aliases={5 + k: k for k in range(len(before))},
        compiler_params=pltpu.CompilerParams(vmem_limit_bytes=32 << 20),
        cost_estimate=pl.CostEstimate(flops=8 * size * units, bytes_accessed=36 * size * units, transcendentals=0),
    )(flag, slow, anchor, own, theirs, *before)


def slow_step(flag, total, slow, anchor):
    axis, cores = "replica", 2
    index = lax.axis_index(axis)
    replicas = lax.axis_size(axis)
    core, chip = index % cores, index // cores
    length = replicas // cores
    half = length // 2
    mine = lax.dynamic_index_in_dim(total, core, 0, keepdims=False)
    other = lax.dynamic_index_in_dim(total, 1 - core, 0, keepdims=False)
    size = mine.shape[0] // chunks

    def moved(part, hops):
        return lax.ppermute(part, axis, [(cores * a + c, cores * b + c) for a, b in hops for c in range(cores)])

    def at(*places):
        return functools.reduce(jnp.logical_or, [chip == place for place in places])

    blocks = []
    for c in range(chunks):
        part = slice(c * size, (c + 1) * size)
        blocks.append(added(mine[part], swapped(other[part], axis, 1)))
    lag = 2
    middle = lag * max(half - 1, 0)
    last = chunks - 1 + 2 * middle
    ticks, results = [], []
    for tick in range(last + 1):
        live = list(range(max(0, tick - 2 * middle), min(chunks, tick + 1)))
        if tick >= lag:
            for c, block in zip(live, tied(ticks[tick - lag], [blocks[c] for c in live])):
                blocks[c] = block
        arrivals, steps = [], []
        for s in range(half):
            inward = tick - lag * s
            outward = inward if s == half - 1 else tick - 2 * middle + lag * s
            inward = inward if 0 <= inward < chunks else None
            outward = outward if 0 <= outward < chunks else None
            if inward is None and outward is None:
                continue
            if s == half - 1:
                arrived = moved(blocks[inward], [(s, s + 1), (s + 1, s)])
            else:
                hops = []
                if inward is not None:
                    hops += [(s, s + 1), (length - 1 - s, length - 2 - s)]
                if outward is not None:
                    hops += [(s + 1, s), (length - 2 - s, length - 1 - s)]
                if inward is None or outward is None:
                    sent = blocks[outward if inward is None else inward]
                else:
                    sent = jnp.where(at(s, length - 1 - s), blocks[inward], blocks[outward])
                arrived = moved(sent, hops)
            arrivals.append(arrived)
            steps.append((s, inward, outward))
        ticks.append(arrivals)
        for (s, inward, outward), arrived in zip(steps, arrivals):
            if s == half - 1:
                blocks[inward] = jnp.where(at(s, s + 1), added(blocks[inward], arrived), blocks[inward])
                continue
            if inward is not None:
                blocks[inward] = jnp.where(at(s + 1, length - 2 - s), added(blocks[inward], arrived), blocks[inward])
            if outward is not None:
                blocks[outward] = jnp.where(at(s, length - 1 - s), arrived, blocks[outward])
        if tick >= 2 * middle:
            done = tick - 2 * middle
            theirs = swapped(blocks[done], axis, 1)
            results = finish(flag, replicas, slow, anchor, blocks[done], theirs, done, results)
    return results


def body(tokens, targets, row_ids, anchor, momentum, slow):
    row_count = tokens.shape[0]
    scale = 1.0 / row_count
    tensors = lax.axis_size("tensor")
    share_rows = row_count // tensors
    order = lax.axis_index("tensor") ^ jnp.arange(tensors)
    picks_all = row_ids[0].reshape(INNER, tensors, share_rows)[:, order].reshape(INNER, row_count)

    replicas = lax.axis_size("replica")
    flag = (lax.axis_index("replica") % 2).astype(jnp.int32).reshape(1)

    def errors_of(partials, step):
        wanted = targets.at[picks_all[step, :share_rows]].get(mode="promise_in_bounds")
        share = partials[0].astype(f32)
        for m in range(1, tensors):
            share = share + swapped(partials[m], "tensor", m).astype(f32)
        own = ((share - wanted.astype(f32)) * scale).astype(bf16)
        return [own] + [swapped(own, "tensor", m) for m in range(1, tensors)]

    def sent(block, distance, which=(0, 1)):
        route = [((i - distance) % replicas, i) for i in range(replicas) if i % 2 in which]
        return lax.ppermute(block, "replica", route)

    inputs = [tokens.at[picks_all[step]].get(mode="promise_in_bounds") for step in range(INNER)]
    inputs_t = [block.T for block in inputs]

    inputs_near = sent(inputs[0], 1)
    moment_near = sent(momentum[0].astype(bf16), 1)
    hidden, slope, *partials = forward(flag, inputs[0], [anchor], only, tensors, emits=False)
    partials = tied(inputs_near, partials)
    error = jnp.concatenate(errors_of(partials, 0))
    error_near = sent(error, 1)
    moment, moment_bf = backward([error], anchor, slope, hidden, inputs_t[0], [momentum[0]], first_update, [f32, bf16])
    moment_far = sent(tied(error_near, moment_bf), 2, (0,))
    hidden, slope = forward(flag, inputs_near, [anchor], only, 0, emits=False)
    moment_near, weights = backward(
        [error_near], anchor, slope, hidden, inputs_near.T, [moment_near, moment, anchor], first_beside, [bf16, bf16]
    )

    inputs_far = sent(tied(error_near, inputs[1]), 2, (1,))
    hidden, slope, *partials = forward(flag, inputs[1], [weights], only, tensors, emits=False)
    error = jnp.concatenate(errors_of(partials, 1))
    error = tied(inputs_far, error)
    error_far = sent(error, 2, (1,))
    moment, weights, known = backward(
        [error], weights, slope, hidden, inputs_t[1], [moment, weights], second_update, [f32, bf16, bf16]
    )
    weights_sent = sent(tied(error_far, weights), 2, (0,))
    moment_two = sent(moment_near, 1, (1,))
    moment_three = sent(moment_far, 1, (1,))
    inputs_far = tied(weights, inputs_far)
    hidden, slope, weights_far = forward(flag, inputs_far, [anchor, moment_two, moment_three], pushed, 0)
    (weights_found,) = backward(
        [error_far], weights_far, slope, hidden, inputs_far.T, [moment_two, weights_far], second_beside, [bf16]
    )

    hidden, slope, *rest = forward(flag, inputs[2], [weights, weights_sent, weights_found], halved, tensors)
    errors = errors_of(rest[:tensors], 2)
    moment, total = backward(
        errors, rest[tensors], slope, hidden, inputs_t[2], [moment, known], third_update, [f32, bf16]
    )
    anchor_new, slow_new = slow_step(flag, total, slow, anchor)
    return (anchor_new, slow_new, moment[None])


def solution(mesh):
    return jax.shard_map(
        body,
        mesh=mesh,
        in_specs=(
            P("replica", None),
            P("replica", None),
            P("replica", None, None),
            P(None, None, "tensor"),
            P("replica", None, None, "tensor"),
            P(None, None, "tensor"),
        ),
        out_specs=(
            P(None, None, "tensor"),
            P(None, None, "tensor"),
            P("replica", None, None, "tensor"),
        ),
        check_vma=False,
    )
```

time: 428 us -> 412 us (0.963)
  other arithmetic: 36.8 us -> 13.8 us
  starting transfers between devices: 99.4 us -> 83.2 us
  Pallas kernels: 95.8 us -> 109 us
  waiting for transfers between devices: 152 us -> 157 us
    ppermute x24 -> x20, waiting for transfers between devices: 23.7 us -> 66.2 us  [moved(): lax.ppermute(part, axis, [(cores * a + c, cores * b + c) for a, b in hops...]
    ppermute x9, waiting for transfers between devices: 80.3 us -> 38.7 us  [sent(): return lax.ppermute(block, 'replica', route)]
    ppermute x24 -> x20, starting transfers between devices: 55.7 us -> 39.3 us  [moved(): lax.ppermute(part, axis, [(cores * a + c, cores * b + c) for a, b in hops...]
    pallas_call x5 -> x13, Pallas kernels: 61.5 us -> 74.5 us  [the longest x5 61.4 us: backward(): pl.pallas_call(functools.partial(backward_kernel, update, len(states), le...]
    sub x1 -> x0, other arithmetic: 8.96 us -> none  [body(): anchor_new = anchor - learn_rate * slow_new]
    unnamed x9 -> x1, other arithmetic: 5.87 us -> 0.01 us
    concatenate x4 -> x2, other arithmetic: 6 us -> 0.14 us  [the longest x1 0.07 us: body(): error = jnp.concatenate(errors_of(partials, 0))]
    unnamed x42 -> x50, local copies, waits for them, and re-layouts: 10.4 us -> 16 us
  transfers between devices with their start and end apart: 67 -> 63, of which waited for: 29 -> 33; matrix products, arithmetic and copies ran while one was open for 9% -> 6% of each run, Pallas kernels for 18% -> 21%
where the time goes in v4:
time: 412 us; the launch traced here: 404 us
  waiting for transfers between devices  157 us (38%)
  Pallas kernels  109 us (26%)
  starting transfers between devices  83.2 us (20%)
  local copies, waits for them, and re-layouts  39.3 us (10%)
  other arithmetic  13.8 us (3%)
    ppermute x20, waiting for transfers between devices, moved(): lax.ppermute(part, axis, [(cores * a + c, cores * b + c) for a, b in hops...  66.2 us
    pallas_call x5, Pallas kernels, backward(): pl.pallas_call(functools.partial(backward_kernel, update, len(states), le...  61.4 us
    ppermute x34, waiting for transfers between devices, swapped(): lax.ppermute(block, axis, [(i, i ^ mask) for i in range(lax.axis_size(axi...  52.2 us
    ppermute x20, starting transfers between devices, moved(): lax.ppermute(part, axis, [(cores * a + c, cores * b + c) for a, b in hops...  39.3 us
    ppermute x9, waiting for transfers between devices, sent(): return lax.ppermute(block, 'replica', route)  38.7 us
    pallas_call x5, Pallas kernels, forward(): pl.pallas_call(functools.partial(forward_kernel, mix, len(sources), sums,...  34.3 us
    ppermute x34, starting transfers between devices, swapped(): lax.ppermute(block, axis, [(i, i ^ mask) for i in range(lax.axis_size(axi...  24.6 us
    ppermute x9, starting transfers between devices, sent(): return lax.ppermute(block, 'replica', route)  19.4 us
  transfers between devices with their start and end apart: 63, of which 33 were waited for; matrix products, arithmetic and copies ran while one was open for 6% of the time, Pallas kernels for 21%

profile of v4, /device:TPU:0, one launch (start us, length us, event | category | flops | bytes accessed | tf_op | source)
XLA Modules:
  0.0 404.0 jit_solution(9456337797020843313)
XLA Ops:
  5.9 6.1 %bitcast_convert_fusion = bf16[2,1024,1024]{2,1,0:T(8,128)(2,1)} fusion(f32[1,2,1024,1024]{3,2,1,0:T(8,128)} %param.10), kind=kLoop, calls=%fused_computation.120 | loop fusion | flops 2097152 | bytes 12582912 | tf_op jit(solution)/shard_map/convert_element_type | solution.py:305
  14.7 6.2 %shard_map.86 = (bf16[512,1024]{1,0:T(8,128)(2,1)S(1)}, bf16[512,1024]{1,0:T(8,128)(2,1)S(1)}, bf16[128,1024]{1,0:T(8,128)(2,1)S(1)}, bf16[128,1024]{1,0:T(8,128...) custom-call(s32[1]{0:T(128)} %bitcast.flag, bf16[512,1024]{1,0:T(8,128)(2,1)S(1)} %gather_fusion.2, ...), custom_call_target="tpu_custom_call" | custom-call | flops 2147483648 | bytes 16777216 | tf_op jit(solution)/shard_map/pallas_call | solution.py:78
  32.1 5.9 %collective-permute-done.3 = bf16[128,1024]{1,0:T(8,128)(2,1)S(1)} collective-permute-done((bf16[128,1024]{1,0:T(8,128)(2,1)S(1)}, bf16[128,1024]{1,0:T(8,128)(2,1)S(1)}, u32[]{:S(2)}, u32[]{:S(2)}) %collective-permute-start.3) | collective-permute-done | bytes 262176 | tf_op jit(solution)/shard_map/ppermute | solution.py:21
  41.7 5.8 %collective-permute-done.5 = bf16[128,1024]{1,0:T(8,128)(2,1)S(1)} collective-permute-done((bf16[128,1024]{1,0:T(8,128)(2,1)S(1)}, bf16[128,1024]{1,0:T(8,128)(2,1)S(1)}, u32[]{:S(2)}, u32[]{:S(2)}) %collective-permute-start.5) | collective-permute-done | bytes 262176 | tf_op jit(solution)/shard_map/ppermute | solution.py:21
  47.5 4.4 %collective-permute-done.6 = bf16[128,1024]{1,0:T(8,128)(2,1)S(1)} collective-permute-done((bf16[128,1024]{1,0:T(8,128)(2,1)S(1)}, bf16[128,1024]{1,0:T(8,128)(2,1)S(1)}, u32[]{:S(2)}, u32[]{:S(2)}) %collective-permute-start.6) | collective-permute-done | bytes 262176 | tf_op jit(solution)/shard_map/ppermute | solution.py:21
  52.9 10.6 %shard_map.87 = (f32[2,1024,1024]{2,1,0:T(8,128)}, bf16[2,1024,1024]{2,1,0:T(8,128)(2,1)}) custom-call(f32[2,1024,1024]{2,1,0:T(8,128)} %anchor.15, bf16[512,1024]{1,0:T(8,128)(2,1)} %copy-done.8, bf16[512,1024]{1,0:T(8,128)(2,1)} %copy-done.7, bf16[1024,512]{1,0:T(8,128)(2,1)} %bitcast.10.inputs_t, f32[2,1024,1024]{2,1,0:T(8,128)} %bitcast.106, ...), custom_call_target="tpu_custom_call" | custom-call | flops 3221225472 | bytes 29360128 | tf_op jit(solution)/shard_map/pallas_call | solution.py:132
  63.5 15.3 %collective-permute-done.8.refs_3_ = bf16[512,1024]{1,0:T(8,128)(2,1)S(1)} collective-permute-done((bf16[512,1024]{1,0:T(8,128)(2,1)S(1)}, bf16[512,1024]{1,0:T(8,128)(2,1)S(1)}, u32[]{:S(2)}, u32[]{:S(2)}) %collective-permute-start.8) | collective-permute-done | bytes 1048608 | tf_op jit(solution)/shard_map/ppermute | solution.py:299
  93.9 13.7 %shard_map.88 = (bf16[2,1024,1024]{2,1,0:T(8,128)(2,1)}, bf16[2,1024,1024]{2,1,0:T(8,128)(2,1)}) custom-call(f32[2,1024,1024]{2,1,0:T(8,128)} %anchor.15, bf16[512,1024]{1,0:T(8,128)(2,1)} %copy-done.10, bf16[512,1024]{1,0:T(8,128)(2,1)} %copy-done.9, bf16[1024,512]{1,0:T(8,128)(2,1)} %bitcast.8.inputs_t, ...), custom_call_target="tpu_custom_call" | custom-call | flops 3221225472 | bytes 29360128 | tf_op jit(solution)/shard_map/pallas_call | solution.py:132
  107.7 5.6 %shard_map.89 = (bf16[512,1024]{1,0:T(8,128)(2,1)S(1)}, bf16[512,1024]{1,0:T(8,128)(2,1)S(1)}, bf16[128,1024]{1,0:T(8,128)(2,1)S(1)}, bf16[128,1024]{1,0:T(8,128...) custom-call(s32[1]{0:T(128)} %bitcast.flag, bf16[512,1024]{1,0:T(8,128)(2,1)S(1)} %gather_fusion.4, ...), custom_call_target="tpu_custom_call" | custom-call | flops 2147483648 | bytes 16777216 | tf_op jit(solution)/shard_map/pallas_call | solution.py:78
  124.5 5.9 %collective-permute-done.11 = bf16[128,1024]{1,0:T(8,128)(2,1)} collective-permute-done((bf16[128,1024]{1,0:T(8,128)(2,1)S(1)}, bf16[128,1024]{1,0:T(8,128)(2,1)}, u32[]{:S(2)}, u32[]{:S(2)}) %collective-permute-start.11) | collective-permute-done | bytes 262176 | tf_op jit(solution)/shard_map/ppermute | solution.py:21
  135.3 5.8 %collective-permute-done.13 = bf16[128,1024]{1,0:T(8,128)(2,1)S(1)} collective-permute-done((bf16[128,1024]{1,0:T(8,128)(2,1)S(1)}, bf16[128,1024]{1,0:T(8,128)(2,1)S(1)}, u32[]{:S(2)}, u32[]{:S(2)}) %collective-permute-start.13) | collective-permute-done | bytes 262176 | tf_op jit(solution)/shard_map/ppermute | solution.py:21
  141.0 4.4 %collective-permute-done.14 = bf16[128,1024]{1,0:T(8,128)(2,1)S(1)} collective-permute-done((bf16[128,1024]{1,0:T(8,128)(2,1)S(1)}, bf16[128,1024]{1,0:T(8,128)(2,1)S(1)}, u32[]{:S(2)}, u32[]{:S(2)}) %collective-permute-start.14) | collective-permute-done | bytes 262176 | tf_op jit(solution)/shard_map/ppermute | solution.py:21
  155.2 14.1 %shard_map.90 = (f32[2,1024,1024]{2,1,0:T(8,128)}, bf16[2,1024,1024]{2,1,0:T(8,128)(2,1)}, bf16[2,1024,1024]{2,1,0:T(8,128)(2,1)}) custom-call(bf16[2,1024,1024]{2,1,0:T(8,128)(2,1)} %get-tuple-element.111.refs_0_.weights.refs_1_, bf16[512,1024]{1,0:T(8,128)(2,1)} %copy-done.4, bf16[512,1024]{1,0:T(8,128)(2,1)} %copy-done.3, bf16[1024,512]{1,0:T(8,128)(2,1)} %bitcast.108, ...), custom_call_target="tpu_custom_call" | custom-call | flops 3221225472 | bytes 29360128 | tf_op jit(solution)/shard_map/pallas_call | solution.py:132
  176.8 9.4 %shard_map.91 = (bf16[512,1024]{1,0:T(8,128)(2,1)S(1)}, bf16[512,1024]{1,0:T(8,128)(2,1)S(1)}, bf16[2,1024,1024]{2,1,0:T(8,128)(2,1)}) custom-call(s32[1]{0:T(128)} %bitcast.flag, bf16[512,1024]{1,0:T(8,128)(2,1)S(1)} %copy.43.inputs, f32[2,1024,1024]{2,1,0:T(8,128)} %anchor.15, bf16[2,1024,1024]{2,1,0:T(8,128)(2,1)} %collective-permute-done.18.refs_1_.refs_0_, ...), custom_call_target="tpu_custom_call" | custom-call | flops 1073741824 | bytes 16777216 | tf_op jit(solution)/shard_map/pallas_call | solution.py:78
  188.2 10.1 %shard_map.92.refs_2_ = bf16[2,1024,1024]{2,1,0:T(8,128)(2,1)} custom-call(bf16[2,1024,1024]{2,1,0:T(8,128)(2,1)} %get-tuple-element.126.weights.refs_1_, bf16[512,1024]{1,0:T(8,128)(2,1)} %copy-done.12, bf16[512,1024]{1,0:T(8,128)(2,1)} %copy-done.11, bf16[1024,512]{1,0:T(8,128)(2,1)} %bitcast.20.inputs_t, ...), custom_call_target="tpu_custom_call" | custom-call | flops 3221225472 | bytes 29360128 | tf_op jit(solution)/shard_map/pallas_call | solution.py:132
  198.3 23.4 %collective-permute-done.17.refs_1_ = bf16[2,1024,1024]{2,1,0:T(8,128)(2,1)} collective-permute-done((bf16[2,1024,1024]{2,1,0:T(8,128)(2,1)}, bf16[2,1024,1024]{2,1,0:T(8,128)(2,1)}, u32[]{:S(2)}, u32[]{:S(2)}) %collective-permute-start.17) | collective-permute-done | bytes 4194336 | tf_op jit(solution)/shard_map/ppermute | solution.py:299
  221.7 8.8 %shard_map.93 = (bf16[512,1024]{1,0:T(8,128)(2,1)S(1)}, bf16[512,1024]{1,0:T(8,128)(2,1)S(1)}, bf16[128,1024]{1,0:T(8,128)(2,1)S(1)}, bf16[128,1024]{1,0:T(8,128...) custom-call(s32[1]{0:T(128)} %bitcast.flag, ...), custom_call_target="tpu_custom_call" | custom-call | flops 2147483648 | bytes 16777216 | tf_op jit(solution)/shard_map/pallas_call | solution.py:78
  255.3 12.8 %shard_map.94 = (f32[2,1024,1024]{2,1,0:T(8,128)}, bf16[2,1024,1024]{2,1,0:T(8,128)(2,1)}) custom-call(bf16[2,1024,1024]{2,1,0:T(8,128)(2,1)} %get-tuple-element.129.weights, bf16[512,1024]{1,0:T(8,128)(2,1)} %copy-done.6, bf16[512,1024]{1,0:T(8,128)(2,1)} %copy-done.5, bf16[1024,512]{1,0:T(8,128)(2,1)} %bitcast.107, ...), custom_call_target="tpu_custom_call" | custom-call | flops 3221225472 | bytes 29360128 | tf_op jit(solution)/shard_map/pallas_call | solution.py:132
  280.7 5.3 %collective-permute-done.28 = bf16[128,1024]{1,0:T(8,128)(2,1)S(1)} collective-permute-done((bf16[128,1024]{1,0:T(8,128)(2,1)S(1)}, bf16[128,1024]{1,0:T(8,128)(2,1)S(1)}, u32[]{:S(2)}, u32[]{:S(2)}) %collective-permute-start.28) | collective-permute-done | bytes 262176 | tf_op jit(solution)/shard_map/ppermute | solution.py:221
  286.1 4.7 %collective-permute-done.30 = bf16[128,1024]{1,0:T(8,128)(2,1)S(1)} collective-permute-done((bf16[128,1024]{1,0:T(8,128)(2,1)S(1)}, bf16[128,1024]{1,0:T(8,128)(2,1)S(1)}, u32[]{:S(2)}, u32[]{:S(2)}) %collective-permute-start.30) | collective-permute-done | bytes 262176 | tf_op jit(solution)/shard_map/ppermute | solution.py:221
  290.9 4.4 %collective-permute-start.33 = (bf16[128,1024]{1,0:T(8,128)(2,1)S(1)}, bf16[128,1024]{1,0:T(8,128)(2,1)S(1)}, u32[]{:S(2)}, u32[]{:S(2)}) collective-permute-start(bf16[128,1024]{1,0:T(8,128)(2,1)S(1)} %get-tuple-element.141), channel_id=1, source_target_pairs={{0,8},{4,12},{24,16},{28,20},{1,9},{5,13},{25,17},{29,21},{2,10},{... | collective-permute-start | bytes 786440 | tf_op jit(solution)/shard_map/ppermute | solution.py:221
  300.5 5.6 %collective-permute-start.35 = (bf16[128,1024]{1,0:T(8,128)(2,1)S(1)}, bf16[128,1024]{1,0:T(8,128)(2,1)S(1)}, u32[]{:S(2)}, u32[]{:S(2)}) collective-permute-start(bf16[128,1024]{1,0:T(8,128)(2,1)S(1)} %get-tuple-element.142), channel_id=1, source_target_pairs={{0,8},{4,12},{24,16},{28,20},{1,9},{5,13},{25,17},{29,21},{2,10},{... | collective-permute-start | bytes 786440 | tf_op jit(solution)/shard_map/ppermute | solution.py:221
  349.7 20.6 %collective-permute-done.52 = bf16[128,1024]{1,0:T(8,128)(2,1)S(1)} collective-permute-done((bf16[128,1024]{1,0:T(8,128)(2,1)S(1)}, bf16[128,1024]{1,0:T(8,128)(2,1)S(1)}, u32[]{:S(2)}, u32[]{:S(2)}) %collective-permute-start.52) | collective-permute-done | bytes 262176 | tf_op jit(solution)/shard_map/ppermute | solution.py:221
  371.6 6.6 %collective-permute-done.50 = bf16[128,1024]{1,0:T(8,128)(2,1)S(1)} collective-permute-done((bf16[128,1024]{1,0:T(8,128)(2,1)S(1)}, bf16[128,1024]{1,0:T(8,128)(2,1)S(1)}, u32[]{:S(2)}, u32[]{:S(2)}) %collective-permute-start.50) | collective-permute-done | bytes 262176 | tf_op jit(solution)/shard_map/ppermute | solution.py:221
  (227 shorter events, 186.8 us)
Async XLA Ops:
  5.5 17.4 %collective-permute-start = (bf16[512,1024]{0,1:T(8,128)(2,1)}, bf16[512,1024]{0,1:T(8,128)(2,1)}, u32[]{:S(2)}, u32[]{:S(2)}) collective-permute-start(bf16[512,1024]{0,1:T(8,128)(2,1)} %copy.38), channel_id=1, source_target_pairs={{28,0},{0,4},{4,8},{8,12},{12,16},{16,20},{20,24},{24,28},{29,1},{... | collective-permute-start | bytes 3145736 | tf_op jit(solution)/shard_map/ppermute | solution.py:299
  12.0 81.9 %collective-permute-start.1 = (bf16[2,1024,1024]{2,1,0:T(8,128)(2,1)}, bf16[2,1024,1024]{2,1,0:T(8,128)(2,1)}, u32[]{:S(2)}, u32[]{:S(2)}) collective-permute-start(bf16[2,1024,1024]{2,1,0:T(8,128)(2,1)} %bitcast_convert_fusion), channel_id=1, source_target_pairs={{28,0},{0,4},{4,8},{8,12},{12,16},{16,20},{20,24},{24,28},{29,1},{... | collective-permute-start | bytes 12582920 | tf_op jit(solution)/shard_map/ppermute | solution.py:299
  24.7 13.2 %collective-permute-start.3 = (bf16[128,1024]{1,0:T(8,128)(2,1)S(1)}, bf16[128,1024]{1,0:T(8,128)(2,1)S(1)}, u32[]{:S(2)}, u32[]{:S(2)}) collective-permute-start(bf16[128,1024]{1,0:T(8,128)(2,1)S(1)} %get-tuple-element.108), channel_id=1, source_target_pairs={{0,2},{1,3},{2,0},{3,1},{4,6},{5,7},{6,4},{7,5},{8,10},{9,11},{10,... | collective-permute-start | bytes 786440 | tf_op jit(solution)/shard_map/ppermute | solution.py:21
  39.5 12.4 %collective-permute-start.6 = (bf16[128,1024]{1,0:T(8,128)(2,1)S(1)}, bf16[128,1024]{1,0:T(8,128)(2,1)S(1)}, u32[]{:S(2)}, u32[]{:S(2)}) collective-permute-start(bf16[128,1024]{1,0:T(8,128)(2,1)S(1)} %multiply_convert_fusion.2), channel_id=1, source_target_pairs={{0,2},{1,3},{2,0},{3,1},{4,6},{5,7},{6,4},{7,5},{8,10},{9,11},{10,... | collective-permute-start | bytes 786440 | tf_op jit(solution)/shard_map/ppermute | solution.py:21
  51.9 26.9 %collective-permute-start.8 = (bf16[512,1024]{1,0:T(8,128)(2,1)S(1)}, bf16[512,1024]{1,0:T(8,128)(2,1)S(1)}, u32[]{:S(2)}, u32[]{:S(2)}) collective-permute-start(bf16[512,1024]{1,0:T(8,128)(2,1)S(1)} %pad_maximum_fusion.refs_1_), channel_id=1, source_target_pairs={{28,0},{0,4},{4,8},{8,12},{12,16},{16,20},{20,24},{24,28},{29,1},{... | collective-permute-start | bytes 3145736 | tf_op jit(solution)/shard_map/ppermute | solution.py:299
  78.8 71.7 %collective-permute-start.19 = (bf16[2,1024,1024]{2,1,0:T(8,128)(2,1)}, bf16[2,1024,1024]{2,1,0:T(8,128)(2,1)}, u32[]{:S(2)}, u32[]{:S(2)}) collective-permute-start(bf16[2,1024,1024]{2,1,0:T(8,128)(2,1)} %get-tuple-element.125), channel_id=1, source_target_pairs={{24,0},{0,8},{8,16},{16,24},{25,1},{1,9},{9,17},{17,25},{26,2},{2,... | collective-permute-start | bytes 12582920 | tf_op jit(solution)/shard_map/ppermute | solution.py:299
  92.1 53.4 %collective-permute-start.9 = (bf16[512,1024]{0,1:T(8,128)(2,1)}, bf16[512,1024]{0,1:T(8,128)(2,1)}, u32[]{:S(2)}, u32[]{:S(2)}) collective-permute-start(bf16[512,1024]{0,1:T(8,128)(2,1)} %copy.42), channel_id=1, source_target_pairs={{28,4},{4,12},{12,20},{20,28},{29,5},{5,13},{13,21},{21,29},{30,6}... | collective-permute-start | bytes 3145736 | tf_op jit(solution)/shard_map/ppermute | solution.py:299
  117.0 13.4 %collective-permute-start.11 = (bf16[128,1024]{1,0:T(8,128)(2,1)S(1)}, bf16[128,1024]{1,0:T(8,128)(2,1)}, u32[]{:S(2)}, u32[]{:S(2)}) collective-permute-start(bf16[128,1024]{1,0:T(8,128)(2,1)S(1)} %get-tuple-element.117), channel_id=1, source_target_pairs={{0,2},{1,3},{2,0},{3,1},{4,6},{5,7},{6,4},{7,5},{8,10},{9,11},{10,... | collective-permute-start | bytes 786440 | tf_op jit(solution)/shard_map/ppermute | solution.py:21
  133.0 12.4 %collective-permute-start.14 = (bf16[128,1024]{1,0:T(8,128)(2,1)S(1)}, bf16[128,1024]{1,0:T(8,128)(2,1)S(1)}, u32[]{:S(2)}, u32[]{:S(2)}) collective-permute-start(bf16[128,1024]{1,0:T(8,128)(2,1)S(1)} %multiply_convert_fusion.1), channel_id=1, source_target_pairs={{0,2},{1,3},{2,0},{3,1},{4,6},{5,7},{6,4},{7,5},{8,10},{9,11},{10,... | collective-permute-start | bytes 786440 | tf_op jit(solution)/shard_map/ppermute | solution.py:21
  145.5 23.7 %collective-permute-start.16 = (bf16[512,1024]{1,0:T(8,128)(2,1)S(1)}, bf16[512,1024]{1,0:T(8,128)(2,1)}, u32[]{:S(2)}, u32[]{:S(2)}) collective-permute-start(bf16[512,1024]{1,0:T(8,128)(2,1)S(1)} %pad_maximum_fusion.1.refs_2_), channel_id=1, source_target_pairs={{28,4},{4,12},{12,20},{20,28},{29,5},{5,13},{13,21},{21,29},{30,6}... | collective-permute-start | bytes 3145736 | tf_op jit(solution)/shard_map/ppermute | solution.py:299
  147.2 29.6 %collective-permute-start.18 = (bf16[2,1024,1024]{2,1,0:T(8,128)(2,1)}, bf16[2,1024,1024]{2,1,0:T(8,128)(2,1)}, u32[]{:S(2)}, u32[]{:S(2)}) collective-permute-start(bf16[2,1024,1024]{2,1,0:T(8,128)(2,1)} %get-tuple-element.123), channel_id=1, source_target_pairs={{0,4},{8,12},{16,20},{24,28},{1,5},{9,13},{17,21},{25,29},{2,6},{1... | collective-permute-start | bytes 12582920 | tf_op jit(solution)/shard_map/ppermute | solution.py:299
  150.5 26.3 %collective-permute-start.20 = (bf16[2,1024,1024]{2,1,0:T(8,128)(2,1)}, bf16[2,1024,1024]{2,1,0:T(8,128)(2,1)}, u32[]{:S(2)}, u32[]{:S(2)}) collective-permute-start(bf16[2,1024,1024]{2,1,0:T(8,128)(2,1)} %collective-permute-done.19), channel_id=1, source_target_pairs={{0,4},{8,12},{16,20},{24,28},{1,5},{9,13},{17,21},{25,29},{2,6},{1... | collective-permute-start | bytes 12582920 | tf_op jit(solution)/shard_map/ppermute | solution.py:299
  169.2 52.5 %collective-permute-start.17 = (bf16[2,1024,1024]{2,1,0:T(8,128)(2,1)}, bf16[2,1024,1024]{2,1,0:T(8,128)(2,1)}, u32[]{:S(2)}, u32[]{:S(2)}) collective-permute-start(bf16[2,1024,1024]{2,1,0:T(8,128)(2,1)} %get-tuple-element.121.refs_0_), channel_id=1, source_target_pairs={{24,0},{0,8},{8,16},{16,24},{25,1},{1,9},{9,17},{17,25},{26,2},{2,... | collective-permute-start | bytes 12582920 | tf_op jit(solution)/shard_map/ppermute | solution.py:299
  346.3 23.9 %collective-permute-start.52 = (bf16[128,1024]{1,0:T(8,128)(2,1)S(1)}, bf16[128,1024]{1,0:T(8,128)(2,1)S(1)}, u32[]{:S(2)}, u32[]{:S(2)}) collective-permute-start(bf16[128,1024]{1,0:T(8,128)(2,1)S(1)} %fusion.26), channel_id=1, source_target_pairs={{8,0},{12,4},{16,24},{20,28},{9,1},{13,5},{17,25},{21,29},{10,2},{... | collective-permute-start | bytes 786440 | tf_op jit(solution)/shard_map/ppermute | solution.py:221
  347.6 35.7 %collective-permute-start.62 = (bf16[128,1024]{1,0:T(8,128)(2,1)S(1)}, bf16[128,1024]{1,0:T(8,128)(2,1)S(1)}, u32[]{:S(2)}, u32[]{:S(2)}) collective-permute-start(bf16[128,1024]{1,0:T(8,128)(2,1)S(1)} %get-tuple-element.209.own), channel_id=1, source_target_pairs={{0,4},{4,0},{8,12},{12,8},{16,20},{20,16},{24,28},{28,24},{1,5},{5... | collective-permute-start | bytes 786440 | tf_op jit(solution)/shard_map/ppermute | solution.py:21
  347.7 36.2 %collective-permute-start.61 = (bf16[128,1024]{1,0:T(8,128)(2,1)S(1)}, bf16[128,1024]{1,0:T(8,128)(2,1)S(1)}, u32[]{:S(2)}, u32[]{:S(2)}) collective-permute-start(bf16[128,1024]{1,0:T(8,128)(2,1)S(1)} %get-tuple-element.211.own), channel_id=1, source_target_pairs={{0,4},{4,0},{8,12},{12,8},{16,20},{20,16},{24,28},{28,24},{1,5},{5... | collective-permute-start | bytes 786440 | tf_op jit(solution)/shard_map/ppermute | solution.py:21
  348.2 38.3 %collective-permute-start.60 = (bf16[128,1024]{1,0:T(8,128)(2,1)S(1)}, bf16[128,1024]{1,0:T(8,128)(2,1)S(1)}, u32[]{:S(2)}, u32[]{:S(2)}) collective-permute-start(bf16[128,1024]{1,0:T(8,128)(2,1)S(1)} %get-tuple-element.213.own), channel_id=1, source_target_pairs={{0,4},{4,0},{8,12},{12,8},{16,20},{20,16},{24,28},{28,24},{1,5},{5... | collective-permute-start | bytes 786440 | tf_op jit(solution)/shard_map/ppermute | solution.py:21
  348.3 29.9 %collective-permute-start.50 = (bf16[128,1024]{1,0:T(8,128)(2,1)S(1)}, bf16[128,1024]{1,0:T(8,128)(2,1)S(1)}, u32[]{:S(2)}, u32[]{:S(2)}) collective-permute-start(bf16[128,1024]{1,0:T(8,128)(2,1)S(1)} %fusion.28), channel_id=1, source_target_pairs={{8,0},{12,4},{16,24},{20,28},{9,1},{13,5},{17,25},{21,29},{10,2},{... | collective-permute-start | bytes 786440 | tf_op jit(solution)/shard_map/ppermute | solution.py:221
  370.3 13.0 %collective-permute-start.55 = (bf16[128,1024]{1,0:T(8,128)(2,1)S(1)}, bf16[128,1024]{1,0:T(8,128)(2,1)S(1)}, u32[]{:S(2)}, u32[]{:S(2)}) collective-permute-start(bf16[128,1024]{1,0:T(8,128)(2,1)S(1)} %fusion.30), channel_id=1, source_target_pairs={{8,0},{12,4},{16,24},{20,28},{9,1},{13,5},{17,25},{21,29},{10,2},{... | collective-permute-start | bytes 786440 | tf_op jit(solution)/shard_map/ppermute | solution.py:221
  383.3 12.1 %collective-permute-start.59 = (bf16[128,1024]{1,0:T(8,128)(2,1)S(1)}, bf16[128,1024]{1,0:T(8,128)(2,1)S(1)}, u32[]{:S(2)}, u32[]{:S(2)}) collective-permute-start(bf16[128,1024]{1,0:T(8,128)(2,1)S(1)} %get-tuple-element.215.own), channel_id=1, source_target_pairs={{0,4},{4,0},{8,12},{12,8},{16,20},{20,16},{24,28},{28,24},{1,5},{5... | collective-permute-start | bytes 786440 | tf_op jit(solution)/shard_map/ppermute | solution.py:21
  383.3 13.7 %collective-permute-start.58 = (bf16[128,1024]{1,0:T(8,128)(2,1)S(1)}, bf16[128,1024]{1,0:T(8,128)(2,1)S(1)}, u32[]{:S(2)}, u32[]{:S(2)}) collective-permute-start(bf16[128,1024]{1,0:T(8,128)(2,1)S(1)} %broadcast_select_fusion.4.own), channel_id=1, source_target_pairs={{0,4},{4,0},{8,12},{12,8},{16,20},{20,16},{24,28},{28,24},{1,5},{5... | collective-permute-start | bytes 786440 | tf_op jit(solution)/shard_map/ppermute | solution.py:21
  383.9 14.8 %collective-permute-start.57 = (bf16[128,1024]{1,0:T(8,128)(2,1)S(1)}, bf16[128,1024]{1,0:T(8,128)(2,1)S(1)}, u32[]{:S(2)}, u32[]{:S(2)}) collective-permute-start(bf16[128,1024]{1,0:T(8,128)(2,1)S(1)} %broadcast_select_fusion.5.own), channel_id=1, source_target_pairs={{0,4},{4,0},{8,12},{12,8},{16,20},{20,16},{24,28},{28,24},{1,5},{5... | collective-permute-start | bytes 786440 | tf_op jit(solution)/shard_map/ppermute | solution.py:21
  386.4 13.9 %collective-permute-start.56 = (bf16[128,1024]{1,0:T(8,128)(2,1)S(1)}, bf16[128,1024]{1,0:T(8,128)(2,1)S(1)}, u32[]{:S(2)}, u32[]{:S(2)}) collective-permute-start(bf16[128,1024]{1,0:T(8,128)(2,1)S(1)} %broadcast_select_fusion.6.own), channel_id=1, source_target_pairs={{0,4},{4,0},{8,12},{12,8},{16,20},{20,16},{24,28},{28,24},{1,5},{5... | collective-permute-start | bytes 786440 | tf_op jit(solution)/shard_map/ppermute | solution.py:21
  386.5 15.5 %collective-permute-start.54 = (bf16[128,1024]{1,0:T(8,128)(2,1)S(1)}, bf16[128,1024]{1,0:T(8,128)(2,1)S(1)}, u32[]{:S(2)}, u32[]{:S(2)}) collective-permute-start(bf16[128,1024]{1,0:T(8,128)(2,1)S(1)} %broadcast_select_fusion.7.own), channel_id=1, source_target_pairs={{0,4},{4,0},{8,12},{12,8},{16,20},{20,16},{24,28},{28,24},{1,5},{5... | collective-permute-start | bytes 786440 | tf_op jit(solution)/shard_map/ppermute | solution.py:21
  (64 other events, 462.5 us)

commit v5 on v4

--- a/solution.py
+++ b/solution.py
@@ -104,7 +104,10 @@
 
 
 def backward_kernel(update, taken, pieces, weights, slope, hidden, inputs_t, *refs):
-    states, refs = refs[:taken], refs[taken:]
+    states, refs = [], list(refs)
+    for split in taken:
+        states.append(tuple(refs[:2]) if split else refs[0])
+        del refs[: 1 + split]
     errors, results, error, error_t = refs[:pieces], refs[pieces:-2], refs[-2], refs[-1]
 
     @pl.when(pl.program_id(0) == 0)
@@ -117,7 +120,7 @@
     back = jnp.dot(error[...], weights[0].astype(bf16), preferred_element_type=f32) * slope[...].astype(f32)
     for k, (left, right) in enumerate(((inputs_t[...], back.astype(bf16)), (error_t[...], hidden[...]))):
         grad = jnp.dot(left, right, preferred_element_type=f32)
-        values = update(grad, *[state[k].astype(f32) for state in states])
+        values = update(grad, *[(state[k] if type(state) is tuple else state.at[k])[...].astype(f32) for state in states])
         for result, value in zip(results, values):
             result[k] = value.astype(result.dtype)
 
@@ -127,13 +130,16 @@
     units = weights.shape[2]
     block = min(units, 512)
     both = pl.BlockSpec((2, width, block), lambda j: (0, 0, j))
+    half = pl.BlockSpec((width, block), lambda j: (0, j))
     out_only = pl.BlockSpec((1, width, block), lambda j: (1, 0, j))
+    split = [type(state) is tuple for state in states]
+    flat = [part for state in states for part in (state if type(state) is tuple else (state,))]
     unit_spec = pl.BlockSpec((rows, block), lambda j: (0, j))
     return pl.pallas_call(
-        functools.partial(backward_kernel, update, len(states), len(errors)),
+        functools.partial(backward_kernel, update, split, len(errors)),
         grid=(units // block,),
         in_specs=[out_only, unit_spec, unit_spec, whole((width, rows))]
-        + [both] * len(states)
+        + [half if part.ndim == 2 else both for part in flat]
         + [whole(piece.shape) for piece in errors],
         out_specs=[both] * len(kinds),
         out_shape=[jax.ShapeDtypeStruct(weights.shape, kind) for kind in kinds],
@@ -142,7 +148,7 @@
         cost_estimate=pl.CostEstimate(
             flops=6 * rows * width * units, bytes_accessed=28 * width * units, transcendentals=0
         ),
-    )(weights, slope, hidden, inputs_t, *states, *errors)
+    )(weights, slope, hidden, inputs_t, *flat, *errors)
 
 
 def first_update(grad, moment):
@@ -181,12 +187,13 @@
 
 
 def finish_kernel(replicas, flag, slow, anchor, own, theirs, *refs):
-    anchor_new, slow_new = refs[-2:]
+    anchor_new, slow_new, token = refs[-3:]
     for k in range(2):
         total = jnp.where(flag[0] == k, own[...].astype(f32), theirs[...].astype(f32))
         value = slow_beta * slow[k] + total / replicas
         slow_new[k] = value
         anchor_new[k] = anchor[k] - learn_rate * value
+    token[...] = jnp.zeros_like(token)
 
 
 def finish(flag, replicas, slow, anchor, own, theirs, position, before):
@@ -198,8 +205,8 @@
         grid=(1,),
         in_specs=[pl.BlockSpec(memory_space=pltpu.SMEM), rows, rows, whole(own.shape), whole(own.shape)]
         + [pl.BlockSpec(memory_space=pl.ANY)] * len(before),
-        out_specs=[rows, rows],
-        out_shape=[shape, shape],
+        out_specs=[rows, rows, whole((8, 128))],
+        out_shape=[shape, shape, jax.ShapeDtypeStruct((8, 128), bf16)],
         input_output_aliases={5 + k: k for k in range(len(before))},
         compiler_params=pltpu.CompilerParams(vmem_limit_bytes=32 << 20),
         cost_estimate=pl.CostEstimate(flops=8 * size * units, bytes_accessed=36 * size * units, transcendentals=0),
@@ -215,63 +222,50 @@
     half = length // 2
     mine = lax.dynamic_index_in_dim(total, core, 0, keepdims=False)
     other = lax.dynamic_index_in_dim(total, 1 - core, 0, keepdims=False)
-    size = mine.shape[0] // chunks
+    rows = mine.shape[0]
+    size = rows // chunks
 
     def moved(part, hops):
         return lax.ppermute(part, axis, [(cores * a + c, cores * b + c) for a, b in hops for c in range(cores)])
 
-    def at(*places):
+    def at(places):
         return functools.reduce(jnp.logical_or, [chip == place for place in places])
 
+    stages = [(True, [(s, s + 1), (length - 1 - s, length - 2 - s)]) for s in range(half - 1)]
+    if half:
+        stages.append((True, [(half - 1, half), (half, half - 1)]))
+    stages += [(False, [(s + 1, s), (length - 2 - s, length - 1 - s)]) for s in reversed(range(half - 1))]
+
+    pair_rows = rows // 2
+    pairs = [swapped(other[p * pair_rows : (p + 1) * pair_rows], axis, 1) for p in range(2)]
     blocks = []
     for c in range(chunks):
-        part = slice(c * size, (c + 1) * size)
-        blocks.append(added(mine[part], swapped(other[part], axis, 1)))
-    lag = 2
-    middle = lag * max(half - 1, 0)
-    last = chunks - 1 + 2 * middle
-    ticks, results = [], []
-    for tick in range(last + 1):
-        live = list(range(max(0, tick - 2 * middle), min(chunks, tick + 1)))
-        if tick >= lag:
-            for c, block in zip(live, tied(ticks[tick - lag], [blocks[c] for c in live])):
-                blocks[c] = block
-        arrivals, steps = [], []
-        for s in range(half):
-            inward = tick - lag * s
-            outward = inward if s == half - 1 else tick - 2 * middle + lag * s
-            inward = inward if 0 <= inward < chunks else None
-            outward = outward if 0 <= outward < chunks else None
-            if inward is None and outward is None:
+        p, start = divmod(c * size, pair_rows)
+        blocks.append(added(mine[c * size : (c + 1) * size], pairs[p][start : start + size]))
+    arrived = {}
+    tokens, results = {}, []
+    for tick in range(chunks + 2 * len(stages) + 1):
+        for s in range(len(stages) + 1):
+            c = tick - 2 * s
+            if not 0 <= c < chunks:
                 continue
-            if s == half - 1:
-                arrived = moved(blocks[inward], [(s, s + 1), (s + 1, s)])
-            else:
-                hops = []
-                if inward is not None:
-                    hops += [(s, s + 1), (length - 1 - s, length - 2 - s)]
-                if outward is not None:
-                    hops += [(s + 1, s), (length - 2 - s, length - 1 - s)]
-                if inward is None or outward is None:
-                    sent = blocks[outward if inward is None else inward]
-                else:
-                    sent = jnp.where(at(s, length - 1 - s), blocks[inward], blocks[outward])
-                arrived = moved(sent, hops)
-            arrivals.append(arrived)
-            steps.append((s, inward, outward))
-        ticks.append(arrivals)
-        for (s, inward, outward), arrived in zip(steps, arrivals):
-            if s == half - 1:
-                blocks[inward] = jnp.where(at(s, s + 1), added(blocks[inward], arrived), blocks[inward])
-                continue
-            if inward is not None:
-                blocks[inward] = jnp.where(at(s + 1, length - 2 - s), added(blocks[inward], arrived), blocks[inward])
-            if outward is not None:
-                blocks[outward] = jnp.where(at(s, length - 1 - s), arrived, blocks[outward])
-        if tick >= 2 * middle:
-            done = tick - 2 * middle
-            theirs = swapped(blocks[done], axis, 1)
-            results = finish(flag, replicas, slow, anchor, blocks[done], theirs, done, results)
+            if s:
+                adds, hops = stages[s - 1]
+                fresh = added(blocks[c], arrived[s - 1, c]) if adds else arrived[s - 1, c]
+                blocks[c] = jnp.where(at([b for _, b in hops]), fresh, blocks[c])
+            if s < len(stages):
+                block = blocks[c]
+                if s:
+                    if (s + 1, c - 4) in arrived:
+                        block = tied(arrived[s + 1, c - 4], block)
+                    if s == len(stages) - 1 and (c - 4) // 2 in tokens:
+                        block = tied(tokens[(c - 4) // 2], block)
+                arrived[s, c] = moved(block, stages[s][1])
+            elif c % 2:
+                own = jnp.concatenate(blocks[c - 1 : c + 1])
+                *results, tokens[c // 2] = finish(
+                    flag, replicas, slow, anchor, own, swapped(own, axis, 1), c // 2, results
+                )
     return results
 
 
@@ -286,55 +280,71 @@
     replicas = lax.axis_size("replica")
     flag = (lax.axis_index("replica") % 2).astype(jnp.int32).reshape(1)
 
-    def errors_of(partials, step):
+    def gathered(own):
+        return [own] + [swapped(own, "tensor", m) for m in range(1, tensors)]
+
+    def error_share(partials, step):
         wanted = targets.at[picks_all[step, :share_rows]].get(mode="promise_in_bounds")
         share = partials[0].astype(f32)
         for m in range(1, tensors):
             share = share + swapped(partials[m], "tensor", m).astype(f32)
-        own = ((share - wanted.astype(f32)) * scale).astype(bf16)
-        return [own] + [swapped(own, "tensor", m) for m in range(1, tensors)]
+        return ((share - wanted.astype(f32)) * scale).astype(bf16)
 
     def sent(block, distance, which=(0, 1)):
         route = [((i - distance) % replicas, i) for i in range(replicas) if i % 2 in which]
         return lax.ppermute(block, "replica", route)
 
-    inputs = [tokens.at[picks_all[step]].get(mode="promise_in_bounds") for step in range(INNER)]
-    inputs_t = [block.T for block in inputs]
-
-    inputs_near = sent(inputs[0], 1)
-    moment_near = sent(momentum[0].astype(bf16), 1)
-    hidden, slope, *partials = forward(flag, inputs[0], [anchor], only, tensors, emits=False)
-    partials = tied(inputs_near, partials)
-    error = jnp.concatenate(errors_of(partials, 0))
-    error_near = sent(error, 1)
-    moment, moment_bf = backward([error], anchor, slope, hidden, inputs_t[0], [momentum[0]], first_update, [f32, bf16])
-    moment_far = sent(tied(error_near, moment_bf), 2, (0,))
-    hidden, slope = forward(flag, inputs_near, [anchor], only, 0, emits=False)
+    def picked(step, count):
+        return tokens.at[picks_all[step, :count]].get(mode="promise_in_bounds")
+
+    near_share = sent(picked(0, share_rows), 1)
+    far_share = sent(picked(1, share_rows), 2, (1,))
+    moment_near_in = sent(tied(near_share, momentum[0, 0]).astype(bf16), 1)
+    inputs_near = jnp.concatenate(gathered(near_share))
+
+    inputs = picked(0, row_count)
+    hidden, slope, *partials = forward(flag, inputs, [anchor], only, tensors, emits=False)
+    own_error = error_share(tied(inputs_near, partials), 0)
+    error_near = sent(own_error, 1)
+    moment_near_out = sent(tied(own_error, momentum[0, 1]).astype(bf16), 1)
+    hidden_near, slope_near = forward(flag, inputs_near, [anchor], only, 0, emits=False)
+    errors = tied(hidden_near, gathered(own_error))
+    moment, moment_bf = backward(errors, anchor, slope, hidden, inputs.T, [momentum[0]], first_update, [f32, bf16])
+    errors_near = gathered(error_near)
+    moment_far = sent(moment_bf, 2, (0,))
     moment_near, weights = backward(
-        [error_near], anchor, slope, hidden, inputs_near.T, [moment_near, moment, anchor], first_beside, [bf16, bf16]
-    )
-
-    inputs_far = sent(tied(error_near, inputs[1]), 2, (1,))
-    hidden, slope, *partials = forward(flag, inputs[1], [weights], only, tensors, emits=False)
-    error = jnp.concatenate(errors_of(partials, 1))
-    error = tied(inputs_far, error)
-    error_far = sent(error, 2, (1,))
+        errors_near,
+        anchor,
+        slope_near,
+        hidden_near,
+        inputs_near.T,
+        [(moment_near_in, moment_near_out), moment, anchor],
+        first_beside,
+        [bf16, bf16],
+    )
+
+    inputs_far = jnp.concatenate(gathered(tied(errors_near, far_share)))
+    inputs = picked(1, row_count)
+    hidden, slope, *partials = forward(flag, inputs, [weights], only, tensors, emits=False)
+    own_error = error_share(tied(inputs_far, partials), 1)
+    error_far = sent(own_error, 2, (1,))
     moment, weights, known = backward(
-        [error], weights, slope, hidden, inputs_t[1], [moment, weights], second_update, [f32, bf16, bf16]
-    )
-    weights_sent = sent(tied(error_far, weights), 2, (0,))
-    moment_two = sent(moment_near, 1, (1,))
-    moment_three = sent(moment_far, 1, (1,))
-    inputs_far = tied(weights, inputs_far)
+        gathered(own_error), weights, slope, hidden, inputs.T, [moment, weights], second_update, [f32, bf16, bf16]
+    )
+    weights_sent = sent(weights, 2, (0,))
+    moment_two, moment_three, error_far = tied(weights, (moment_near, moment_far, error_far))
+    moment_two = sent(moment_two, 1, (1,))
+    moment_three = sent(moment_three, 1, (1,))
     hidden, slope, weights_far = forward(flag, inputs_far, [anchor, moment_two, moment_three], pushed, 0)
     (weights_found,) = backward(
-        [error_far], weights_far, slope, hidden, inputs_far.T, [moment_two, weights_far], second_beside, [bf16]
-    )
-
-    hidden, slope, *rest = forward(flag, inputs[2], [weights, weights_sent, weights_found], halved, tensors)
-    errors = errors_of(rest[:tensors], 2)
+        gathered(error_far), weights_far, slope, hidden, inputs_far.T, [moment_two, weights_far], second_beside, [bf16]
+    )
+
+    inputs = picked(2, row_count)
+    hidden, slope, *rest = forward(flag, inputs, [weights, weights_sent, weights_found], halved, tensors)
+    errors = gathered(error_share(rest[:tensors], 2))
     moment, total = backward(
-        errors, rest[tensors], slope, hidden, inputs_t[2], [moment, known], third_update, [f32, bf16]
+        errors, rest[tensors], slope, hidden, inputs.T, [moment, known], third_update, [f32, bf16]
     )
     anchor_new, slow_new = slow_step(flag, total, slow, anchor)
     return (anchor_new, slow_new, moment[None])

time: 412 us -> 504 us (1.22)
  waiting for transfers between devices: 157 us -> 245 us
  local copies, waits for them, and re-layouts: 39.3 us -> 51.7 us
    ppermute x9 -> x10, waiting for transfers between devices: 38.7 us -> 115 us  [sent(): return lax.ppermute(block, 'replica', route)]
    ppermute x34 -> x36, waiting for transfers between devices: 52.2 us -> 66.1 us  [swapped(): lax.ppermute(block, axis, [(i, i ^ mask) for i in range(lax.axis_size(axi...]
    ppermute x34 -> x36, starting transfers between devices: 24.6 us -> 31.4 us  [swapped(): lax.ppermute(block, axis, [(i, i ^ mask) for i in range(lax.axis_size(axi...]
    squeeze x0 -> x1, local copies, waits for them, and re-layouts: none -> 6.12 us  [body(): moment_near_out = sent(tied(own_error, momentum[0, 1]).astype(bf16), 1)]
    unnamed x50 -> x80, local copies, waits for them, and re-layouts: 16 us -> 21 us
    ppermute x9 -> x10, starting transfers between devices: 19.4 us -> 14.6 us  [sent(): return lax.ppermute(block, 'replica', route)]
    ppermute x20 -> x24, starting transfers between devices: 39.3 us -> 35.6 us  [moved(): lax.ppermute(part, axis, [(cores * a + c, cores * b + c) for a, b in hops...]
    ppermute x20 -> x24, waiting for transfers between devices: 66.2 us -> 63.2 us  [moved(): lax.ppermute(part, axis, [(cores * a + c, cores * b + c) for a, b in hops...]
  transfers between devices with their start and end apart: 63 -> 70, of which waited for: 33 -> 35; matrix products, arithmetic and copies ran while one was open for 6% -> 7% of each run, Pallas kernels for 21% -> 14%
where the time goes in v5:
time: 504 us; the launch traced here: 496 us
  waiting for transfers between devices  245 us (49%)
  Pallas kernels  107 us (21%)
  starting transfers between devices  81.6 us (16%)
  local copies, waits for them, and re-layouts  51.7 us (10%)
  other arithmetic  9.5 us (2%)
    ppermute x10, waiting for transfers between devices, sent(): return lax.ppermute(block, 'replica', route)  115 us
    ppermute x36, waiting for transfers between devices, swapped(): lax.ppermute(block, axis, [(i, i ^ mask) for i in range(lax.axis_size(axi...  66.1 us
    ppermute x24, waiting for transfers between devices, moved(): lax.ppermute(part, axis, [(cores * a + c, cores * b + c) for a, b in hops...  63.2 us
    pallas_call x5, Pallas kernels, backward(): pl.pallas_call(functools.partial(backward_kernel, update, split, len(erro...  61.7 us
    ppermute x24, starting transfers between devices, moved(): lax.ppermute(part, axis, [(cores * a + c, cores * b + c) for a, b in hops...  35.6 us
    pallas_call x5, Pallas kernels, forward(): pl.pallas_call(functools.partial(forward_kernel, mix, len(sources), sums,...  34.3 us
    ppermute x36, starting transfers between devices, swapped(): lax.ppermute(block, axis, [(i, i ^ mask) for i in range(lax.axis_size(axi...  31.4 us
    unnamed x80, local copies, waits for them, and re-layouts  21 us
  transfers between devices with their start and end apart: 70, of which 35 were waited for; matrix products, arithmetic and copies ran while one was open for 7% of the time, Pallas kernels for 14%

profile of v5, /device:TPU:0, one launch (start us, length us, event | category | flops | bytes accessed | tf_op | source)
XLA Modules:
  0.0 496.2 jit_solution(16226901590617619921)
XLA Ops:
  5.7 6.0 %collective-permute-done = bf16[128,1024]{0,1:T(8,128)(2,1)S(1)} collective-permute-done((bf16[128,1024]{0,1:T(8,128)(2,1)S(1)}, bf16[128,1024]{0,1:T(8,128)(2,1)S(1)}, u32[]{:S(2)}, u32[]{:S(2)}) %collective-permute-start) | collective-permute-done | bytes 262176 | tf_op jit(solution)/shard_map/ppermute | solution.py:295
  15.2 6.2 %shard_map.86 = (bf16[512,1024]{1,0:T(8,128)(2,1)S(1)}, bf16[512,1024]{1,0:T(8,128)(2,1)S(1)}, bf16[128,1024]{1,0:T(8,128)(2,1)S(1)}, bf16[128,1024]{1,0:T(8,128...) custom-call(s32[1]{0:T(128)} %bitcast.flag, bf16[512,1024]{1,0:T(8,128)(2,1)S(1)} %gather_fusion.3, ...), custom_call_target="tpu_custom_call" | custom-call | flops 2147483648 | bytes 16777216 | tf_op jit(solution)/shard_map/pallas_call | solution.py:78
  23.6 8.6 %collective-permute-done.3 = bf16[128,1024]{0,1:T(8,128)(2,1)S(1)} collective-permute-done((bf16[128,1024]{0,1:T(8,128)(2,1)S(1)}, bf16[128,1024]{0,1:T(8,128)(2,1)S(1)}, u32[]{:S(2)}, u32[]{:S(2)}) %collective-permute-start.3) | collective-permute-done | bytes 262176 | tf_op jit(solution)/shard_map/ppermute | solution.py:21
  57.3 10.7 %shard_map.87 = (f32[2,1024,1024]{2,1,0:T(8,128)}, bf16[2,1024,1024]{2,1,0:T(8,128)(2,1)}) custom-call(f32[2,1024,1024]{2,1,0:T(8,128)} %anchor.7, bf16[512,1024]{1,0:T(8,128)(2,1)} %copy-done.6, bf16[512,1024]{1,0:T(8,128)(2,1)} %copy-done.5, bf16[1024,512]{1,0:T(8,128)(2,1)} %bitcast.101, f32[2,1024,1024]{2,1,0:T(8,128)} %bitcast.97, ...), custom_call_target="tpu_custom_call" | custom-call | flops 3221225472 | bytes 29360128 | tf_op jit(solution)/shard_map/pallas_call | solution.py:138
  70.0 6.1 %slice_bitcast_fusion = (bf16[1024,1024]{1,0:T(8,128)(2,1)}, bf16[1024,1024]{1,0:T(8,128)(2,1)}) fusion(f32[1,2,1024,1024]{3,2,1,0:T(8,128)} %param.10), kind=kLoop, calls=%fused_computation.9 | loop fusion | bytes 8388608 | tf_op jit(solution)/shard_map/squeeze | solution.py:309
  79.8 88.4 %collective-permute-done.12.refs_4_ = bf16[128,1024]{1,0:T(8,128)(2,1)S(1)} collective-permute-done((bf16[128,1024]{1,0:T(8,128)(2,1)}, bf16[128,1024]{1,0:T(8,128)(2,1)S(1)}, u32[]{:S(2)}, u32[]{:S(2)}) %collective-permute-start.12) | collective-permute-done | bytes 262176 | tf_op jit(solution)/shard_map/ppermute | solution.py:295
  169.6 4.9 collective-permute-done.13.refs_5_
  175.4 8.8 %collective-permute-done.14.refs_6_ = bf16[128,1024]{1,0:T(8,128)(2,1)S(1)} collective-permute-done((bf16[128,1024]{1,0:T(8,128)(2,1)S(1)}, bf16[128,1024]{1,0:T(8,128)(2,1)S(1)}, u32[]{:S(2)}, u32[]{:S(2)}) %collective-permute-start.14) | collective-permute-done | bytes 262176 | tf_op jit(solution)/shard_map/ppermute | solution.py:21
  186.5 6.2 %collective-permute-done.17 = bf16[128,1024]{0,1:T(8,128)(2,1)} collective-permute-done((bf16[128,1024]{0,1:T(8,128)(2,1)S(1)}, bf16[128,1024]{0,1:T(8,128)(2,1)}, u32[]{:S(2)}, u32[]{:S(2)}) %collective-permute-start.17) | collective-permute-done | bytes 262176 | tf_op jit(solution)/shard_map/ppermute | solution.py:21
  201.9 14.0 %shard_map.88 = (bf16[2,1024,1024]{2,1,0:T(8,128)(2,1)}, bf16[2,1024,1024]{2,1,0:T(8,128)(2,1)}) custom-call(f32[2,1024,1024]{2,1,0:T(8,128)} %anchor.7, bf16[512,1024]{1,0:T(8,128)(2,1)} %copy-done.4, bf16[512,1024]{1,0:T(8,128)(2,1)} %copy-done.3, bf16[1024,512]{1,0:T(8,128)(2,1)} %bitcast.98, bf16[1024,1024]{1,0:T(8,128)(2,1)} %collective-permute-done.4.refs_0_, ...), custom_call_target="tpu_custom_call" | custom-call | flops 3221225472 | bytes 29360128 | tf_op jit(solution)/shard_map/pallas_call | solution.py:138
  215.9 5.6 %shard_map.89 = (bf16[512,1024]{1,0:T(8,128)(2,1)S(1)}, bf16[512,1024]{1,0:T(8,128)(2,1)S(1)}, bf16[128,1024]{1,0:T(8,128)(2,1)S(1)}, bf16[128,1024]{1,0:T(8,128...) custom-call(s32[1]{0:T(128)} %bitcast.flag, bf16[512,1024]{1,0:T(8,128)(2,1)S(1)} %gather_fusion.5, ...), custom_call_target="tpu_custom_call" | custom-call | flops 2147483648 | bytes 16777216 | tf_op jit(solution)/shard_map/pallas_call | solution.py:78
  251.6 14.2 %shard_map.90 = (f32[2,1024,1024]{2,1,0:T(8,128)}, bf16[2,1024,1024]{2,1,0:T(8,128)(2,1)}, bf16[2,1024,1024]{2,1,0:T(8,128)(2,1)}) custom-call(bf16[2,1024,1024]{2,1,0:T(8,128)(2,1)} %get-tuple-element.91.refs_0_.weights.refs_1_, bf16[512,1024]{1,0:T(8,128)(2,1)} %copy-done.10, bf16[512,1024]{1,0:T(8,128)(2,1)} %copy-done.9, bf16[1024,512]{1,0:T(8,128)(2,1)} %bitcast.100, ...), custom_call_target="tpu_custom_call" | custom-call | flops 3221225472 | bytes 29360128 | tf_op jit(solution)/shard_map/pallas_call | solution.py:138
  281.8 9.4 %shard_map.91 = (bf16[512,1024]{1,0:T(8,128)(2,1)S(1)}, bf16[512,1024]{1,0:T(8,128)(2,1)S(1)}, bf16[2,1024,1024]{2,1,0:T(8,128)(2,1)}) custom-call(s32[1]{0:T(128)} %bitcast.flag, bf16[512,1024]{1,0:T(8,128)(2,1)S(1)} %copy.35.inputs, f32[2,1024,1024]{2,1,0:T(8,128)} %anchor.7, bf16[2,1024,1024]{2,1,0:T(8,128)(2,1)} %collective-permute-done.29.refs_1_.refs_0_, ...), custom_call_target="tpu_custom_call" | custom-call | flops 1073741824 | bytes 16777216 | tf_op jit(solution)/shard_map/pallas_call | solution.py:78
  294.1 10.1 %shard_map.92.refs_2_ = bf16[2,1024,1024]{2,1,0:T(8,128)(2,1)} custom-call(bf16[2,1024,1024]{2,1,0:T(8,128)(2,1)} %get-tuple-element.108.weights.refs_1_, bf16[512,1024]{1,0:T(8,128)(2,1)} %copy-done.12, bf16[512,1024]{1,0:T(8,128)(2,1)} %copy-done.11, bf16[1024,512]{1,0:T(8,128)(2,1)} %bitcast.22.inputs_t, ...), custom_call_target="tpu_custom_call" | custom-call | flops 3221225472 | bytes 29360128 | tf_op jit(solution)/shard_map/pallas_call | solution.py:138
  304.2 20.9 %collective-permute-done.26.refs_1_ = bf16[2,1024,1024]{2,1,0:T(8,128)(2,1)} collective-permute-done((bf16[2,1024,1024]{2,1,0:T(8,128)(2,1)}, bf16[2,1024,1024]{2,1,0:T(8,128)(2,1)}, u32[]{:S(2)}, u32[]{:S(2)}) %collective-permute-start.26) | collective-permute-done | bytes 4194336 | tf_op jit(solution)/shard_map/ppermute | solution.py:295
  325.0 8.8 %shard_map.93 = (bf16[512,1024]{1,0:T(8,128)(2,1)S(1)}, bf16[512,1024]{1,0:T(8,128)(2,1)S(1)}, bf16[128,1024]{1,0:T(8,128)(2,1)S(1)}, bf16[128,1024]{1,0:T(8,128...) custom-call(s32[1]{0:T(128)} %bitcast.flag, ...), custom_call_target="tpu_custom_call" | custom-call | flops 2147483648 | bytes 16777216 | tf_op jit(solution)/shard_map/pallas_call | solution.py:78
  358.6 12.8 %shard_map.94 = (f32[2,1024,1024]{2,1,0:T(8,128)}, bf16[2,1024,1024]{2,1,0:T(8,128)(2,1)}) custom-call(bf16[2,1024,1024]{2,1,0:T(8,128)(2,1)} %get-tuple-element.112.weights, bf16[512,1024]{1,0:T(8,128)(2,1)} %copy-done.8, bf16[512,1024]{1,0:T(8,128)(2,1)} %copy-done.7, bf16[1024,512]{1,0:T(8,128)(2,1)} %bitcast.99, ...), custom_call_target="tpu_custom_call" | custom-call | flops 3221225472 | bytes 29360128 | tf_op jit(solution)/shard_map/pallas_call | solution.py:138
  411.4 4.9 collective-permute-done.44
  417.0 4.9 collective-permute-done.56
  432.9 5.3 %collective-permute-done.50 = bf16[128,1024]{1,0:T(8,128)(2,1)S(1)} collective-permute-done((bf16[128,1024]{1,0:T(8,128)(2,1)S(1)}, bf16[128,1024]{1,0:T(8,128)(2,1)S(1)}, u32[]{:S(2)}, u32[]{:S(2)}) %collective-permute-start.50) | collective-permute-done | bytes 262176 | tf_op jit(solution)/shard_map/ppermute | solution.py:229
  439.0 4.9 collective-permute-done.53
  474.1 5.6 %collective-permute-done.68 = bf16[128,1024]{1,0:T(8,128)(2,1)S(1)} collective-permute-done((bf16[128,1024]{1,0:T(8,128)(2,1)S(1)}, bf16[128,1024]{1,0:T(8,128)(2,1)S(1)}, u32[]{:S(2)}, u32[]{:S(2)}) %collective-permute-start.68) | collective-permute-done | bytes 262176 | tf_op jit(solution)/shard_map/ppermute | solution.py:229
  479.9 5.5 %collective-permute-done.58 = bf16[128,1024]{1,0:T(8,128)(2,1)S(1)} collective-permute-done((bf16[128,1024]{1,0:T(8,128)(2,1)S(1)}, bf16[128,1024]{1,0:T(8,128)(2,1)S(1)}, u32[]{:S(2)}, u32[]{:S(2)}) %collective-permute-start.58) | collective-permute-done | bytes 262176 | tf_op jit(solution)/shard_map/ppermute | solution.py:229
  485.4 4.9 collective-permute-done.61
  (273 shorter events, 216.6 us)
Async XLA Ops:
  68.0 197.9 %collective-permute-start.27 = (bf16[2,1024,1024]{2,1,0:T(8,128)(2,1)}, bf16[2,1024,1024]{2,1,0:T(8,128)(2,1)}, u32[]{:S(2)}, u32[]{:S(2)}) collective-permute-start(bf16[2,1024,1024]{2,1,0:T(8,128)(2,1)} %get-tuple-element.105), channel_id=1, source_target_pairs={{24,0},{0,8},{8,16},{16,24},{25,1},{1,9},{9,17},{17,25},{26,2},{2,... | collective-permute-start | bytes 12582920 | tf_op jit(solution)/shard_map/ppermute | solution.py:295
  76.1 125.7 %collective-permute-start.4 = (bf16[1024,1024]{1,0:T(8,128)(2,1)}, bf16[1024,1024]{1,0:T(8,128)(2,1)}, u32[]{:S(2)}, u32[]{:S(2)}) collective-permute-start(bf16[1024,1024]{1,0:T(8,128)(2,1)} %get-tuple-element.74), channel_id=1, source_target_pairs={{28,0},{0,4},{4,8},{8,12},{12,16},{16,20},{20,24},{24,28},{29,1},{... | collective-permute-start | bytes 6291464 | tf_op jit(solution)/shard_map/ppermute | solution.py:295
  76.2 125.7 %collective-permute-start.8 = (bf16[1024,1024]{1,0:T(8,128)(2,1)}, bf16[1024,1024]{1,0:T(8,128)(2,1)}, u32[]{:S(2)}, u32[]{:S(2)}) collective-permute-start(bf16[1024,1024]{1,0:T(8,128)(2,1)} %get-tuple-element.83), channel_id=1, source_target_pairs={{28,0},{0,4},{4,8},{8,12},{12,16},{16,20},{20,24},{24,28},{29,1},{... | collective-permute-start | bytes 6291464 | tf_op jit(solution)/shard_map/ppermute | solution.py:295
  77.8 90.3 %collective-permute-start.12 = (bf16[128,1024]{1,0:T(8,128)(2,1)}, bf16[128,1024]{1,0:T(8,128)(2,1)S(1)}, u32[]{:S(2)}, u32[]{:S(2)}) collective-permute-start(bf16[128,1024]{1,0:T(8,128)(2,1)} %multiply_convert_fusion.2.refs_1_), channel_id=1, source_target_pairs={{28,0},{0,4},{4,8},{8,12},{12,16},{16,20},{20,24},{24,28},{29,1},{... | collective-permute-start | bytes 786440 | tf_op jit(solution)/shard_map/ppermute | solution.py:295
  78.9 90.7 %collective-permute-start.16 = (bf16[128,1024]{0,1:T(8,128)(2,1)S(1)}, bf16[128,1024]{0,1:T(8,128)(2,1)S(1)}, u32[]{:S(2)}, u32[]{:S(2)}) collective-permute-start(bf16[128,1024]{0,1:T(8,128)(2,1)S(1)} %copy.34), channel_id=1, source_target_pairs={{28,4},{4,12},{12,20},{20,28},{29,5},{5,13},{13,21},{21,29},{30,6}... | collective-permute-start | bytes 786440 | tf_op jit(solution)/shard_map/ppermute | solution.py:295
  243.2 22.6 %collective-permute-start.28 = (bf16[128,1024]{1,0:T(8,128)(2,1)S(1)}, bf16[128,1024]{1,0:T(8,128)(2,1)S(1)}, u32[]{:S(2)}, u32[]{:S(2)}) collective-permute-start(bf16[128,1024]{1,0:T(8,128)(2,1)S(1)} %multiply_convert_fusion.1.refs_2_), channel_id=1, source_target_pairs={{28,4},{4,12},{12,20},{20,28},{29,5},{5,13},{13,21},{21,29},{30,6}... | collective-permute-start | bytes 786440 | tf_op jit(solution)/shard_map/ppermute | solution.py:295
  272.5 52.5 %collective-permute-start.26 = (bf16[2,1024,1024]{2,1,0:T(8,128)(2,1)}, bf16[2,1024,1024]{2,1,0:T(8,128)(2,1)}, u32[]{:S(2)}, u32[]{:S(2)}) collective-permute-start(bf16[2,1024,1024]{2,1,0:T(8,128)(2,1)} %get-tuple-element.103.refs_0_), channel_id=1, source_target_pairs={{24,0},{0,8},{8,16},{16,24},{25,1},{1,9},{9,17},{17,25},{26,2},{2,... | collective-permute-start | bytes 12582920 | tf_op jit(solution)/shard_map/ppermute | solution.py:295
  274.7 18.5 %collective-permute-start.31 = (bf16[128,1024]{1,0:T(8,128)(2,1)S(1)}, bf16[128,1024]{1,0:T(8,128)(2,1)S(1)}, u32[]{:S(2)}, u32[]{:S(2)}) collective-permute-start(bf16[128,1024]{1,0:T(8,128)(2,1)S(1)} %collective-permute-done.28.refs_2_), channel_id=1, source_target_pairs={{0,1},{1,0},{2,3},{3,2},{4,5},{5,4},{6,7},{7,6},{8,9},{9,8},{10,11... | collective-permute-start | bytes 786440 | tf_op jit(solution)/shard_map/ppermute | solution.py:21
  275.6 17.6 %collective-permute-start.32 = (bf16[128,1024]{1,0:T(8,128)(2,1)S(1)}, bf16[128,1024]{1,0:T(8,128)(2,1)S(1)}, u32[]{:S(2)}, u32[]{:S(2)}) collective-permute-start(bf16[128,1024]{1,0:T(8,128)(2,1)S(1)} %collective-permute-done.28.refs_2_), channel_id=1, source_target_pairs={{0,2},{1,3},{2,0},{3,1},{4,6},{5,7},{6,4},{7,5},{8,10},{9,11},{10,... | collective-permute-start | bytes 786440 | tf_op jit(solution)/shard_map/ppermute | solution.py:21
  276.9 16.4 %collective-permute-start.33 = (bf16[128,1024]{1,0:T(8,128)(2,1)S(1)}, bf16[128,1024]{1,0:T(8,128)(2,1)S(1)}, u32[]{:S(2)}, u32[]{:S(2)}) collective-permute-start(bf16[128,1024]{1,0:T(8,128)(2,1)S(1)} %collective-permute-done.28.refs_2_), channel_id=1, source_target_pairs={{0,3},{1,2},{2,1},{3,0},{4,7},{5,6},{6,5},{7,4},{8,11},{9,10},{10,... | collective-permute-start | bytes 786440 | tf_op jit(solution)/shard_map/ppermute | solution.py:21
  382.9 16.5 %collective-permute-start.51 = (bf16[128,1024]{1,0:T(8,128)(2,1)S(1)}, bf16[128,1024]{1,0:T(8,128)(2,1)S(1)}, u32[]{:S(2)}, u32[]{:S(2)}) collective-permute-start(bf16[128,1024]{1,0:T(8,128)(2,1)S(1)} %get-tuple-element.153), channel_id=1, source_target_pairs={{0,8},{4,12},{24,16},{28,20},{1,9},{5,13},{25,17},{29,21},{2,10},{... | collective-permute-start | bytes 786440 | tf_op jit(solution)/shard_map/ppermute | solution.py:229
  384.2 20.8 %collective-permute-start.66 = (bf16[128,1024]{1,0:T(8,128)(2,1)S(1)}, bf16[128,1024]{1,0:T(8,128)(2,1)S(1)}, u32[]{:S(2)}, u32[]{:S(2)}) collective-permute-start(bf16[128,1024]{1,0:T(8,128)(2,1)S(1)} %get-tuple-element.144), channel_id=1, source_target_pairs={{0,8},{4,12},{24,16},{28,20},{1,9},{5,13},{25,17},{29,21},{2,10},{... | collective-permute-start | bytes 786440 | tf_op jit(solution)/shard_map/ppermute | solution.py:229
  385.5 25.1 %collective-permute-start.41 = (bf16[128,1024]{1,0:T(8,128)(2,1)S(1)}, bf16[128,1024]{1,0:T(8,128)(2,1)S(1)}, u32[]{:S(2)}, u32[]{:S(2)}) collective-permute-start(bf16[128,1024]{1,0:T(8,128)(2,1)S(1)} %get-tuple-element.151), channel_id=1, source_target_pairs={{0,8},{4,12},{24,16},{28,20},{1,9},{5,13},{25,17},{29,21},{2,10},{... | collective-permute-start | bytes 786440 | tf_op jit(solution)/shard_map/ppermute | solution.py:229
  388.1 28.1 %collective-permute-start.44 = (bf16[128,1024]{1,0:T(8,128)(2,1)S(1)}, bf16[128,1024]{1,0:T(8,128)(2,1)S(1)}, u32[]{:S(2)}, u32[]{:S(2)}) collective-permute-start(bf16[128,1024]{1,0:T(8,128)(2,1)S(1)} %get-tuple-element.152), channel_id=1, source_target_pairs={{0,8},{4,12},{24,16},{28,20},{1,9},{5,13},{25,17},{29,21},{2,10},{... | collective-permute-start | bytes 786440 | tf_op jit(solution)/shard_map/ppermute | solution.py:229
  393.7 28.1 %collective-permute-start.56 = (bf16[128,1024]{1,0:T(8,128)(2,1)S(1)}, bf16[128,1024]{1,0:T(8,128)(2,1)S(1)}, u32[]{:S(2)}, u32[]{:S(2)}) collective-permute-start(bf16[128,1024]{1,0:T(8,128)(2,1)S(1)} %get-tuple-element.146), channel_id=1, source_target_pairs={{0,8},{4,12},{24,16},{28,20},{1,9},{5,13},{25,17},{29,21},{2,10},{... | collective-permute-start | bytes 786440 | tf_op jit(solution)/shard_map/ppermute | solution.py:229
  399.4 27.6 %collective-permute-start.59 = (bf16[128,1024]{1,0:T(8,128)(2,1)S(1)}, bf16[128,1024]{1,0:T(8,128)(2,1)S(1)}, u32[]{:S(2)}, u32[]{:S(2)}) collective-permute-start(bf16[128,1024]{1,0:T(8,128)(2,1)S(1)} %get-tuple-element.145), channel_id=1, source_target_pairs={{0,8},{4,12},{24,16},{28,20},{1,9},{5,13},{25,17},{29,21},{2,10},{... | collective-permute-start | bytes 786440 | tf_op jit(solution)/shard_map/ppermute | solution.py:229
  405.0 22.1 %collective-permute-start.49 = (bf16[128,1024]{1,0:T(8,128)(2,1)S(1)}, bf16[128,1024]{1,0:T(8,128)(2,1)S(1)}, u32[]{:S(2)}, u32[]{:S(2)}) collective-permute-start(bf16[128,1024]{1,0:T(8,128)(2,1)S(1)} %fusion.20), channel_id=1, source_target_pairs={{8,16},{12,20},{16,8},{20,12},{9,17},{13,21},{17,9},{21,13},{10,18... | collective-permute-start | bytes 786440 | tf_op jit(solution)/shard_map/ppermute | solution.py:229
  410.6 17.9 %collective-permute-start.52 = (bf16[128,1024]{1,0:T(8,128)(2,1)S(1)}, bf16[128,1024]{1,0:T(8,128)(2,1)S(1)}, u32[]{:S(2)}, u32[]{:S(2)}) collective-permute-start(bf16[128,1024]{1,0:T(8,128)(2,1)S(1)} %fusion.22), channel_id=1, source_target_pairs={{8,16},{12,20},{16,8},{20,12},{9,17},{13,21},{17,9},{21,13},{10,18... | collective-permute-start | bytes 786440 | tf_op jit(solution)/shard_map/ppermute | solution.py:229
  430.2 19.3 %collective-permute-start.43 = (bf16[128,1024]{1,0:T(8,128)(2,1)S(1)}, bf16[128,1024]{1,0:T(8,128)(2,1)S(1)}, u32[]{:S(2)}, u32[]{:S(2)}) collective-permute-start(bf16[128,1024]{1,0:T(8,128)(2,1)S(1)} %fusion.17), channel_id=1, source_target_pairs={{8,0},{12,4},{16,24},{20,28},{9,1},{13,5},{17,25},{21,29},{10,2},{... | collective-permute-start | bytes 786440 | tf_op jit(solution)/shard_map/ppermute | solution.py:229
  431.6 22.2 %collective-permute-start.46 = (bf16[128,1024]{1,0:T(8,128)(2,1)S(1)}, bf16[128,1024]{1,0:T(8,128)(2,1)S(1)}, u32[]{:S(2)}, u32[]{:S(2)}) collective-permute-start(bf16[128,1024]{1,0:T(8,128)(2,1)S(1)} %fusion.19), channel_id=1, source_target_pairs={{8,0},{12,4},{16,24},{20,28},{9,1},{13,5},{17,25},{21,29},{10,2},{... | collective-permute-start | bytes 786440 | tf_op jit(solution)/shard_map/ppermute | solution.py:229
  438.3 16.4 %collective-permute-start.64 = (bf16[128,1024]{1,0:T(8,128)(2,1)S(1)}, bf16[128,1024]{1,0:T(8,128)(2,1)S(1)}, u32[]{:S(2)}, u32[]{:S(2)}) collective-permute-start(bf16[128,1024]{1,0:T(8,128)(2,1)S(1)} %fusion.28), channel_id=1, source_target_pairs={{8,16},{12,20},{16,8},{20,12},{9,17},{13,21},{17,9},{21,13},{10,18... | collective-permute-start | bytes 786440 | tf_op jit(solution)/shard_map/ppermute | solution.py:229
  463.1 16.6 %collective-permute-start.68 = (bf16[128,1024]{1,0:T(8,128)(2,1)S(1)}, bf16[128,1024]{1,0:T(8,128)(2,1)S(1)}, u32[]{:S(2)}, u32[]{:S(2)}) collective-permute-start(bf16[128,1024]{1,0:T(8,128)(2,1)S(1)} %fusion.31), channel_id=1, source_target_pairs={{8,0},{12,4},{16,24},{20,28},{9,1},{13,5},{17,25},{21,29},{10,2},{... | collective-permute-start | bytes 786440 | tf_op jit(solution)/shard_map/ppermute | solution.py:229
  467.2 18.2 %collective-permute-start.58 = (bf16[128,1024]{1,0:T(8,128)(2,1)S(1)}, bf16[128,1024]{1,0:T(8,128)(2,1)S(1)}, u32[]{:S(2)}, u32[]{:S(2)}) collective-permute-start(bf16[128,1024]{1,0:T(8,128)(2,1)S(1)} %fusion.25), channel_id=1, source_target_pairs={{8,0},{12,4},{16,24},{20,28},{9,1},{13,5},{17,25},{21,29},{10,2},{... | collective-permute-start | bytes 786440 | tf_op jit(solution)/shard_map/ppermute | solution.py:229
  468.5 21.8 %collective-permute-start.61 = (bf16[128,1024]{1,0:T(8,128)(2,1)S(1)}, bf16[128,1024]{1,0:T(8,128)(2,1)S(1)}, u32[]{:S(2)}, u32[]{:S(2)}) collective-permute-start(bf16[128,1024]{1,0:T(8,128)(2,1)S(1)} %fusion.27), channel_id=1, source_target_pairs={{8,0},{12,4},{16,24},{20,28},{9,1},{13,5},{17,25},{21,29},{10,2},{... | collective-permute-start | bytes 786440 | tf_op jit(solution)/shard_map/ppermute | solution.py:229
  (83 other events, 697.2 us)

commit v6 on v5

--- a/solution.py
+++ b/solution.py
@@ -34,12 +34,39 @@
     return pl.BlockSpec(shape, lambda j: (0,) * len(shape))
 
 
+def loaded(state, k):
+    if type(state) is not tuple:
+        return state[k].astype(f32)
+    each = len(state) // 2
+    return jnp.concatenate([piece[...].astype(f32) for piece in state[k * each : (k + 1) * each]], axis=0)
+
+
+def regrouped(refs, counts):
+    refs, states = list(refs), []
+    for count in counts:
+        states.append(tuple(refs[:count]) if count > 1 else refs[0])
+        del refs[:count]
+    return states, refs
+
+
+def flattened(states):
+    flat = [state if type(state) is tuple else (state,) for state in states]
+    return [len(state) for state in flat], [part for state in flat for part in state]
+
+
+def block_of(part, block, parts=2):
+    if part.ndim == 2:
+        return pl.BlockSpec((part.shape[0], block), lambda j: (0, j))
+    return pl.BlockSpec((parts, part.shape[1], block), lambda j: (0, 0, j))
+
+
 def forward_kernel(mix, taken, sums, emits, flag, inputs, *refs):
-    sources, refs = refs[:taken], list(refs[taken:])
+    sources, refs = regrouped(refs, taken)
     hidden, slope = refs[:2]
-    block = mix(flag[0], *[source[...].astype(f32) for source in sources]).astype(bf16)
+    block = [mix(flag[0], *[loaded(source, k) for source in sources]).astype(bf16) for k in range(2 if sums or emits else 1)]
     if emits:
-        refs[2 + sums][...] = block
+        for k in range(2):
+            refs[2 + sums][k] = block[k]
     j = pl.program_id(0)
     value, slope_val = gelu_pair(jnp.dot(inputs[...], block[0], preferred_element_type=f32))
     value = value.astype(bf16)
@@ -69,16 +96,17 @@
     units = sources[0].shape[2]
     block = min(units, 512)
     parts = 2 if sums or emits else 1
-    weight_spec = pl.BlockSpec((parts, width, block), lambda j: (0, 0, j))
+    counts, flat = flattened(sources)
     unit_spec = pl.BlockSpec((rows, block), lambda j: (0, j))
     shapes = [((rows, units), unit_spec), ((rows, units), unit_spec)]
     if sums:
         shapes += [((rows // sums, width), whole((rows // sums, width)))] * sums
-    shapes += [(sources[0].shape, weight_spec)] * emits
+    shapes += [(sources[0].shape, block_of(sources[0], block))] * emits
     return pl.pallas_call(
-        functools.partial(forward_kernel, mix, len(sources), sums, emits),
+        functools.partial(forward_kernel, mix, counts, sums, emits),
         grid=(units // block,),
-        in_specs=[pl.BlockSpec(memory_space=pltpu.SMEM), whole((rows, width))] + [weight_spec] * len(sources),
+        in_specs=[pl.BlockSpec(memory_space=pltpu.SMEM), whole((rows, width))]
+        + [block_of(part, block, parts) for part in flat],
         out_specs=[spec for _, spec in shapes],
         out_shape=[jax.ShapeDtypeStruct(shape, bf16) for shape, _ in shapes],
         scratch_shapes=[pltpu.VMEM((rows, width), f32)] * bool(sums),
@@ -88,7 +116,7 @@
             bytes_accessed=16 * width * units,
             transcendentals=rows * units,
         ),
-    )(flag, inputs, *sources)
+    )(flag, inputs, *flat)
 
 
 def only(flag, weights):
@@ -99,16 +127,14 @@
     return weights - 0.5 * learn_rate * (first + second)
 
 
-def halved(flag, weights, sent, found):
+def halved(flag, found, weights, sent):
     return 0.5 * (weights + jnp.where(flag == 0, sent, found))
 
 
-def backward_kernel(update, taken, pieces, weights, slope, hidden, inputs_t, *refs):
-    states, refs = [], list(refs)
-    for split in taken:
-        states.append(tuple(refs[:2]) if split else refs[0])
-        del refs[: 1 + split]
-    errors, results, error, error_t = refs[:pieces], refs[pieces:-2], refs[-2], refs[-1]
+def backward_kernel(update, taken, pieces, given, weights, slope, hidden, inputs_t, *refs):
+    states, refs = regrouped(refs, taken)
+    errors, refs, error, error_t = refs[:pieces], refs[pieces:-2], refs[-2], refs[-1]
+    results, _ = regrouped(refs, given)
 
     @pl.when(pl.program_id(0) == 0)
     def _():
@@ -120,35 +146,47 @@
     back = jnp.dot(error[...], weights[0].astype(bf16), preferred_element_type=f32) * slope[...].astype(f32)
     for k, (left, right) in enumerate(((inputs_t[...], back.astype(bf16)), (error_t[...], hidden[...]))):
         grad = jnp.dot(left, right, preferred_element_type=f32)
-        values = update(grad, *[(state[k] if type(state) is tuple else state.at[k])[...].astype(f32) for state in states])
+        values = update(grad, *[loaded(state, k) for state in states])
         for result, value in zip(results, values):
-            result[k] = value.astype(result.dtype)
+            if type(result) is not tuple:
+                result[k] = value.astype(result.dtype)
+                continue
+            each = len(result) // 2
+            for i, piece in enumerate(result[k * each : (k + 1) * each]):
+                size = piece.shape[0]
+                piece[...] = value[i * size : (i + 1) * size].astype(piece.dtype)
 
 
 def backward(errors, weights, slope, hidden, inputs_t, states, update, kinds):
     width, rows = inputs_t.shape
     units = weights.shape[2]
     block = min(units, 512)
-    both = pl.BlockSpec((2, width, block), lambda j: (0, 0, j))
-    half = pl.BlockSpec((width, block), lambda j: (0, j))
-    out_only = pl.BlockSpec((1, width, block), lambda j: (1, 0, j))
-    split = [type(state) is tuple for state in states]
-    flat = [part for state in states for part in (state if type(state) is tuple else (state,))]
-    unit_spec = pl.BlockSpec((rows, block), lambda j: (0, j))
-    return pl.pallas_call(
-        functools.partial(backward_kernel, update, split, len(errors)),
+    counts, flat = flattened(states)
+    kinds = [kind if type(kind) is tuple else (kind, 1) for kind in kinds]
+    shapes = []
+    for kind, count in kinds:
+        shape = weights.shape if count == 1 else (2 * width // count, units)
+        shapes += [jax.ShapeDtypeStruct(shape, kind)] * count
+    results = pl.pallas_call(
+        functools.partial(backward_kernel, update, counts, len(errors), [count for _, count in kinds]),
         grid=(units // block,),
-        in_specs=[out_only, unit_spec, unit_spec, whole((width, rows))]
-        + [half if part.ndim == 2 else both for part in flat]
+        in_specs=[
+            pl.BlockSpec((1, width, block), lambda j: (1, 0, j)),
+            pl.BlockSpec((rows, block), lambda j: (0, j)),
+            pl.BlockSpec((rows, block), lambda j: (0, j)),
+            whole((width, rows)),
+        ]
+        + [block_of(part, block) for part in flat]
         + [whole(piece.shape) for piece in errors],
-        out_specs=[both] * len(kinds),
-        out_shape=[jax.ShapeDtypeStruct(weights.shape, kind) for kind in kinds],
+        out_specs=[block_of(shape, block) for shape in shapes],
+        out_shape=shapes,
         scratch_shapes=[pltpu.VMEM((rows, width), bf16), pltpu.VMEM((width, rows), bf16)],
         compiler_params=pltpu.CompilerParams(vmem_limit_bytes=56 << 20),
         cost_estimate=pl.CostEstimate(
             flops=6 * rows * width * units, bytes_accessed=28 * width * units, transcendentals=0
         ),
     )(weights, slope, hidden, inputs_t, *flat, *errors)
+    return regrouped(results, [count for _, count in kinds])[0]
 
 
 def first_update(grad, moment):
@@ -244,8 +282,15 @@
         blocks.append(added(mine[c * size : (c + 1) * size], pairs[p][start : start + size]))
     arrived = {}
     tokens, results = {}, []
+    final = len(stages) - 1
+
+    def after(block, *waits):
+        waits = [arrived.get(wait, tokens.get(wait)) for wait in waits]
+        waits = [wait for wait in waits if wait is not None]
+        return tied(waits, block) if waits else block
+
     for tick in range(chunks + 2 * len(stages) + 1):
-        for s in range(len(stages) + 1):
+        for s in reversed(range(len(stages) + 1)):
             c = tick - 2 * s
             if not 0 <= c < chunks:
                 continue
@@ -255,11 +300,12 @@
                 blocks[c] = jnp.where(at([b for _, b in hops]), fresh, blocks[c])
             if s < len(stages):
                 block = blocks[c]
-                if s:
-                    if (s + 1, c - 4) in arrived:
-                        block = tied(arrived[s + 1, c - 4], block)
-                    if s == len(stages) - 1 and (c - 4) // 2 in tokens:
-                        block = tied(tokens[(c - 4) // 2], block)
+                if s == 0:
+                    block = after(block, (0, c - 2), *((t, c - 1 - 2 * t) for t in range(1, len(stages))))
+                elif s < final:
+                    block = after(block, (s + 1, c - 3))
+                else:
+                    block = after(block, (c - 4) // 2)
                 arrived[s, c] = moved(block, stages[s][1])
             elif c % 2:
                 own = jnp.concatenate(blocks[c - 1 : c + 1])
@@ -297,51 +343,60 @@
     def picked(step, count):
         return tokens.at[picks_all[step, :count]].get(mode="promise_in_bounds")
 
-    near_share = sent(picked(0, share_rows), 1)
+    near_rows = picked(0, share_rows)
+    near_share = sent(near_rows, 1)
     far_share = sent(picked(1, share_rows), 2, (1,))
-    moment_near_in = sent(tied(near_share, momentum[0, 0]).astype(bf16), 1)
+    quarter = anchor.shape[1] // 2
+    moment_pieces = [momentum[0, k, i * quarter : (i + 1) * quarter] for k in range(2) for i in range(2)]
+    moment_near = [sent(tied(near_rows, moment_pieces[0]).astype(bf16), 1)]
     inputs_near = jnp.concatenate(gathered(near_share))
 
     inputs = picked(0, row_count)
     hidden, slope, *partials = forward(flag, inputs, [anchor], only, tensors, emits=False)
-    own_error = error_share(tied(inputs_near, partials), 0)
+    moment_near.append(sent(tied(near_share, moment_pieces[1]).astype(bf16), 1))
+    own_error = error_share(tied((inputs_near, moment_near[0]), partials), 0)
     error_near = sent(own_error, 1)
-    moment_near_out = sent(tied(own_error, momentum[0, 1]).astype(bf16), 1)
+    moment_near.append(sent(tied(moment_near[0], moment_pieces[2]).astype(bf16), 1))
     hidden_near, slope_near = forward(flag, inputs_near, [anchor], only, 0, emits=False)
-    errors = tied(hidden_near, gathered(own_error))
-    moment, moment_bf = backward(errors, anchor, slope, hidden, inputs.T, [momentum[0]], first_update, [f32, bf16])
+    errors = tied((hidden_near, moment_near[1]), gathered(tied(moment_near[0], own_error)))
+    moment_near.append(sent(tied(moment_near[1], moment_pieces[3]).astype(bf16), 1))
+    errors = tied(moment_near[2], errors)
+    moment, moment_bf = backward(errors, anchor, slope, hidden, inputs.T, [momentum[0]], first_update, [f32, (bf16, 4)])
     errors_near = gathered(error_near)
-    moment_far = sent(moment_bf, 2, (0,))
+    moment_far = [sent(tied(moment_near[3], piece), 2, (0,)) for piece in moment_bf]
     moment_near, weights = backward(
         errors_near,
         anchor,
         slope_near,
         hidden_near,
         inputs_near.T,
-        [(moment_near_in, moment_near_out), moment, anchor],
+        [tuple(moment_near), moment, anchor],
         first_beside,
         [bf16, bf16],
     )
 
-    inputs_far = jnp.concatenate(gathered(tied(errors_near, far_share)))
+    weights = tied(moment_far[0], weights)
     inputs = picked(1, row_count)
     hidden, slope, *partials = forward(flag, inputs, [weights], only, tensors, emits=False)
+    inputs_far = jnp.concatenate(gathered(tied(errors_near, far_share)))
     own_error = error_share(tied(inputs_far, partials), 1)
+    moment_two = sent(tied(weights, moment_near), 1, (1,))
+    own_error = tied((moment_far[1], moment_two), own_error)
     error_far = sent(own_error, 2, (1,))
+    errors = tied(moment_far[2], gathered(own_error))
     moment, weights, known = backward(
-        gathered(own_error), weights, slope, hidden, inputs.T, [moment, weights], second_update, [f32, bf16, bf16]
+        errors, weights, slope, hidden, inputs.T, [moment, weights], second_update, [f32, (bf16, 2), bf16]
     )
-    weights_sent = sent(weights, 2, (0,))
-    moment_two, moment_three, error_far = tied(weights, (moment_near, moment_far, error_far))
-    moment_two = sent(moment_two, 1, (1,))
-    moment_three = sent(moment_three, 1, (1,))
+    weights_sent = tuple(sent(part, 2, (0,)) for part in weights)
+    errors_far = gathered(tied(weights, error_far))
+    moment_three = tuple(sent(tied(weights, piece), 1, (1,)) for piece in moment_far)
     hidden, slope, weights_far = forward(flag, inputs_far, [anchor, moment_two, moment_three], pushed, 0)
     (weights_found,) = backward(
-        gathered(error_far), weights_far, slope, hidden, inputs_far.T, [moment_two, weights_far], second_beside, [bf16]
+        errors_far, weights_far, slope, hidden, inputs_far.T, [moment_two, weights_far], second_beside, [bf16]
     )
 
     inputs = picked(2, row_count)
-    hidden, slope, *rest = forward(flag, inputs, [weights, weights_sent, weights_found], halved, tensors)
+    hidden, slope, *rest = forward(flag, inputs, [weights_found, weights, weights_sent], halved, tensors)
     errors = gathered(error_share(rest[:tensors], 2))
     moment, total = backward(
         errors, rest[tensors], slope, hidden, inputs.T, [moment, known], third_update, [f32, bf16]

time: 504 us -> 432 us (0.86)
  waiting for transfers between devices: 245 us -> 118 us
  starting transfers between devices: 81.6 us -> 132 us
    ppermute x10 -> x19, waiting for transfers between devices: 115 us -> 31.1 us  [sent(): return lax.ppermute(block, 'replica', route)]
    ppermute x24, waiting for transfers between devices: 63.2 us -> 29.5 us  [moved(): lax.ppermute(part, axis, [(cores * a + c, cores * b + c) for a, b in hops...]
    ppermute x10 -> x19, starting transfers between devices: 14.6 us -> 47.2 us  [sent(): return lax.ppermute(block, 'replica', route)]
    ppermute x24, starting transfers between devices: 35.6 us -> 49.6 us  [moved(): lax.ppermute(part, axis, [(cores * a + c, cores * b + c) for a, b in hops...]
    ppermute x36, waiting for transfers between devices: 66.1 us -> 57.9 us  [swapped(): lax.ppermute(block, axis, [(i, i ^ mask) for i in range(lax.axis_size(axi...]
    unnamed x80 -> x84, local copies, waits for them, and re-layouts: 21 us -> 25.7 us
  transfers between devices with their start and end apart: 70 -> 79, of which waited for: 35 -> 30; matrix products, arithmetic and copies ran while one was open for 7% -> 7% of each run, Pallas kernels for 14% -> 19%
where the time goes in v6:
time: 432 us; the launch traced here: 423 us
  starting transfers between devices  132 us (31%)
  waiting for transfers between devices  118 us (27%)
  Pallas kernels  105 us (24%)
  local copies, waits for them, and re-layouts  56.2 us (13%)
  other arithmetic  8.64 us (2%)
    pallas_call x5, Pallas kernels, backward(): pl.pallas_call(functools.partial(backward_kernel, update, counts, len(err...  61 us
    ppermute x36, waiting for transfers between devices, swapped(): lax.ppermute(block, axis, [(i, i ^ mask) for i in range(lax.axis_size(axi...  57.9 us
    ppermute x24, starting transfers between devices, moved(): lax.ppermute(part, axis, [(cores * a + c, cores * b + c) for a, b in hops...  49.6 us
    ppermute x19, starting transfers between devices, sent(): return lax.ppermute(block, 'replica', route)  47.2 us
    ppermute x36, starting transfers between devices, swapped(): lax.ppermute(block, axis, [(i, i ^ mask) for i in range(lax.axis_size(axi...  35.3 us
    pallas_call x5, Pallas kernels, forward(): pl.pallas_call(functools.partial(forward_kernel, mix, counts, sums, emits...  33.7 us
    ppermute x19, waiting for transfers between devices, sent(): return lax.ppermute(block, 'replica', route)  31.1 us
    ppermute x24, waiting for transfers between devices, moved(): lax.ppermute(part, axis, [(cores * a + c, cores * b + c) for a, b in hops...  29.5 us
  transfers between devices with their start and end apart: 79, of which 30 were waited for; matrix products, arithmetic and copies ran while one was open for 7% of the time, Pallas kernels for 19%

profile of v6, /device:TPU:0, one launch (start us, length us, event | category | flops | bytes accessed | tf_op | source)
XLA Modules:
  0.0 423.3 jit_solution(3277001222827074543)
XLA Ops:
  2.0 5.8 %slice_bitcast_fusion = (bf16[512,1024]{1,0:T(8,128)(2,1)}, bf16[512,1024]{1,0:T(8,128)(2,1)}, bf16[512,1024]{1,0:T(8,128)(2,1)}, bf16[512,1024]{1,0:T(8,128)(2,1)}) fusion(f32[1,2,1024,1024]{3,2,1,0:T(8,128)} %param.10), kind=kLoop, calls=%fused_computation.9 | loop fusion | bytes 8388608 | tf_op jit(solution)/shard_map/squeeze | solution.py:350
  12.1 16.6 %collective-permute-done = bf16[128,1024]{0,1:T(8,128)(2,1)S(1)} collective-permute-done((bf16[128,1024]{0,1:T(8,128)(2,1)S(1)}, bf16[128,1024]{0,1:T(8,128)(2,1)S(1)}, u32[]{:S(2)}, u32[]{:S(2)}) %collective-permute-start) | collective-permute-done | bytes 262176 | tf_op jit(solution)/shard_map/ppermute | solution.py:341
  34.4 6.2 %shard_map.85 = (bf16[512,1024]{1,0:T(8,128)(2,1)S(1)}, bf16[512,1024]{1,0:T(8,128)(2,1)S(1)}, bf16[128,1024]{1,0:T(8,128)(2,1)S(1)}, bf16[128,1024]{1,0:T(8,128...) custom-call(s32[1]{0:T(128)} %bitcast.flag, bf16[512,1024]{1,0:T(8,128)(2,1)S(1)} %gather_fusion.3, ...), custom_call_target="tpu_custom_call" | custom-call | flops 2147483648 | bytes 16777216 | tf_op jit(solution)/shard_map/pallas_call | solution.py:105
  42.9 8.1 %collective-permute-done.3 = bf16[128,1024]{0,1:T(8,128)(2,1)S(1)} collective-permute-done((bf16[128,1024]{0,1:T(8,128)(2,1)S(1)}, bf16[128,1024]{0,1:T(8,128)(2,1)S(1)}, u32[]{:S(2)}, u32[]{:S(2)}) %collective-permute-start.3) | collective-permute-done | bytes 262176 | tf_op jit(solution)/shard_map/ppermute | solution.py:21
  80.9 10.3 %shard_map.87 = (f32[2,1024,1024]{2,1,0:T(8,128)}, bf16[512,1024]{1,0:T(8,128)(2,1)}, bf16[512,1024]{1,0:T(8,128)(2,1)}, bf16[512,1024]{1,0:T(8,128)(2,1)}, bf16[512,1024]{1,0:T(8,128)(2,1)}) custom-call(f32[2,1024,1024]{2,1,0:T(8,128)} %anchor.7, bf16[512,1024]{1,0:T(8,128)(2,1)} %copy-done.5, bf16[512,1024]{1,0:T(8,128)(2,1)} %copy-done.4, ...), custom_call_target="tpu_custom_call" | custom-call | flops 3221225472 | bytes 29360128 | tf_op jit(solution)/shard_map/pallas_call | solution.py:170
  96.1 10.7 %collective-permute-done.8.refs_6_ = bf16[128,1024]{1,0:T(8,128)(2,1)S(1)} collective-permute-done((bf16[128,1024]{1,0:T(8,128)(2,1)}, bf16[128,1024]{1,0:T(8,128)(2,1)S(1)}, u32[]{:S(2)}, u32[]{:S(2)}) %collective-permute-start.8) | collective-permute-done | bytes 262176 | tf_op jit(solution)/shard_map/ppermute | solution.py:341
  119.1 14.0 %shard_map.88 = (bf16[2,1024,1024]{2,1,0:T(8,128)(2,1)}, bf16[2,1024,1024]{2,1,0:T(8,128)(2,1)}) custom-call(f32[2,1024,1024]{2,1,0:T(8,128)} %anchor.7, bf16[512,1024]{1,0:T(8,128)(2,1)} %copy-done.11, bf16[512,1024]{1,0:T(8,128)(2,1)} %copy-done.10, bf16[1024,512]{1,0:T(8,128)(2,1)} %bitcast.100, bf16[512,1024]{1,0:T(8,128)(2,1)} %collective-permute-done.4.refs_0_, ...), custom_call_target="tpu_custom_call" | custom-call | flops 3221225472 | bytes 29360128 | tf_op jit(solution)/shard_map/pallas_call | solution.py:170
  147.2 5.8 %collective-permute-start.25 = (bf16[512,1024]{1,0:T(8,128)(2,1)}, bf16[512,1024]{1,0:T(8,128)(2,1)}, u32[]{:S(2)}, u32[]{:S(2)}) collective-permute-start(bf16[512,1024]{1,0:T(8,128)(2,1)} %get-tuple-element.141), channel_id=1, source_target_pairs={{24,0},{0,8},{8,16},{16,24},{25,1},{1,9},{9,17},{17,25},{26,2},{2,... | collective-permute-start | bytes 3145736 | tf_op jit(solution)/shard_map/ppermute | solution.py:341
  153.8 5.6 %shard_map.89 = (bf16[512,1024]{1,0:T(8,128)(2,1)S(1)}, bf16[512,1024]{1,0:T(8,128)(2,1)S(1)}, bf16[128,1024]{1,0:T(8,128)(2,1)S(1)}, bf16[128,1024]{1,0:T(8,128...) custom-call(s32[1]{0:T(128)} %bitcast.flag, bf16[512,1024]{1,0:T(8,128)(2,1)S(1)} %gather_fusion.6, ...), custom_call_target="tpu_custom_call" | custom-call | flops 2147483648 | bytes 16777216 | tf_op jit(solution)/shard_map/pallas_call | solution.py:105
  171.7 5.2 %collective-permute-done.27 = bf16[128,1024]{1,0:T(8,128)(2,1)S(1)} collective-permute-done((bf16[128,1024]{1,0:T(8,128)(2,1)S(1)}, bf16[128,1024]{1,0:T(8,128)(2,1)S(1)}, u32[]{:S(2)}, u32[]{:S(2)}) %collective-permute-start.27) | collective-permute-done | bytes 262176 | tf_op jit(solution)/shard_map/ppermute | solution.py:21
  188.2 5.9 %collective-permute-done.30.refs_4_ = bf16[128,1024]{1,0:T(8,128)(2,1)S(1)} collective-permute-done((bf16[128,1024]{1,0:T(8,128)(2,1)S(1)}, bf16[128,1024]{1,0:T(8,128)(2,1)S(1)}, u32[]{:S(2)}, u32[]{:S(2)}) %collective-permute-start.30) | collective-permute-done | bytes 262176 | tf_op jit(solution)/shard_map/ppermute | solution.py:21
  194.9 13.8 %shard_map.90 = (f32[2,1024,1024]{2,1,0:T(8,128)}, bf16[1024,1024]{1,0:T(8,128)(2,1)}, bf16[1024,1024]{1,0:T(8,128)(2,1)}, bf16[2,1024,1024]{2,1,0:T(8,128)(2,1)}) custom-call(bf16[2,1024,1024]{2,1,0:T(8,128)(2,1)} %get-tuple-element.133.refs_0_.weights.refs_1_, bf16[512,1024]{1,0:T(8,128)(2,1)} %copy-done.7, bf16[512,1024]{1,0:T(8,128)(2,1)} %copy-done.6, ...), custom_call_target="tpu_custom_call" | custom-call | flops 3221225472 | bytes 29360128 | tf_op jit(solution)/shard_map/pallas_call | solution.py:170
  219.7 9.4 %collective-permute-start.34 = (bf16[512,1024]{1,0:T(8,128)(2,1)}, bf16[512,1024]{1,0:T(8,128)(2,1)}, u32[]{:S(2)}, u32[]{:S(2)}) collective-permute-start(bf16[512,1024]{1,0:T(8,128)(2,1)} %collective-permute-done.24), channel_id=1, source_target_pairs={{0,4},{8,12},{16,20},{24,28},{1,5},{9,13},{17,21},{25,29},{2,6},{1... | collective-permute-start | bytes 3145736 | tf_op jit(solution)/shard_map/ppermute | solution.py:341
  240.9 9.0 %shard_map.91 = (bf16[512,1024]{1,0:T(8,128)(2,1)S(1)}, bf16[512,1024]{1,0:T(8,128)(2,1)S(1)}, bf16[2,1024,1024]{2,1,0:T(8,128)(2,1)}) custom-call(s32[1]{0:T(128)} %bitcast.flag, bf16[512,1024]{1,0:T(8,128)(2,1)S(1)} %copy.35.inputs, f32[2,1024,1024]{2,1,0:T(8,128)} %anchor.7, bf16[2,1024,1024]{2,1,0:T(8,128)(2,1)} %collective-permute-done.23.refs_1_.refs_0_, ...), custom_call_target="tpu_custom_call" | custom-call | flops 1073741824 | bytes 16777216 | tf_op jit(solution)/shard_map/pallas_call | solution.py:105
  251.8 10.2 %shard_map.92.refs_0_ = bf16[2,1024,1024]{2,1,0:T(8,128)(2,1)} custom-call(bf16[2,1024,1024]{2,1,0:T(8,128)(2,1)} %get-tuple-element.163.weights.refs_1_, bf16[512,1024]{1,0:T(8,128)(2,1)} %copy-done.15, bf16[512,1024]{1,0:T(8,128)(2,1)} %copy-done.14, bf16[1024,512]{1,0:T(8,128)(2,1)} %bitcast.24.inputs_t, ...), custom_call_target="tpu_custom_call" | custom-call | flops 3221225472 | bytes 29360128 | tf_op jit(solution)/shard_map/pallas_call | solution.py:170
  265.9 8.8 %shard_map.93 = (bf16[512,1024]{1,0:T(8,128)(2,1)S(1)}, bf16[512,1024]{1,0:T(8,128)(2,1)S(1)}, bf16[128,1024]{1,0:T(8,128)(2,1)S(1)}, bf16[128,1024]{1,0:T(8,128...) custom-call(s32[1]{0:T(128)} %bitcast.flag, ...), custom_call_target="tpu_custom_call" | custom-call | flops 2147483648 | bytes 16777216 | tf_op jit(solution)/shard_map/pallas_call | solution.py:105
  302.0 12.8 %shard_map.94 = (f32[2,1024,1024]{2,1,0:T(8,128)}, bf16[2,1024,1024]{2,1,0:T(8,128)(2,1)}) custom-call(bf16[2,1024,1024]{2,1,0:T(8,128)(2,1)} %get-tuple-element.167.weights, bf16[512,1024]{1,0:T(8,128)(2,1)} %copy-done.9, bf16[512,1024]{1,0:T(8,128)(2,1)} %copy-done.8, bf16[1024,512]{1,0:T(8,128)(2,1)} %bitcast.101, ...), custom_call_target="tpu_custom_call" | custom-call | flops 3221225472 | bytes 29360128 | tf_op jit(solution)/shard_map/pallas_call | solution.py:170
  327.9 5.3 %collective-permute-done.50 = bf16[128,1024]{1,0:T(8,128)(2,1)S(1)} collective-permute-done((bf16[128,1024]{1,0:T(8,128)(2,1)S(1)}, bf16[128,1024]{1,0:T(8,128)(2,1)S(1)}, u32[]{:S(2)}, u32[]{:S(2)}) %collective-permute-start.50) | collective-permute-done | bytes 262176 | tf_op jit(solution)/shard_map/ppermute | solution.py:267
  334.0 5.6 %collective-permute-start.51 = (bf16[128,1024]{1,0:T(8,128)(2,1)S(1)}, bf16[128,1024]{1,0:T(8,128)(2,1)S(1)}, u32[]{:S(2)}, u32[]{:S(2)}) collective-permute-start(bf16[128,1024]{1,0:T(8,128)(2,1)S(1)} %get-tuple-element.177), channel_id=1, source_target_pairs={{0,8},{4,12},{24,16},{28,20},{1,9},{5,13},{25,17},{29,21},{2,10},{... | collective-permute-start | bytes 786440 | tf_op jit(solution)/shard_map/ppermute | solution.py:267
  340.4 5.8 %collective-permute-start.56 = (bf16[128,1024]{1,0:T(8,128)(2,1)S(1)}, bf16[128,1024]{1,0:T(8,128)(2,1)S(1)}, u32[]{:S(2)}, u32[]{:S(2)}) collective-permute-start(bf16[128,1024]{1,0:T(8,128)(2,1)S(1)} %get-tuple-element.178), channel_id=1, source_target_pairs={{0,8},{4,12},{24,16},{28,20},{1,9},{5,13},{25,17},{29,21},{2,10},{... | collective-permute-start | bytes 786440 | tf_op jit(solution)/shard_map/ppermute | solution.py:267
  349.9 6.1 %collective-permute-start.65 = (bf16[128,1024]{1,0:T(8,128)(2,1)S(1)}, bf16[128,1024]{1,0:T(8,128)(2,1)S(1)}, u32[]{:S(2)}, u32[]{:S(2)}) collective-permute-start(bf16[128,1024]{1,0:T(8,128)(2,1)S(1)} %get-tuple-element.183), channel_id=1, source_target_pairs={{0,8},{4,12},{24,16},{28,20},{1,9},{5,13},{25,17},{29,21},{2,10},{... | collective-permute-start | bytes 786440 | tf_op jit(solution)/shard_map/ppermute | solution.py:267
  366.8 6.2 %collective-permute-start.71 = (bf16[128,1024]{1,0:T(8,128)(2,1)S(1)}, bf16[128,1024]{1,0:T(8,128)(2,1)S(1)}, u32[]{:S(2)}, u32[]{:S(2)}) collective-permute-start(bf16[128,1024]{1,0:T(8,128)(2,1)S(1)} %get-tuple-element.189), channel_id=1, source_target_pairs={{0,8},{4,12},{24,16},{28,20},{1,9},{5,13},{25,17},{29,21},{2,10},{... | collective-permute-start | bytes 786440 | tf_op jit(solution)/shard_map/ppermute | solution.py:267
  388.5 7.5 %collective-permute-done.72 = bf16[128,1024]{1,0:T(8,128)(2,1)S(1)} collective-permute-done((bf16[128,1024]{1,0:T(8,128)(2,1)S(1)}, bf16[128,1024]{1,0:T(8,128)(2,1)S(1)}, u32[]{:S(2)}, u32[]{:S(2)}) %collective-permute-start.72) | collective-permute-done | bytes 262176 | tf_op jit(solution)/shard_map/ppermute | solution.py:267
  402.8 11.0 %collective-permute-done.74 = bf16[128,1024]{1,0:T(8,128)(2,1)S(1)} collective-permute-done((bf16[128,1024]{1,0:T(8,128)(2,1)S(1)}, bf16[128,1024]{1,0:T(8,128)(2,1)S(1)}, u32[]{:S(2)}, u32[]{:S(2)}) %collective-permute-start.74) | collective-permute-done | bytes 262176 | tf_op jit(solution)/shard_map/ppermute | solution.py:267
  (294 shorter events, 215.3 us)
Async XLA Ops:
  8.7 34.0 %collective-permute-start.4 = (bf16[512,1024]{1,0:T(8,128)(2,1)}, bf16[512,1024]{1,0:T(8,128)(2,1)}, u32[]{:S(2)}, u32[]{:S(2)}) collective-permute-start(bf16[512,1024]{1,0:T(8,128)(2,1)} %get-tuple-element.103), channel_id=1, source_target_pairs={{28,0},{0,4},{4,8},{8,12},{12,16},{16,20},{20,24},{24,28},{29,1},{... | collective-permute-start | bytes 3145736 | tf_op jit(solution)/shard_map/ppermute | solution.py:341
  9.4 19.4 %collective-permute-start = (bf16[128,1024]{0,1:T(8,128)(2,1)S(1)}, bf16[128,1024]{0,1:T(8,128)(2,1)S(1)}, u32[]{:S(2)}, u32[]{:S(2)}) collective-permute-start(bf16[128,1024]{0,1:T(8,128)(2,1)S(1)} %copy.30), channel_id=1, source_target_pairs={{28,0},{0,4},{4,8},{8,12},{12,16},{16,20},{20,24},{24,28},{29,1},{... | collective-permute-start | bytes 786440 | tf_op jit(solution)/shard_map/ppermute | solution.py:341
  28.7 26.0 %collective-permute-start.16 = (bf16[512,1024]{1,0:T(8,128)(2,1)}, bf16[512,1024]{1,0:T(8,128)(2,1)}, u32[]{:S(2)}, u32[]{:S(2)}) collective-permute-start(bf16[512,1024]{1,0:T(8,128)(2,1)} %get-tuple-element.113), channel_id=1, source_target_pairs={{28,0},{0,4},{4,8},{8,12},{12,16},{16,20},{20,24},{24,28},{29,1},{... | collective-permute-start | bytes 3145736 | tf_op jit(solution)/shard_map/ppermute | solution.py:341
  42.7 37.4 %collective-permute-start.18 = (bf16[512,1024]{1,0:T(8,128)(2,1)}, bf16[512,1024]{1,0:T(8,128)(2,1)}, u32[]{:S(2)}, u32[]{:S(2)}) collective-permute-start(bf16[512,1024]{1,0:T(8,128)(2,1)} %get-tuple-element.117), channel_id=1, source_target_pairs={{28,0},{0,4},{4,8},{8,12},{12,16},{16,20},{20,24},{24,28},{29,1},{... | collective-permute-start | bytes 3145736 | tf_op jit(solution)/shard_map/ppermute | solution.py:341
  54.7 36.4 %collective-permute-start.17 = (bf16[512,1024]{1,0:T(8,128)(2,1)}, bf16[512,1024]{1,0:T(8,128)(2,1)}, u32[]{:S(2)}, u32[]{:S(2)}) collective-permute-start(bf16[512,1024]{1,0:T(8,128)(2,1)} %get-tuple-element.114), channel_id=1, source_target_pairs={{28,0},{0,4},{4,8},{8,12},{12,16},{16,20},{20,24},{24,28},{29,1},{... | collective-permute-start | bytes 3145736 | tf_op jit(solution)/shard_map/ppermute | solution.py:341
  91.1 41.9 %collective-permute-start.22 = (bf16[512,1024]{1,0:T(8,128)(2,1)}, bf16[512,1024]{1,0:T(8,128)(2,1)S(1)}, u32[]{:S(2)}, u32[]{:S(2)}) collective-permute-start(bf16[512,1024]{1,0:T(8,128)(2,1)} %get-tuple-element.129), channel_id=1, source_target_pairs={{24,0},{0,8},{8,16},{16,24},{25,1},{1,9},{9,17},{17,25},{26,2},{2,... | collective-permute-start | bytes 3145736 | tf_op jit(solution)/shard_map/ppermute | solution.py:341
  133.0 46.0 %collective-permute-start.23 = (bf16[2,1024,1024]{2,1,0:T(8,128)(2,1)}, bf16[2,1024,1024]{2,1,0:T(8,128)(2,1)}, u32[]{:S(2)}, u32[]{:S(2)}) collective-permute-start(bf16[2,1024,1024]{2,1,0:T(8,128)(2,1)} %get-tuple-element.135), channel_id=1, source_target_pairs={{0,4},{8,12},{16,20},{24,28},{1,5},{9,13},{17,21},{25,29},{2,6},{1... | collective-permute-start | bytes 12582920 | tf_op jit(solution)/shard_map/ppermute | solution.py:341
  147.2 31.8 %collective-permute-start.25 = (bf16[512,1024]{1,0:T(8,128)(2,1)}, bf16[512,1024]{1,0:T(8,128)(2,1)}, u32[]{:S(2)}, u32[]{:S(2)}) collective-permute-start(bf16[512,1024]{1,0:T(8,128)(2,1)} %get-tuple-element.141), channel_id=1, source_target_pairs={{24,0},{0,8},{8,16},{16,24},{25,1},{1,9},{9,17},{17,25},{26,2},{2,... | collective-permute-start | bytes 3145736 | tf_op jit(solution)/shard_map/ppermute | solution.py:341
  162.6 24.3 %collective-permute-start.24 = (bf16[512,1024]{1,0:T(8,128)(2,1)}, bf16[512,1024]{1,0:T(8,128)(2,1)}, u32[]{:S(2)}, u32[]{:S(2)}) collective-permute-start(bf16[512,1024]{1,0:T(8,128)(2,1)} %get-tuple-element.139), channel_id=1, source_target_pairs={{24,0},{0,8},{8,16},{16,24},{25,1},{1,9},{9,17},{17,25},{26,2},{2,... | collective-permute-start | bytes 3145736 | tf_op jit(solution)/shard_map/ppermute | solution.py:341
  179.5 14.5 %collective-permute-start.30 = (bf16[128,1024]{1,0:T(8,128)(2,1)S(1)}, bf16[128,1024]{1,0:T(8,128)(2,1)S(1)}, u32[]{:S(2)}, u32[]{:S(2)}) collective-permute-start(bf16[128,1024]{1,0:T(8,128)(2,1)S(1)} %multiply_convert_fusion.1.refs_2_), channel_id=1, source_target_pairs={{0,2},{1,3},{2,0},{3,1},{4,6},{5,7},{6,4},{7,5},{8,10},{9,11},{10,... | collective-permute-start | bytes 786440 | tf_op jit(solution)/shard_map/ppermute | solution.py:21
  183.9 33.4 %collective-permute-start.35 = (bf16[512,1024]{1,0:T(8,128)(2,1)}, bf16[512,1024]{1,0:T(8,128)(2,1)S(1)}, u32[]{:S(2)}, u32[]{:S(2)}) collective-permute-start(bf16[512,1024]{1,0:T(8,128)(2,1)} %get-tuple-element.161), channel_id=1, source_target_pairs={{24,0},{0,8},{8,16},{16,24},{25,1},{1,9},{9,17},{17,25},{26,2},{2,... | collective-permute-start | bytes 3145736 | tf_op jit(solution)/shard_map/ppermute | solution.py:341
  208.7 20.4 %collective-permute-start.32 = (bf16[512,1024]{1,0:T(8,128)(2,1)S(1)}, bf16[512,1024]{1,0:T(8,128)(2,1)S(1)}, u32[]{:S(2)}, u32[]{:S(2)}) collective-permute-start(bf16[512,1024]{1,0:T(8,128)(2,1)S(1)} %copy-done.38), channel_id=1, source_target_pairs={{0,4},{8,12},{16,20},{24,28},{1,5},{9,13},{17,21},{25,29},{2,6},{1... | collective-permute-start | bytes 3145736 | tf_op jit(solution)/shard_map/ppermute | solution.py:341
  210.5 51.5 %collective-permute-start.41 = (bf16[1024,1024]{1,0:T(8,128)(2,1)}, bf16[1024,1024]{1,0:T(8,128)(2,1)}, u32[]{:S(2)}, u32[]{:S(2)}) collective-permute-start(bf16[1024,1024]{1,0:T(8,128)(2,1)} %get-tuple-element.155.refs_1_), channel_id=1, source_target_pairs={{24,0},{0,8},{8,16},{16,24},{25,1},{1,9},{9,17},{17,25},{26,2},{2,... | collective-permute-start | bytes 6291464 | tf_op jit(solution)/shard_map/ppermute | solution.py:341
  214.7 51.2 %collective-permute-start.42 = (bf16[1024,1024]{1,0:T(8,128)(2,1)}, bf16[1024,1024]{1,0:T(8,128)(2,1)}, u32[]{:S(2)}, u32[]{:S(2)}) collective-permute-start(bf16[1024,1024]{1,0:T(8,128)(2,1)} %get-tuple-element.156.refs_2_), channel_id=1, source_target_pairs={{24,0},{0,8},{8,16},{16,24},{25,1},{1,9},{9,17},{17,25},{26,2},{2,... | collective-permute-start | bytes 6291464 | tf_op jit(solution)/shard_map/ppermute | solution.py:341
  219.7 14.6 %collective-permute-start.34 = (bf16[512,1024]{1,0:T(8,128)(2,1)}, bf16[512,1024]{1,0:T(8,128)(2,1)}, u32[]{:S(2)}, u32[]{:S(2)}) collective-permute-start(bf16[512,1024]{1,0:T(8,128)(2,1)} %collective-permute-done.24), channel_id=1, source_target_pairs={{0,4},{8,12},{16,20},{24,28},{1,5},{9,13},{17,21},{25,29},{2,6},{1... | collective-permute-start | bytes 3145736 | tf_op jit(solution)/shard_map/ppermute | solution.py:341
  232.6 19.2 %collective-permute-start.38 = (bf16[128,1024]{1,0:T(8,128)(2,1)S(1)}, bf16[128,1024]{1,0:T(8,128)(2,1)}, u32[]{:S(2)}, u32[]{:S(2)}) collective-permute-start(bf16[128,1024]{1,0:T(8,128)(2,1)S(1)} %collective-permute-done.37.refs_2_), channel_id=1, source_target_pairs={{0,1},{1,0},{2,3},{3,2},{4,5},{5,4},{6,7},{7,6},{8,9},{9,8},{10,11... | collective-permute-start | bytes 786440 | tf_op jit(solution)/shard_map/ppermute | solution.py:21
  234.3 17.5 %collective-permute-start.39 = (bf16[128,1024]{1,0:T(8,128)(2,1)S(1)}, bf16[128,1024]{1,0:T(8,128)(2,1)}, u32[]{:S(2)}, u32[]{:S(2)}) collective-permute-start(bf16[128,1024]{1,0:T(8,128)(2,1)S(1)} %collective-permute-done.37.refs_2_), channel_id=1, source_target_pairs={{0,2},{1,3},{2,0},{3,1},{4,6},{5,7},{6,4},{7,5},{8,10},{9,11},{10,... | collective-permute-start | bytes 786440 | tf_op jit(solution)/shard_map/ppermute | solution.py:21
  234.4 17.4 %collective-permute-start.40 = (bf16[128,1024]{1,0:T(8,128)(2,1)S(1)}, bf16[128,1024]{1,0:T(8,128)(2,1)}, u32[]{:S(2)}, u32[]{:S(2)}) collective-permute-start(bf16[128,1024]{1,0:T(8,128)(2,1)S(1)} %collective-permute-done.37.refs_2_), channel_id=1, source_target_pairs={{0,3},{1,2},{2,1},{3,0},{4,7},{5,6},{6,5},{7,4},{8,11},{9,10},{10,... | collective-permute-start | bytes 786440 | tf_op jit(solution)/shard_map/ppermute | solution.py:21
  340.4 15.6 %collective-permute-start.56 = (bf16[128,1024]{1,0:T(8,128)(2,1)S(1)}, bf16[128,1024]{1,0:T(8,128)(2,1)S(1)}, u32[]{:S(2)}, u32[]{:S(2)}) collective-permute-start(bf16[128,1024]{1,0:T(8,128)(2,1)S(1)} %get-tuple-element.178), channel_id=1, source_target_pairs={{0,8},{4,12},{24,16},{28,20},{1,9},{5,13},{25,17},{29,21},{2,10},{... | collective-permute-start | bytes 786440 | tf_op jit(solution)/shard_map/ppermute | solution.py:267
  348.6 14.5 %collective-permute-start.62 = (bf16[128,1024]{1,0:T(8,128)(2,1)S(1)}, bf16[128,1024]{1,0:T(8,128)(2,1)S(1)}, u32[]{:S(2)}, u32[]{:S(2)}) collective-permute-start(bf16[128,1024]{1,0:T(8,128)(2,1)S(1)} %fusion.23), channel_id=1, source_target_pairs={{8,0},{12,4},{16,24},{20,28},{9,1},{13,5},{17,25},{21,29},{10,2},{... | collective-permute-start | bytes 786440 | tf_op jit(solution)/shard_map/ppermute | solution.py:267
  366.8 21.6 %collective-permute-start.71 = (bf16[128,1024]{1,0:T(8,128)(2,1)S(1)}, bf16[128,1024]{1,0:T(8,128)(2,1)S(1)}, u32[]{:S(2)}, u32[]{:S(2)}) collective-permute-start(bf16[128,1024]{1,0:T(8,128)(2,1)S(1)} %get-tuple-element.189), channel_id=1, source_target_pairs={{0,8},{4,12},{24,16},{28,20},{1,9},{5,13},{25,17},{29,21},{2,10},{... | collective-permute-start | bytes 786440 | tf_op jit(solution)/shard_map/ppermute | solution.py:267
  375.4 21.4 %collective-permute-start.60 = (bf16[256,1024]{1,0:T(8,128)(2,1)S(1)}, bf16[256,1024]{1,0:T(8,128)(2,1)S(1)}, u32[]{:S(2)}, u32[]{:S(2)}) collective-permute-start(bf16[256,1024]{1,0:T(8,128)(2,1)S(1)} %pad_maximum_fusion.own), channel_id=1, source_target_pairs={{0,4},{4,0},{8,12},{12,8},{16,20},{20,16},{24,28},{28,24},{1,5},{5... | collective-permute-start | bytes 1572872 | tf_op jit(solution)/shard_map/ppermute | solution.py:21
  401.4 15.9 %collective-permute-start.68 = (bf16[128,1024]{1,0:T(8,128)(2,1)S(1)}, bf16[128,1024]{1,0:T(8,128)(2,1)S(1)}, u32[]{:S(2)}, u32[]{:S(2)}) collective-permute-start(bf16[128,1024]{1,0:T(8,128)(2,1)S(1)} %fusion.25), channel_id=1, source_target_pairs={{8,0},{12,4},{16,24},{20,28},{9,1},{13,5},{17,25},{21,29},{10,2},{... | collective-permute-start | bytes 786440 | tf_op jit(solution)/shard_map/ppermute | solution.py:267
  402.7 14.7 %collective-permute-start.78 = (bf16[256,1024]{1,0:T(8,128)(2,1)S(1)}, bf16[256,1024]{1,0:T(8,128)(2,1)S(1)}, u32[]{:S(2)}, u32[]{:S(2)}) collective-permute-start(bf16[256,1024]{1,0:T(8,128)(2,1)S(1)} %pad_maximum_fusion.3.own), channel_id=1, source_target_pairs={{0,4},{4,0},{8,12},{12,8},{16,20},{20,16},{24,28},{28,24},{1,5},{5... | collective-permute-start | bytes 1572872 | tf_op jit(solution)/shard_map/ppermute | solution.py:21
  (94 other events, 689.1 us)

commit v7 on v6

--- a/solution.py
+++ b/solution.py
@@ -13,7 +13,7 @@
 learn_rate = 0.02
 inner_beta = 0.9
 slow_beta = 0.5
-chunks = 8
+chunks = 4
 bf16, f32 = jnp.bfloat16, jnp.float32
 
 
@@ -131,7 +131,7 @@
     return 0.5 * (weights + jnp.where(flag == 0, sent, found))
 
 
-def backward_kernel(update, taken, pieces, given, weights, slope, hidden, inputs_t, *refs):
+def backward_kernel(update, taken, pieces, given, by_core, flag, weights, slope, hidden, inputs_t, *refs):
     states, refs = regrouped(refs, taken)
     errors, refs, error, error_t = refs[:pieces], refs[pieces:-2], refs[-2], refs[-1]
     results, _ = regrouped(refs, given)
@@ -147,9 +147,17 @@
     for k, (left, right) in enumerate(((inputs_t[...], back.astype(bf16)), (error_t[...], hidden[...]))):
         grad = jnp.dot(left, right, preferred_element_type=f32)
         values = update(grad, *[loaded(state, k) for state in states])
-        for result, value in zip(results, values):
+        for result, apart, value in zip(results, by_core, values):
             if type(result) is not tuple:
                 result[k] = value.astype(result.dtype)
+                continue
+            if apart:
+                for place, piece in enumerate(result):
+
+                    @pl.when((flag[0] == k) == (place == 0))
+                    def _():
+                        piece[...] = value.astype(piece.dtype)
+
                 continue
             each = len(result) // 2
             for i, piece in enumerate(result[k * each : (k + 1) * each]):
@@ -157,20 +165,23 @@
                 piece[...] = value[i * size : (i + 1) * size].astype(piece.dtype)
 
 
-def backward(errors, weights, slope, hidden, inputs_t, states, update, kinds):
+def backward(flag, errors, weights, slope, hidden, inputs_t, states, update, kinds):
     width, rows = inputs_t.shape
     units = weights.shape[2]
     block = min(units, 512)
     counts, flat = flattened(states)
     kinds = [kind if type(kind) is tuple else (kind, 1) for kind in kinds]
+    by_core = [count == "core" for _, count in kinds]
+    kinds = [(kind, 2 if apart else count) for (kind, count), apart in zip(kinds, by_core)]
     shapes = []
     for kind, count in kinds:
         shape = weights.shape if count == 1 else (2 * width // count, units)
         shapes += [jax.ShapeDtypeStruct(shape, kind)] * count
     results = pl.pallas_call(
-        functools.partial(backward_kernel, update, counts, len(errors), [count for _, count in kinds]),
+        functools.partial(backward_kernel, update, counts, len(errors), [count for _, count in kinds], by_core),
         grid=(units // block,),
         in_specs=[
+            pl.BlockSpec(memory_space=pltpu.SMEM),
             pl.BlockSpec((1, width, block), lambda j: (1, 0, j)),
             pl.BlockSpec((rows, block), lambda j: (0, j)),
             pl.BlockSpec((rows, block), lambda j: (0, j)),
@@ -185,7 +196,7 @@
         cost_estimate=pl.CostEstimate(
             flops=6 * rows * width * units, bytes_accessed=28 * width * units, transcendentals=0
         ),
-    )(weights, slope, hidden, inputs_t, *flat, *errors)
+    )(flag, weights, slope, hidden, inputs_t, *flat, *errors)
     return regrouped(results, [count for _, count in kinds])[0]
 
 
@@ -246,20 +257,18 @@
         out_specs=[rows, rows, whole((8, 128))],
         out_shape=[shape, shape, jax.ShapeDtypeStruct((8, 128), bf16)],
         input_output_aliases={5 + k: k for k in range(len(before))},
-        compiler_params=pltpu.CompilerParams(vmem_limit_bytes=32 << 20),
+        compiler_params=pltpu.CompilerParams(vmem_limit_bytes=60 << 20),
         cost_estimate=pl.CostEstimate(flops=8 * size * units, bytes_accessed=36 * size * units, transcendentals=0),
     )(flag, slow, anchor, own, theirs, *before)
 
 
-def slow_step(flag, total, slow, anchor):
+def slow_step(flag, mine, other, slow, anchor):
     axis, cores = "replica", 2
     index = lax.axis_index(axis)
     replicas = lax.axis_size(axis)
-    core, chip = index % cores, index // cores
+    chip = index // cores
     length = replicas // cores
     half = length // 2
-    mine = lax.dynamic_index_in_dim(total, core, 0, keepdims=False)
-    other = lax.dynamic_index_in_dim(total, 1 - core, 0, keepdims=False)
     rows = mine.shape[0]
     size = rows // chunks
 
@@ -300,18 +309,14 @@
                 blocks[c] = jnp.where(at([b for _, b in hops]), fresh, blocks[c])
             if s < len(stages):
                 block = blocks[c]
-                if s == 0:
-                    block = after(block, (0, c - 2), *((t, c - 1 - 2 * t) for t in range(1, len(stages))))
-                elif s < final:
+                if 0 < s < final:
                     block = after(block, (s + 1, c - 3))
-                else:
-                    block = after(block, (c - 4) // 2)
+                elif s:
+                    block = after(block, c - 3)
                 arrived[s, c] = moved(block, stages[s][1])
-            elif c % 2:
-                own = jnp.concatenate(blocks[c - 1 : c + 1])
-                *results, tokens[c // 2] = finish(
-                    flag, replicas, slow, anchor, own, swapped(own, axis, 1), c // 2, results
-                )
+            else:
+                own = blocks[c]
+                *results, tokens[c] = finish(flag, replicas, slow, anchor, own, swapped(own, axis, 1), c, results)
     return results
 
 
@@ -345,63 +350,57 @@
 
     near_rows = picked(0, share_rows)
     near_share = sent(near_rows, 1)
-    far_share = sent(picked(1, share_rows), 2, (1,))
-    quarter = anchor.shape[1] // 2
-    moment_pieces = [momentum[0, k, i * quarter : (i + 1) * quarter] for k in range(2) for i in range(2)]
-    moment_near = [sent(tied(near_rows, moment_pieces[0]).astype(bf16), 1)]
+    moment_near = sent(tied(near_rows, momentum[0]).astype(bf16), 1)
     inputs_near = jnp.concatenate(gathered(near_share))
 
     inputs = picked(0, row_count)
     hidden, slope, *partials = forward(flag, inputs, [anchor], only, tensors, emits=False)
-    moment_near.append(sent(tied(near_share, moment_pieces[1]).astype(bf16), 1))
-    own_error = error_share(tied((inputs_near, moment_near[0]), partials), 0)
-    error_near = sent(own_error, 1)
-    moment_near.append(sent(tied(moment_near[0], moment_pieces[2]).astype(bf16), 1))
+    own_error = error_share(partials, 0)
     hidden_near, slope_near = forward(flag, inputs_near, [anchor], only, 0, emits=False)
-    errors = tied((hidden_near, moment_near[1]), gathered(tied(moment_near[0], own_error)))
-    moment_near.append(sent(tied(moment_near[1], moment_pieces[3]).astype(bf16), 1))
-    errors = tied(moment_near[2], errors)
-    moment, moment_bf = backward(errors, anchor, slope, hidden, inputs.T, [momentum[0]], first_update, [f32, (bf16, 4)])
-    errors_near = gathered(error_near)
-    moment_far = [sent(tied(moment_near[3], piece), 2, (0,)) for piece in moment_bf]
+    error = tied((hidden_near, inputs_near.T), jnp.concatenate(gathered(own_error)))
+    error_near = sent(error, 1)
+    moment, moment_bf = backward(
+        flag, [error], anchor, slope, hidden, inputs.T, [momentum[0]], first_update, [f32, bf16]
+    )
+    moment_far = sent(tied(error_near, moment_bf), 2, (0,))
     moment_near, weights = backward(
-        errors_near,
+        flag,
+        [error_near],
         anchor,
         slope_near,
         hidden_near,
         inputs_near.T,
-        [tuple(moment_near), moment, anchor],
+        [moment_near, moment, anchor],
         first_beside,
         [bf16, bf16],
     )
 
-    weights = tied(moment_far[0], weights)
     inputs = picked(1, row_count)
+    inputs_far = sent(tied(error_near, inputs), 2, (1,))
     hidden, slope, *partials = forward(flag, inputs, [weights], only, tensors, emits=False)
-    inputs_far = jnp.concatenate(gathered(tied(errors_near, far_share)))
-    own_error = error_share(tied(inputs_far, partials), 1)
-    moment_two = sent(tied(weights, moment_near), 1, (1,))
-    own_error = tied((moment_far[1], moment_two), own_error)
-    error_far = sent(own_error, 2, (1,))
-    errors = tied(moment_far[2], gathered(own_error))
+    moment_two = sent(moment_near, 1, (1,))
+    own_error = error_share(partials, 1)
+    own_error = tied(moment_two, own_error)
+    error = tied((inputs_far, inputs.T), jnp.concatenate(gathered(own_error)))
+    error_far = sent(error, 2, (1,))
     moment, weights, known = backward(
-        errors, weights, slope, hidden, inputs.T, [moment, weights], second_update, [f32, (bf16, 2), bf16]
-    )
-    weights_sent = tuple(sent(part, 2, (0,)) for part in weights)
-    errors_far = gathered(tied(weights, error_far))
-    moment_three = tuple(sent(tied(weights, piece), 1, (1,)) for piece in moment_far)
+        flag, [error], weights, slope, hidden, inputs.T, [moment, weights], second_update, [f32, bf16, bf16]
+    )
+    weights_sent = sent(weights, 2, (0,))
+    moment_three = sent(moment_far, 1, (1,))
+    inputs_far = tied(weights, inputs_far)
     hidden, slope, weights_far = forward(flag, inputs_far, [anchor, moment_two, moment_three], pushed, 0)
     (weights_found,) = backward(
-        errors_far, weights_far, slope, hidden, inputs_far.T, [moment_two, weights_far], second_beside, [bf16]
+        flag, [error_far], weights_far, slope, hidden, inputs_far.T, [moment_two, weights_far], second_beside, [bf16]
     )
 
     inputs = picked(2, row_count)
     hidden, slope, *rest = forward(flag, inputs, [weights_found, weights, weights_sent], halved, tensors)
-    errors = gathered(error_share(rest[:tensors], 2))
+    errors = tied(inputs.T, gathered(error_share(rest[:tensors], 2)))
     moment, total = backward(
-        errors, rest[tensors], slope, hidden, inputs.T, [moment, known], third_update, [f32, bf16]
-    )
-    anchor_new, slow_new = slow_step(flag, total, slow, anchor)
+        flag, errors, rest[tensors], slope, hidden, inputs.T, [moment, known], third_update, [f32, (bf16, "core")]
+    )
+    anchor_new, slow_new = slow_step(flag, *total, slow, anchor)
     return (anchor_new, slow_new, moment[None])
 
 

time: 432 us -> 441 us (1.021)
  waiting for transfers between devices: 118 us -> 199 us
  starting transfers between devices: 132 us -> 56.3 us
  local copies, waits for them, and re-layouts: 56.2 us -> 42.3 us
  Pallas kernels: 105 us -> 117 us
  other arithmetic: 8.64 us -> 15.8 us
    ppermute x19 -> x9, waiting for transfers between devices: 31.1 us -> 91.6 us  [sent(): return lax.ppermute(block, 'replica', route)]
    ppermute x24 -> x12, waiting for transfers between devices: 29.5 us -> 71.6 us  [moved(): lax.ppermute(part, axis, [(cores * a + c, cores * b + c) for a, b in hops...]
    ppermute x24 -> x12, starting transfers between devices: 49.6 us -> 13.2 us  [moved(): lax.ppermute(part, axis, [(cores * a + c, cores * b + c) for a, b in hops...]
    ppermute x19 -> x9, starting transfers between devices: 47.2 us -> 17.3 us  [sent(): return lax.ppermute(block, 'replica', route)]
    ppermute x36 -> x27, waiting for transfers between devices: 57.9 us -> 35.7 us  [swapped(): lax.ppermute(block, axis, [(i, i ^ mask) for i in range(lax.axis_size(axi...]
    pallas_call x4, Pallas kernels: 10.7 us -> 20.7 us  [finish(): pl.pallas_call(functools.partial(finish_kernel, replicas), grid=(1,), in_...]
    ppermute x36 -> x27, starting transfers between devices: 35.3 us -> 25.8 us  [swapped(): lax.ppermute(block, axis, [(i, i ^ mask) for i in range(lax.axis_size(axi...]
    unnamed x84 -> x57, local copies, waits for them, and re-layouts: 25.7 us -> 16.5 us
  transfers between devices with their start and end apart: 79 -> 48, of which waited for: 30 -> 21; matrix products, arithmetic and copies ran while one was open for 7% -> 7% of each run, Pallas kernels for 19% -> 18%
where the time goes in v7:
time: 441 us; the launch traced here: 432 us
  waiting for transfers between devices  199 us (45%)
  Pallas kernels  117 us (27%)
  starting transfers between devices  56.3 us (13%)
  local copies, waits for them, and re-layouts  42.3 us (10%)
  other arithmetic  15.8 us (4%)
    ppermute x9, waiting for transfers between devices, sent(): return lax.ppermute(block, 'replica', route)  91.6 us
    ppermute x12, waiting for transfers between devices, moved(): lax.ppermute(part, axis, [(cores * a + c, cores * b + c) for a, b in hops...  71.6 us
    pallas_call x5, Pallas kernels, backward(): pl.pallas_call(functools.partial(backward_kernel, update, counts, len(err...  61.9 us
    ppermute x27, waiting for transfers between devices, swapped(): lax.ppermute(block, axis, [(i, i ^ mask) for i in range(lax.axis_size(axi...  35.7 us
    pallas_call x5, Pallas kernels, forward(): pl.pallas_call(functools.partial(forward_kernel, mix, counts, sums, emits...  34.3 us
    ppermute x27, starting transfers between devices, swapped(): lax.ppermute(block, axis, [(i, i ^ mask) for i in range(lax.axis_size(axi...  25.8 us
    pallas_call x4, Pallas kernels, finish(): pl.pallas_call(functools.partial(finish_kernel, replicas), grid=(1,), in_...  20.7 us
    ppermute x9, starting transfers between devices, sent(): return lax.ppermute(block, 'replica', route)  17.3 us
  transfers between devices with their start and end apart: 48, of which 21 were waited for; matrix products, arithmetic and copies ran while one was open for 7% of the time, Pallas kernels for 18%

profile of v7, /device:TPU:0, one launch (start us, length us, event | category | flops | bytes accessed | tf_op | source)
XLA Modules:
  0.0 431.9 jit_solution(13751636706784390509)
XLA Ops:
  2.9 6.1 %convert_element_type.165 = bf16[2,1024,1024]{2,1,0:T(8,128)(2,1)} convert(f32[2,1024,1024]{2,1,0:T(8,128)} %bitcast.47) | non-fusion elementwise | flops 2097152 | bytes 12582912 | tf_op jit(solution)/shard_map/convert_element_type | solution.py:353
  15.1 6.2 %shard_map.86 = (bf16[512,1024]{1,0:T(8,128)(2,1)S(1)}, bf16[512,1024]{1,0:T(8,128)(2,1)S(1)}, bf16[128,1024]{1,0:T(8,128)(2,1)S(1)}, bf16[128,1024]{1,0:T(8,128...) custom-call(s32[1]{0:T(128)} %bitcast.flag, bf16[512,1024]{1,0:T(8,128)(2,1)S(1)} %gather_fusion.3, ...), custom_call_target="tpu_custom_call" | custom-call | flops 2147483648 | bytes 16777216 | tf_op jit(solution)/shard_map/pallas_call | solution.py:105
  29.1 33.7 %collective-permute-done = bf16[128,1024]{0,1:T(8,128)(2,1)} collective-permute-done((bf16[128,1024]{0,1:T(8,128)(2,1)}, bf16[128,1024]{0,1:T(8,128)(2,1)}, u32[]{:S(2)}, u32[]{:S(2)}) %collective-permute-start) | collective-permute-done | bytes 262176 | tf_op jit(solution)/shard_map/ppermute | solution.py:346
  74.9 8.0 %collective-permute-done.2 = bf16[128,1024]{0,1:T(8,128)(2,1)S(1)} collective-permute-done((bf16[128,1024]{0,1:T(8,128)(2,1)}, bf16[128,1024]{0,1:T(8,128)(2,1)S(1)}, u32[]{:S(2)}, u32[]{:S(2)}) %collective-permute-start.2) | collective-permute-done | bytes 262176 | tf_op jit(solution)/shard_map/ppermute | solution.py:21
  97.4 10.6 %shard_map.87 = (f32[2,1024,1024]{2,1,0:T(8,128)}, bf16[2,1024,1024]{2,1,0:T(8,128)(2,1)}) custom-call(s32[1]{0:T(128)} %bitcast.flag, f32[2,1024,1024]{2,1,0:T(8,128)} %anchor.7, bf16[512,1024]{1,0:T(8,128)(2,1)} %copy-done.3, bf16[512,1024]{1,0:T(8,128)(2,1)} %copy-done.2, bf16[1024,512]{1,0:T(8,128)(2,1)} %bitcast.51, f32[2,1024,1024]{2,1,0:T(8,128)} %bitcast.48, ...), custom_call_target="tpu_custom_call" | custom-call | flops 3221225472 | bytes 29360128 | tf_op jit(solution)/shard_map/pallas_call | solution.py:180
  112.2 13.8 %shard_map.88 = (bf16[2,1024,1024]{2,1,0:T(8,128)(2,1)}, bf16[2,1024,1024]{2,1,0:T(8,128)(2,1)}) custom-call(s32[1]{0:T(128)} %bitcast.flag, f32[2,1024,1024]{2,1,0:T(8,128)} %anchor.7, bf16[512,1024]{1,0:T(8,128)(2,1)} %copy-done.9, bf16[512,1024]{1,0:T(8,128)(2,1)} %copy-done.8, bf16[1024,512]{1,0:T(8,128)(2,1)} %bitcast.9.inputs_t, ...), custom_call_target="tpu_custom_call" | custom-call | flops 3221225472 | bytes 29360128 | tf_op jit(solution)/shard_map/pallas_call | solution.py:180
  133.4 5.6 %shard_map.89 = (bf16[512,1024]{1,0:T(8,128)(2,1)S(1)}, bf16[512,1024]{1,0:T(8,128)(2,1)S(1)}, bf16[128,1024]{1,0:T(8,128)(2,1)S(1)}, bf16[128,1024]{1,0:T(8,128...) custom-call(s32[1]{0:T(128)} %bitcast.flag, bf16[512,1024]{1,0:T(8,128)(2,1)S(1)} %gather_fusion.5, ...), custom_call_target="tpu_custom_call" | custom-call | flops 2147483648 | bytes 16777216 | tf_op jit(solution)/shard_map/pallas_call | solution.py:105
  144.6 5.3 %collective-permute-done.14 = bf16[128,1024]{1,0:T(8,128)(2,1)S(1)} collective-permute-done((bf16[128,1024]{1,0:T(8,128)(2,1)S(1)}, bf16[128,1024]{1,0:T(8,128)(2,1)S(1)}, u32[]{:S(2)}, u32[]{:S(2)}) %collective-permute-start.14) | collective-permute-done | bytes 262176 | tf_op jit(solution)/shard_map/ppermute | solution.py:21
  152.4 7.4 %collective-permute-done.16 = bf16[128,1024]{1,0:T(8,128)(2,1)} collective-permute-done((bf16[128,1024]{1,0:T(8,128)(2,1)S(1)}, bf16[128,1024]{1,0:T(8,128)(2,1)}, u32[]{:S(2)}, u32[]{:S(2)}) %collective-permute-start.16) | collective-permute-done | bytes 262176 | tf_op jit(solution)/shard_map/ppermute | solution.py:21
  166.0 30.1 %collective-permute-done.20 = bf16[2,1024,1024]{2,1,0:T(8,128)(2,1)} collective-permute-done((bf16[2,1024,1024]{2,1,0:T(8,128)(2,1)}, bf16[2,1024,1024]{2,1,0:T(8,128)(2,1)}, u32[]{:S(2)}, u32[]{:S(2)}) %collective-permute-start.20) | collective-permute-done | bytes 4194336 | tf_op jit(solution)/shard_map/ppermute | solution.py:346
  200.5 14.1 %shard_map.90 = (f32[2,1024,1024]{2,1,0:T(8,128)}, bf16[2,1024,1024]{2,1,0:T(8,128)(2,1)}, bf16[2,1024,1024]{2,1,0:T(8,128)(2,1)}) custom-call(s32[1]{0:T(128)} %bitcast.flag, bf16[2,1024,1024]{2,1,0:T(8,128)(2,1)} %get-tuple-element.68.refs_0_.weights.refs_1_, bf16[512,1024]{1,0:T(8,128)(2,1)} %copy-done.5, bf16[512,1024]{1,0:T(8,128)(2,1)} %copy-done.4, ...), custom_call_target="tpu_custom_call" | custom-call | flops 3221225472 | bytes 29360128 | tf_op jit(solution)/shard_map/pallas_call | solution.py:180
  222.0 9.4 %shard_map.91 = (bf16[512,1024]{1,0:T(8,128)(2,1)S(1)}, bf16[512,1024]{1,0:T(8,128)(2,1)S(1)}, bf16[2,1024,1024]{2,1,0:T(8,128)(2,1)}) custom-call(s32[1]{0:T(128)} %bitcast.flag, bf16[512,1024]{1,0:T(8,128)(2,1)S(1)} %copy.35.inputs, f32[2,1024,1024]{2,1,0:T(8,128)} %anchor.7, bf16[2,1024,1024]{2,1,0:T(8,128)(2,1)} %collective-permute-done.13.refs_1_.refs_0_, ...), custom_call_target="tpu_custom_call" | custom-call | flops 1073741824 | bytes 16777216 | tf_op jit(solution)/shard_map/pallas_call | solution.py:105
  233.4 10.0 %shard_map.92.refs_0_ = bf16[2,1024,1024]{2,1,0:T(8,128)(2,1)} custom-call(s32[1]{0:T(128)} %bitcast.flag, bf16[2,1024,1024]{2,1,0:T(8,128)(2,1)} %get-tuple-element.83.weights.refs_1_, bf16[512,1024]{1,0:T(8,128)(2,1)} %copy-done.11, bf16[512,1024]{1,0:T(8,128)(2,1)} %copy-done.10, bf16[1024,512]{1,0:T(8,128)(2,1)} %bitcast.20.inputs_t, ...), custom_call_target="tpu_custom_call" | custom-call | flops 3221225472 | bytes 29360128 | tf_op jit(solution)/shard_map/pallas_call | solution.py:180
  243.5 23.7 %collective-permute-done.23.refs_2_ = bf16[2,1024,1024]{2,1,0:T(8,128)(2,1)} collective-permute-done((bf16[2,1024,1024]{2,1,0:T(8,128)(2,1)}, bf16[2,1024,1024]{2,1,0:T(8,128)(2,1)}, u32[]{:S(2)}, u32[]{:S(2)}) %collective-permute-start.23) | collective-permute-done | bytes 4194336 | tf_op jit(solution)/shard_map/ppermute | solution.py:346
  267.2 8.8 %shard_map.93 = (bf16[512,1024]{1,0:T(8,128)(2,1)S(1)}, bf16[512,1024]{1,0:T(8,128)(2,1)S(1)}, bf16[128,1024]{1,0:T(8,128)(2,1)S(1)}, bf16[128,1024]{1,0:T(8,128...) custom-call(s32[1]{0:T(128)} %bitcast.flag, ...), custom_call_target="tpu_custom_call" | custom-call | flops 2147483648 | bytes 16777216 | tf_op jit(solution)/shard_map/pallas_call | solution.py:105
  300.7 13.3 %shard_map.94 = (f32[2,1024,1024]{2,1,0:T(8,128)}, bf16[1024,1024]{1,0:T(8,128)(2,1)}, bf16[1024,1024]{1,0:T(8,128)(2,1)}) custom-call(s32[1]{0:T(128)} %bitcast.flag, bf16[2,1024,1024]{2,1,0:T(8,128)(2,1)} %get-tuple-element.86.weights, bf16[512,1024]{1,0:T(8,128)(2,1)} %copy-done.7, bf16[512,1024]{1,0:T(8,128)(2,1)} %copy-done.6, ...), custom_call_target="tpu_custom_call" | custom-call | flops 3221225472 | bytes 29360128 | tf_op jit(solution)/shard_map/pallas_call | solution.py:180
  326.5 8.2 %collective-permute-done.33 = bf16[256,1024]{1,0:T(8,128)(2,1)S(1)} collective-permute-done((bf16[256,1024]{1,0:T(8,128)(2,1)S(1)}, bf16[256,1024]{1,0:T(8,128)(2,1)S(1)}, u32[]{:S(2)}, u32[]{:S(2)}) %collective-permute-start.33) | collective-permute-done | bytes 524320 | tf_op jit(solution)/shard_map/ppermute | solution.py:276
  335.6 10.3 %collective-permute-done.43 = bf16[256,1024]{1,0:T(8,128)(2,1)S(1)} collective-permute-done((bf16[256,1024]{1,0:T(8,128)(2,1)S(1)}, bf16[256,1024]{1,0:T(8,128)(2,1)S(1)}, u32[]{:S(2)}, u32[]{:S(2)}) %collective-permute-start.43) | collective-permute-done | bytes 524320 | tf_op jit(solution)/shard_map/ppermute | solution.py:276
  346.8 10.3 %collective-permute-done.39 = bf16[256,1024]{1,0:T(8,128)(2,1)S(1)} collective-permute-done((bf16[256,1024]{1,0:T(8,128)(2,1)S(1)}, bf16[256,1024]{1,0:T(8,128)(2,1)S(1)}, u32[]{:S(2)}, u32[]{:S(2)}) %collective-permute-start.39) | collective-permute-done | bytes 524320 | tf_op jit(solution)/shard_map/ppermute | solution.py:276
  359.6 8.3 %collective-permute-done.31 = bf16[256,1024]{1,0:T(8,128)(2,1)S(1)} collective-permute-done((bf16[256,1024]{1,0:T(8,128)(2,1)S(1)}, bf16[256,1024]{1,0:T(8,128)(2,1)S(1)}, u32[]{:S(2)}, u32[]{:S(2)}) %collective-permute-start.31) | collective-permute-done | bytes 524320 | tf_op jit(solution)/shard_map/ppermute | solution.py:276
  369.6 6.5 %collective-permute-done.35 = bf16[256,1024]{1,0:T(8,128)(2,1)S(1)} collective-permute-done((bf16[256,1024]{1,0:T(8,128)(2,1)S(1)}, bf16[256,1024]{1,0:T(8,128)(2,1)S(1)}, u32[]{:S(2)}, u32[]{:S(2)}) %collective-permute-start.35) | collective-permute-done | bytes 524320 | tf_op jit(solution)/shard_map/ppermute | solution.py:276
  380.0 7.4 %collective-permute-done.45 = bf16[256,1024]{1,0:T(8,128)(2,1)S(1)} collective-permute-done((bf16[256,1024]{1,0:T(8,128)(2,1)S(1)}, bf16[256,1024]{1,0:T(8,128)(2,1)S(1)}, u32[]{:S(2)}, u32[]{:S(2)}) %collective-permute-start.45) | collective-permute-done | bytes 524320 | tf_op jit(solution)/shard_map/ppermute | solution.py:276
  387.5 11.1 %collective-permute-done.41 = bf16[256,1024]{1,0:T(8,128)(2,1)S(1)} collective-permute-done((bf16[256,1024]{1,0:T(8,128)(2,1)S(1)}, bf16[256,1024]{1,0:T(8,128)(2,1)S(1)}, u32[]{:S(2)}, u32[]{:S(2)}) %collective-permute-start.41) | collective-permute-done | bytes 524320 | tf_op jit(solution)/shard_map/ppermute | solution.py:276
  398.7 9.5 %collective-permute-done.37 = bf16[256,1024]{1,0:T(8,128)(2,1)S(1)} collective-permute-done((bf16[256,1024]{1,0:T(8,128)(2,1)S(1)}, bf16[256,1024]{1,0:T(8,128)(2,1)S(1)}, u32[]{:S(2)}, u32[]{:S(2)}) %collective-permute-start.37) | collective-permute-done | bytes 524320 | tf_op jit(solution)/shard_map/ppermute | solution.py:276
  (190 shorter events, 152.3 us)
Async XLA Ops:
  9.0 103.2 %collective-permute-start.4 = (bf16[2,1024,1024]{2,1,0:T(8,128)(2,1)}, bf16[2,1024,1024]{2,1,0:T(8,128)(2,1)}, u32[]{:S(2)}, u32[]{:S(2)}) collective-permute-start(bf16[2,1024,1024]{2,1,0:T(8,128)(2,1)} %convert_element_type.165), channel_id=1, source_target_pairs={{28,0},{0,4},{4,8},{8,12},{12,16},{16,20},{20,24},{24,28},{29,1},{... | collective-permute-start | bytes 12582920 | tf_op jit(solution)/shard_map/ppermute | solution.py:346
  10.3 52.5 %collective-permute-start = (bf16[128,1024]{0,1:T(8,128)(2,1)}, bf16[128,1024]{0,1:T(8,128)(2,1)}, u32[]{:S(2)}, u32[]{:S(2)}) collective-permute-start(bf16[128,1024]{0,1:T(8,128)(2,1)} %copy.30), channel_id=1, source_target_pairs={{28,0},{0,4},{4,8},{8,12},{12,16},{16,20},{20,24},{24,28},{29,1},{... | collective-permute-start | bytes 786440 | tf_op jit(solution)/shard_map/ppermute | solution.py:346
  23.2 41.6 %collective-permute-start.5 = (bf16[128,1024]{1,0:T(8,128)(2,1)S(1)}, bf16[128,1024]{1,0:T(8,128)(2,1)}, u32[]{:S(2)}, u32[]{:S(2)}) collective-permute-start(bf16[128,1024]{1,0:T(8,128)(2,1)S(1)} %get-tuple-element.63), channel_id=1, source_target_pairs={{0,1},{1,0},{2,3},{3,2},{4,5},{5,4},{6,7},{7,6},{8,9},{9,8},{10,11... | collective-permute-start | bytes 786440 | tf_op jit(solution)/shard_map/ppermute | solution.py:21
  24.7 41.6 %collective-permute-start.6 = (bf16[128,1024]{1,0:T(8,128)(2,1)S(1)}, bf16[128,1024]{1,0:T(8,128)(2,1)}, u32[]{:S(2)}, u32[]{:S(2)}) collective-permute-start(bf16[128,1024]{1,0:T(8,128)(2,1)S(1)} %get-tuple-element.64), channel_id=1, source_target_pairs={{0,2},{1,3},{2,0},{3,1},{4,6},{5,7},{6,4},{7,5},{8,10},{9,11},{10,... | collective-permute-start | bytes 786440 | tf_op jit(solution)/shard_map/ppermute | solution.py:21
  26.2 40.1 %collective-permute-start.7 = (bf16[128,1024]{1,0:T(8,128)(2,1)S(1)}, bf16[128,1024]{1,0:T(8,128)(2,1)}, u32[]{:S(2)}, u32[]{:S(2)}) collective-permute-start(bf16[128,1024]{1,0:T(8,128)(2,1)S(1)} %get-tuple-element.65), channel_id=1, source_target_pairs={{0,3},{1,2},{2,1},{3,0},{4,7},{5,6},{6,5},{7,4},{8,11},{9,10},{10,... | collective-permute-start | bytes 786440 | tf_op jit(solution)/shard_map/ppermute | solution.py:21
  68.3 26.5 %collective-permute-start.10 = (bf16[128,1024]{1,0:T(8,128)(2,1)}, bf16[128,1024]{1,0:T(8,128)(2,1)S(1)}, u32[]{:S(2)}, u32[]{:S(2)}) collective-permute-start(bf16[128,1024]{1,0:T(8,128)(2,1)} %multiply_convert_fusion.2), channel_id=1, source_target_pairs={{0,3},{1,2},{2,1},{3,0},{4,7},{5,6},{6,5},{7,4},{8,11},{9,10},{10,... | collective-permute-start | bytes 786440 | tf_op jit(solution)/shard_map/ppermute | solution.py:21
  73.0 21.8 %collective-permute-start.8 = (bf16[128,1024]{1,0:T(8,128)(2,1)}, bf16[128,1024]{1,0:T(8,128)(2,1)}, u32[]{:S(2)}, u32[]{:S(2)}) collective-permute-start(bf16[128,1024]{1,0:T(8,128)(2,1)} %multiply_convert_fusion.2), channel_id=1, source_target_pairs={{0,1},{1,0},{2,3},{3,2},{4,5},{5,4},{6,7},{7,6},{8,9},{9,8},{10,11... | collective-permute-start | bytes 786440 | tf_op jit(solution)/shard_map/ppermute | solution.py:21
  125.9 35.2 %collective-permute-start.13 = (bf16[2,1024,1024]{2,1,0:T(8,128)(2,1)}, bf16[2,1024,1024]{2,1,0:T(8,128)(2,1)}, u32[]{:S(2)}, u32[]{:S(2)}) collective-permute-start(bf16[2,1024,1024]{2,1,0:T(8,128)(2,1)} %get-tuple-element.72), channel_id=1, source_target_pairs={{0,4},{8,12},{16,20},{24,28},{1,5},{9,13},{17,21},{25,29},{2,6},{1... | collective-permute-start | bytes 12582920 | tf_op jit(solution)/shard_map/ppermute | solution.py:346
  129.3 66.9 %collective-permute-start.20 = (bf16[2,1024,1024]{2,1,0:T(8,128)(2,1)}, bf16[2,1024,1024]{2,1,0:T(8,128)(2,1)}, u32[]{:S(2)}, u32[]{:S(2)}) collective-permute-start(bf16[2,1024,1024]{2,1,0:T(8,128)(2,1)} %get-tuple-element.82), channel_id=1, source_target_pairs={{24,0},{0,8},{8,16},{16,24},{25,1},{1,9},{9,17},{17,25},{26,2},{2,... | collective-permute-start | bytes 12582920 | tf_op jit(solution)/shard_map/ppermute | solution.py:346
  142.4 58.1 %collective-permute-start.12 = (bf16[512,1024]{0,1:T(8,128)(2,1)}, bf16[512,1024]{0,1:T(8,128)(2,1)}, u32[]{:S(2)}, u32[]{:S(2)}) collective-permute-start(bf16[512,1024]{0,1:T(8,128)(2,1)} %copy.34), channel_id=1, source_target_pairs={{28,4},{4,12},{12,20},{20,28},{29,5},{5,13},{13,21},{21,29},{30,6}... | collective-permute-start | bytes 3145736 | tf_op jit(solution)/shard_map/ppermute | solution.py:346
  161.1 38.3 %collective-permute-start.17 = (bf16[128,1024]{1,0:T(8,128)(2,1)S(1)}, bf16[128,1024]{1,0:T(8,128)(2,1)S(1)}, u32[]{:S(2)}, u32[]{:S(2)}) collective-permute-start(bf16[128,1024]{1,0:T(8,128)(2,1)S(1)} %multiply_convert_fusion.1), channel_id=1, source_target_pairs={{0,1},{1,0},{2,3},{3,2},{4,5},{5,4},{6,7},{7,6},{8,9},{9,8},{10,11... | collective-permute-start | bytes 786440 | tf_op jit(solution)/shard_map/ppermute | solution.py:21
  161.2 38.3 %collective-permute-start.18 = (bf16[128,1024]{1,0:T(8,128)(2,1)S(1)}, bf16[128,1024]{1,0:T(8,128)(2,1)S(1)}, u32[]{:S(2)}, u32[]{:S(2)}) collective-permute-start(bf16[128,1024]{1,0:T(8,128)(2,1)S(1)} %multiply_convert_fusion.1), channel_id=1, source_target_pairs={{0,2},{1,3},{2,0},{3,1},{4,6},{5,7},{6,4},{7,5},{8,10},{9,11},{10,... | collective-permute-start | bytes 786440 | tf_op jit(solution)/shard_map/ppermute | solution.py:21
  161.3 38.2 %collective-permute-start.19 = (bf16[128,1024]{1,0:T(8,128)(2,1)S(1)}, bf16[128,1024]{1,0:T(8,128)(2,1)S(1)}, u32[]{:S(2)}, u32[]{:S(2)}) collective-permute-start(bf16[128,1024]{1,0:T(8,128)(2,1)S(1)} %multiply_convert_fusion.1), channel_id=1, source_target_pairs={{0,3},{1,2},{2,1},{3,0},{4,7},{5,6},{6,5},{7,4},{8,11},{9,10},{10,... | collective-permute-start | bytes 786440 | tf_op jit(solution)/shard_map/ppermute | solution.py:21
  196.1 25.9 %collective-permute-start.21 = (bf16[2,1024,1024]{2,1,0:T(8,128)(2,1)}, bf16[2,1024,1024]{2,1,0:T(8,128)(2,1)}, u32[]{:S(2)}, u32[]{:S(2)}) collective-permute-start(bf16[2,1024,1024]{2,1,0:T(8,128)(2,1)} %collective-permute-done.20), channel_id=1, source_target_pairs={{0,4},{8,12},{16,20},{24,28},{1,5},{9,13},{17,21},{25,29},{2,6},{1... | collective-permute-start | bytes 12582920 | tf_op jit(solution)/shard_map/ppermute | solution.py:346
  214.7 52.5 %collective-permute-start.23 = (bf16[2,1024,1024]{2,1,0:T(8,128)(2,1)}, bf16[2,1024,1024]{2,1,0:T(8,128)(2,1)}, u32[]{:S(2)}, u32[]{:S(2)}) collective-permute-start(bf16[2,1024,1024]{2,1,0:T(8,128)(2,1)} %get-tuple-element.79.refs_1_), channel_id=1, source_target_pairs={{24,0},{0,8},{8,16},{16,24},{25,1},{1,9},{9,17},{17,25},{26,2},{2,... | collective-permute-start | bytes 12582920 | tf_op jit(solution)/shard_map/ppermute | solution.py:346
  322.5 23.4 %collective-permute-start.43 = (bf16[256,1024]{1,0:T(8,128)(2,1)S(1)}, bf16[256,1024]{1,0:T(8,128)(2,1)S(1)}, u32[]{:S(2)}, u32[]{:S(2)}) collective-permute-start(bf16[256,1024]{1,0:T(8,128)(2,1)S(1)} %get-tuple-element.111), channel_id=1, source_target_pairs={{0,8},{4,12},{24,16},{28,20},{1,9},{5,13},{25,17},{29,21},{2,10},{... | collective-permute-start | bytes 1572872 | tf_op jit(solution)/shard_map/ppermute | solution.py:276
  323.8 33.3 %collective-permute-start.39 = (bf16[256,1024]{1,0:T(8,128)(2,1)S(1)}, bf16[256,1024]{1,0:T(8,128)(2,1)S(1)}, u32[]{:S(2)}, u32[]{:S(2)}) collective-permute-start(bf16[256,1024]{1,0:T(8,128)(2,1)S(1)} %get-tuple-element.116), channel_id=1, source_target_pairs={{0,8},{4,12},{24,16},{28,20},{1,9},{5,13},{25,17},{29,21},{2,10},{... | collective-permute-start | bytes 1572872 | tf_op jit(solution)/shard_map/ppermute | solution.py:276
  325.2 42.7 %collective-permute-start.31 = (bf16[256,1024]{1,0:T(8,128)(2,1)S(1)}, bf16[256,1024]{1,0:T(8,128)(2,1)S(1)}, u32[]{:S(2)}, u32[]{:S(2)}) collective-permute-start(bf16[256,1024]{1,0:T(8,128)(2,1)S(1)} %get-tuple-element.115), channel_id=1, source_target_pairs={{0,8},{4,12},{24,16},{28,20},{1,9},{5,13},{25,17},{29,21},{2,10},{... | collective-permute-start | bytes 1572872 | tf_op jit(solution)/shard_map/ppermute | solution.py:276
  334.9 23.2 %collective-permute-start.34 = (bf16[256,1024]{1,0:T(8,128)(2,1)S(1)}, bf16[256,1024]{1,0:T(8,128)(2,1)S(1)}, u32[]{:S(2)}, u32[]{:S(2)}) collective-permute-start(bf16[256,1024]{1,0:T(8,128)(2,1)S(1)} %fusion.1), channel_id=1, source_target_pairs={{8,16},{12,20},{16,8},{20,12},{9,17},{13,21},{17,9},{21,13},{10,18... | collective-permute-start | bytes 1572872 | tf_op jit(solution)/shard_map/ppermute | solution.py:276
  346.1 22.0 %collective-permute-start.44 = (bf16[256,1024]{1,0:T(8,128)(2,1)S(1)}, bf16[256,1024]{1,0:T(8,128)(2,1)S(1)}, u32[]{:S(2)}, u32[]{:S(2)}) collective-permute-start(bf16[256,1024]{1,0:T(8,128)(2,1)S(1)} %fusion.6), channel_id=1, source_target_pairs={{8,16},{12,20},{16,8},{20,12},{9,17},{13,21},{17,9},{21,13},{10,18... | collective-permute-start | bytes 1572872 | tf_op jit(solution)/shard_map/ppermute | solution.py:276
  377.0 21.6 %collective-permute-start.41 = (bf16[256,1024]{1,0:T(8,128)(2,1)S(1)}, bf16[256,1024]{1,0:T(8,128)(2,1)S(1)}, u32[]{:S(2)}, u32[]{:S(2)}) collective-permute-start(bf16[256,1024]{1,0:T(8,128)(2,1)S(1)} %fusion.5), channel_id=1, source_target_pairs={{8,0},{12,4},{16,24},{20,28},{9,1},{13,5},{17,25},{21,29},{10,2},{... | collective-permute-start | bytes 1572872 | tf_op jit(solution)/shard_map/ppermute | solution.py:276
  378.4 30.0 %collective-permute-start.47 = (bf16[256,1024]{1,0:T(8,128)(2,1)S(1)}, bf16[256,1024]{1,0:T(8,128)(2,1)}, u32[]{:S(2)}, u32[]{:S(2)}) collective-permute-start(bf16[256,1024]{1,0:T(8,128)(2,1)S(1)} %broadcast_select_fusion.own), channel_id=1, source_target_pairs={{0,4},{4,0},{8,12},{12,8},{16,20},{20,16},{24,28},{28,24},{1,5},{5... | collective-permute-start | bytes 1572872 | tf_op jit(solution)/shard_map/ppermute | solution.py:21
  378.7 29.5 %collective-permute-start.37 = (bf16[256,1024]{1,0:T(8,128)(2,1)S(1)}, bf16[256,1024]{1,0:T(8,128)(2,1)S(1)}, u32[]{:S(2)}, u32[]{:S(2)}) collective-permute-start(bf16[256,1024]{1,0:T(8,128)(2,1)S(1)} %fusion.3), channel_id=1, source_target_pairs={{8,0},{12,4},{16,24},{20,28},{9,1},{13,5},{17,25},{21,29},{10,2},{... | collective-permute-start | bytes 1572872 | tf_op jit(solution)/shard_map/ppermute | solution.py:276
  387.4 26.2 %collective-permute-start.46 = (bf16[256,1024]{1,0:T(8,128)(2,1)S(1)}, bf16[256,1024]{1,0:T(8,128)(2,1)S(1)}, u32[]{:S(2)}, u32[]{:S(2)}) collective-permute-start(bf16[256,1024]{1,0:T(8,128)(2,1)S(1)} %broadcast_select_fusion.1.own), channel_id=1, source_target_pairs={{0,4},{4,0},{8,12},{12,8},{16,20},{20,16},{24,28},{28,24},{1,5},{5... | collective-permute-start | bytes 1572872 | tf_op jit(solution)/shard_map/ppermute | solution.py:21
  (51 other events, 459.9 us)

commit v8 on v7

--- a/solution.py
+++ b/solution.py
@@ -134,7 +134,7 @@
 def backward_kernel(update, taken, pieces, given, by_core, flag, weights, slope, hidden, inputs_t, *refs):
     states, refs = regrouped(refs, taken)
     errors, refs, error, error_t = refs[:pieces], refs[pieces:-2], refs[-2], refs[-1]
-    results, _ = regrouped(refs, given)
+    results, _ = regrouped(refs[len(refs) - sum(given) :], given)
 
     @pl.when(pl.program_id(0) == 0)
     def _():
@@ -165,7 +165,7 @@
                 piece[...] = value[i * size : (i + 1) * size].astype(piece.dtype)
 
 
-def backward(flag, errors, weights, slope, hidden, inputs_t, states, update, kinds):
+def backward(flag, errors, weights, slope, hidden, inputs_t, states, update, kinds, waits=()):
     width, rows = inputs_t.shape
     units = weights.shape[2]
     block = min(units, 512)
@@ -188,7 +188,8 @@
             whole((width, rows)),
         ]
         + [block_of(part, block) for part in flat]
-        + [whole(piece.shape) for piece in errors],
+        + [whole(piece.shape) for piece in errors]
+        + [ANY] * len(waits),
         out_specs=[block_of(shape, block) for shape in shapes],
         out_shape=shapes,
         scratch_shapes=[pltpu.VMEM((rows, width), bf16), pltpu.VMEM((width, rows), bf16)],
@@ -196,7 +197,7 @@
         cost_estimate=pl.CostEstimate(
             flops=6 * rows * width * units, bytes_accessed=28 * width * units, transcendentals=0
         ),
-    )(flag, weights, slope, hidden, inputs_t, *flat, *errors)
+    )(flag, weights, slope, hidden, inputs_t, *flat, *errors, *waits)
     return regrouped(results, [count for _, count in kinds])[0]
 
 
@@ -231,8 +232,38 @@
     return rounded(left.astype(f32) + right.astype(f32))
 
 
-def tied(early, late):
-    return lax.optimization_barrier((early, late))[1]
+ANY = pl.BlockSpec(memory_space=pl.ANY)
+
+
+def nothing(*refs):
+    pass
+
+
+def tied(waits, block):
+    return pl.pallas_call(
+        nothing,
+        in_specs=[ANY] * (1 + len(waits)),
+        out_specs=ANY,
+        out_shape=jax.ShapeDtypeStruct(block.shape, block.dtype),
+        input_output_aliases={0: 0},
+    )(block, *waits)
+
+
+def cast_kernel(block, *refs):
+    refs[-1][...] = block[...].astype(bf16)
+
+
+def narrowed(block, waits):
+    _, rows, units = block.shape
+    spec = pl.BlockSpec((1, rows // 4, units), lambda k, j: (k, j, 0))
+    return pl.pallas_call(
+        cast_kernel,
+        grid=(2, 4),
+        in_specs=[spec] + [ANY] * len(waits),
+        out_specs=spec,
+        out_shape=jax.ShapeDtypeStruct(block.shape, bf16),
+        cost_estimate=pl.CostEstimate(flops=2 * rows * units, bytes_accessed=12 * rows * units, transcendentals=0),
+    )(block, *waits)
 
 
 def finish_kernel(replicas, flag, slow, anchor, own, theirs, *refs):
@@ -245,21 +276,22 @@
     token[...] = jnp.zeros_like(token)
 
 
-def finish(flag, replicas, slow, anchor, own, theirs, position, before):
+def finish(flag, replicas, slow, anchor, own, theirs, position, before, waits):
     size, units = own.shape
-    rows = pl.BlockSpec((2, size, units), lambda j: (0, position, 0))
+    steps = 4
+    rows = pl.BlockSpec((2, size // steps, units), lambda j: (0, position * steps + j, 0))
+    part = pl.BlockSpec((size // steps, units), lambda j: (j, 0))
     shape = jax.ShapeDtypeStruct(slow.shape, f32)
     return pl.pallas_call(
         functools.partial(finish_kernel, replicas),
-        grid=(1,),
-        in_specs=[pl.BlockSpec(memory_space=pltpu.SMEM), rows, rows, whole(own.shape), whole(own.shape)]
-        + [pl.BlockSpec(memory_space=pl.ANY)] * len(before),
+        grid=(steps,),
+        in_specs=[pl.BlockSpec(memory_space=pltpu.SMEM), rows, rows, part, part] + [ANY] * (len(before) + len(waits)),
         out_specs=[rows, rows, whole((8, 128))],
         out_shape=[shape, shape, jax.ShapeDtypeStruct((8, 128), bf16)],
         input_output_aliases={5 + k: k for k in range(len(before))},
         compiler_params=pltpu.CompilerParams(vmem_limit_bytes=60 << 20),
         cost_estimate=pl.CostEstimate(flops=8 * size * units, bytes_accessed=36 * size * units, transcendentals=0),
-    )(flag, slow, anchor, own, theirs, *before)
+    )(flag, slow, anchor, own, theirs, *before, *waits)
 
 
 def slow_step(flag, mine, other, slow, anchor):
@@ -289,34 +321,31 @@
     for c in range(chunks):
         p, start = divmod(c * size, pair_rows)
         blocks.append(added(mine[c * size : (c + 1) * size], pairs[p][start : start + size]))
+    order = []
+    for tick in range(chunks + 2 * len(stages) + 1):
+        for s in range(len(stages) + 1):
+            c = tick - 2 * s
+            if 0 <= c < chunks:
+                order.append((s, c))
     arrived = {}
-    tokens, results = {}, []
-    final = len(stages) - 1
-
-    def after(block, *waits):
-        waits = [arrived.get(wait, tokens.get(wait)) for wait in waits]
-        waits = [wait for wait in waits if wait is not None]
-        return tied(waits, block) if waits else block
-
-    for tick in range(chunks + 2 * len(stages) + 1):
-        for s in reversed(range(len(stages) + 1)):
-            c = tick - 2 * s
-            if not 0 <= c < chunks:
-                continue
-            if s:
-                adds, hops = stages[s - 1]
-                fresh = added(blocks[c], arrived[s - 1, c]) if adds else arrived[s - 1, c]
-                blocks[c] = jnp.where(at([b for _, b in hops]), fresh, blocks[c])
-            if s < len(stages):
-                block = blocks[c]
-                if 0 < s < final:
-                    block = after(block, (s + 1, c - 3))
-                elif s:
-                    block = after(block, c - 3)
-                arrived[s, c] = moved(block, stages[s][1])
-            else:
-                own = blocks[c]
-                *results, tokens[c] = finish(flag, replicas, slow, anchor, own, swapped(own, axis, 1), c, results)
+    results, last = [], None
+
+    def chained(block):
+        return block if last is None else jnp.where(chip < length, block, last)
+
+    for s, c in order:
+        if s:
+            adds, hops = stages[s - 1]
+            fresh = added(blocks[c], arrived[s - 1, c]) if adds else arrived[s - 1, c]
+            last = blocks[c] = chained(jnp.where(at([b for _, b in hops]), fresh, blocks[c]))
+        if s < len(stages):
+            arrived[s, c] = moved(blocks[c], stages[s][1])
+        else:
+            own = blocks[c]
+            *results, token = finish(
+                flag, replicas, slow, anchor, own, swapped(own, axis, 1), c, results, [] if c == 0 else [last]
+            )
+            last = jnp.broadcast_to(token[:1, :1], own.shape)
     return results
 
 
@@ -348,55 +377,70 @@
     def picked(step, count):
         return tokens.at[picks_all[step, :count]].get(mode="promise_in_bounds")
 
-    near_rows = picked(0, share_rows)
-    near_share = sent(near_rows, 1)
-    moment_near = sent(tied(near_rows, momentum[0]).astype(bf16), 1)
-    inputs_near = jnp.concatenate(gathered(near_share))
-
     inputs = picked(0, row_count)
+    inputs_near = sent(inputs, 1)
+    moment_near = sent(narrowed(momentum[0], [inputs]), 1)
+
     hidden, slope, *partials = forward(flag, inputs, [anchor], only, tensors, emits=False)
-    own_error = error_share(partials, 0)
+    error = jnp.concatenate(gathered(error_share(partials, 0)))
+    error_near = sent(error, 1)
     hidden_near, slope_near = forward(flag, inputs_near, [anchor], only, 0, emits=False)
-    error = tied((hidden_near, inputs_near.T), jnp.concatenate(gathered(own_error)))
-    error_near = sent(error, 1)
+    inputs_near_t = inputs_near.T
     moment, moment_bf = backward(
-        flag, [error], anchor, slope, hidden, inputs.T, [momentum[0]], first_update, [f32, bf16]
-    )
-    moment_far = sent(tied(error_near, moment_bf), 2, (0,))
+        flag,
+        [error],
+        anchor,
+        slope,
+        hidden,
+        inputs.T,
+        [momentum[0]],
+        first_update,
+        [f32, bf16],
+        waits=[hidden_near, inputs_near_t],
+    )
+    moment_far = sent(moment_bf, 2, (0,))
+    inputs = tied([moment], picked(1, row_count))
+    inputs_far = sent(inputs, 2, (1,))
     moment_near, weights = backward(
         flag,
         [error_near],
         anchor,
         slope_near,
         hidden_near,
-        inputs_near.T,
+        inputs_near_t,
         [moment_near, moment, anchor],
         first_beside,
         [bf16, bf16],
     )
 
-    inputs = picked(1, row_count)
-    inputs_far = sent(tied(error_near, inputs), 2, (1,))
+    moment_two = sent(moment_near, 1, (1,))
     hidden, slope, *partials = forward(flag, inputs, [weights], only, tensors, emits=False)
-    moment_two = sent(moment_near, 1, (1,))
-    own_error = error_share(partials, 1)
-    own_error = tied(moment_two, own_error)
-    error = tied((inputs_far, inputs.T), jnp.concatenate(gathered(own_error)))
+    error = jnp.concatenate(gathered(error_share(partials, 1)))
     error_far = sent(error, 2, (1,))
+    inputs_far_t = inputs_far.T
     moment, weights, known = backward(
-        flag, [error], weights, slope, hidden, inputs.T, [moment, weights], second_update, [f32, bf16, bf16]
-    )
+        flag,
+        [error],
+        weights,
+        slope,
+        hidden,
+        inputs.T,
+        [moment, weights],
+        second_update,
+        [f32, bf16, bf16],
+        waits=[inputs_far_t, moment_two],
+    )
+    weights = tied([error_far], weights)
     weights_sent = sent(weights, 2, (0,))
-    moment_three = sent(moment_far, 1, (1,))
-    inputs_far = tied(weights, inputs_far)
+    moment_three = sent(tied([weights], moment_far), 1, (1,))
     hidden, slope, weights_far = forward(flag, inputs_far, [anchor, moment_two, moment_three], pushed, 0)
     (weights_found,) = backward(
-        flag, [error_far], weights_far, slope, hidden, inputs_far.T, [moment_two, weights_far], second_beside, [bf16]
+        flag, [error_far], weights_far, slope, hidden, inputs_far_t, [moment_two, weights_far], second_beside, [bf16]
     )
 
     inputs = picked(2, row_count)
     hidden, slope, *rest = forward(flag, inputs, [weights_found, weights, weights_sent], halved, tensors)
-    errors = tied(inputs.T, gathered(error_share(rest[:tensors], 2)))
+    errors = gathered(error_share(rest[:tensors], 2))
     moment, total = backward(
         flag, errors, rest[tensors], slope, hidden, inputs.T, [moment, known], third_update, [f32, (bf16, "core")]
     )

time: 441 us -> 438 us (level)
  waiting for transfers between devices: 199 us -> 178 us
  starting transfers between devices: 56.3 us -> 63.9 us
  Pallas kernels: 117 us -> 124 us
    ppermute x9, waiting for transfers between devices: 91.6 us -> 59.5 us  [sent(): return lax.ppermute(block, 'replica', route)]
    ppermute x27 -> x24, waiting for transfers between devices: 35.7 us -> 50.3 us  [swapped(): lax.ppermute(block, axis, [(i, i ^ mask) for i in range(lax.axis_size(axi...]
    select_n x12 -> x6, other arithmetic: 1.81 us -> 10.9 us  [the longest x5 9.69 us: chained(): return block if last is None else jnp.where(chip < length, block, last)]
    ppermute x12, starting transfers between devices: 13.2 us -> 20.8 us  [moved(): lax.ppermute(part, axis, [(cores * a + c, cores * b + c) for a, b in hops...]
    pallas_call x4 -> x8, Pallas kernels: 20.7 us -> 27.9 us  [the longest x4 20.1 us: finish(): pl.pallas_call(functools.partial(finish_kernel, replicas), grid=(steps,),...]
    convert_element_type x1 -> x0, other arithmetic: 6.06 us -> none  [body(): moment_near = sent(tied(near_rows, momentum[0]).astype(bf16), 1)]
    ppermute x27 -> x24, starting transfers between devices: 25.8 us -> 22.5 us  [swapped(): lax.ppermute(block, axis, [(i, i ^ mask) for i in range(lax.axis_size(axi...]
    unnamed x57 -> x80, local copies, waits for them, and re-layouts: 16.5 us -> 18.7 us
  transfers between devices with their start and end apart: 48 -> 45, of which waited for: 21 -> 30; matrix products, arithmetic and copies ran while one was open for 7% -> 7% of each run, Pallas kernels for 18% -> 18%
where the time goes in v8:
time: 438 us; the launch traced here: 430 us
  waiting for transfers between devices  178 us (41%)
  Pallas kernels  124 us (28%)
  starting transfers between devices  63.9 us (15%)
  local copies, waits for them, and re-layouts  44.1 us (10%)
  other arithmetic  17.9 us (4%)
    ppermute x12, waiting for transfers between devices, moved(): lax.ppermute(part, axis, [(cores * a + c, cores * b + c) for a, b in hops...  68.1 us
    pallas_call x5, Pallas kernels, backward(): pl.pallas_call(functools.partial(backward_kernel, update, counts, len(err...  62 us
    ppermute x9, waiting for transfers between devices, sent(): return lax.ppermute(block, 'replica', route)  59.5 us
    ppermute x24, waiting for transfers between devices, swapped(): lax.ppermute(block, axis, [(i, i ^ mask) for i in range(lax.axis_size(axi...  50.3 us
    pallas_call x5, Pallas kernels, forward(): pl.pallas_call(functools.partial(forward_kernel, mix, counts, sums, emits...  34.3 us
    ppermute x24, starting transfers between devices, swapped(): lax.ppermute(block, axis, [(i, i ^ mask) for i in range(lax.axis_size(axi...  22.5 us
    ppermute x12, starting transfers between devices, moved(): lax.ppermute(part, axis, [(cores * a + c, cores * b + c) for a, b in hops...  20.8 us
    ppermute x9, starting transfers between devices, sent(): return lax.ppermute(block, 'replica', route)  20.7 us
  transfers between devices with their start and end apart: 45, of which 30 were waited for; matrix products, arithmetic and copies ran while one was open for 7% of the time, Pallas kernels for 18%

profile of v8, /device:TPU:0, one launch (start us, length us, event | category | flops | bytes accessed | tf_op | source)
XLA Modules:
  0.0 429.7 jit_solution(11835479819307656221)
XLA Ops:
  4.8 7.8 %shard_map.89 = bf16[2,1024,1024]{2,1,0:T(8,128)(2,1)} custom-call(f32[2,1024,1024]{2,1,0:T(8,128)} %bitcast.50, bf16[512,1024]{1,0:T(8,128)(2,1)} %gather_fusion.3), custom_call_target="tpu_custom_call" | custom-call | flops 2097152 | bytes 12582912 | tf_op jit(solution)/shard_map/pallas_call | solution.py:259
  13.1 6.2 %shard_map.85 = (bf16[512,1024]{1,0:T(8,128)(2,1)S(1)}, bf16[512,1024]{1,0:T(8,128)(2,1)S(1)}, bf16[128,1024]{1,0:T(8,128)(2,1)S(1)}, bf16[128,1024]{1,0:T(8,128...) custom-call(s32[1]{0:T(128)} %bitcast.flag, bf16[512,1024]{1,0:T(8,128)(2,1)S(1)} %copy-done.2, ...), custom_call_target="tpu_custom_call" | custom-call | flops 2147483648 | bytes 16777216 | tf_op jit(solution)/shard_map/pallas_call | solution.py:105
  30.4 8.0 %collective-permute-done.1 = bf16[128,1024]{1,0:T(8,128)(2,1)} collective-permute-done((bf16[128,1024]{1,0:T(8,128)(2,1)S(1)}, bf16[128,1024]{1,0:T(8,128)(2,1)}, u32[]{:S(2)}, u32[]{:S(2)}) %collective-permute-start.1) | collective-permute-done | bytes 262176 | tf_op jit(solution)/shard_map/ppermute | solution.py:21
  43.2 5.6 %collective-permute-done.3 = bf16[128,1024]{1,0:T(8,128)(2,1)S(1)} collective-permute-done((bf16[128,1024]{1,0:T(8,128)(2,1)S(1)}, bf16[128,1024]{1,0:T(8,128)(2,1)S(1)}, u32[]{:S(2)}, u32[]{:S(2)}) %collective-permute-start.3) | collective-permute-done | bytes 262176 | tf_op jit(solution)/shard_map/ppermute | solution.py:21
  55.1 19.7 %collective-permute-done.6 = bf16[512,1024]{0,1:T(8,128)(2,1)} collective-permute-done((bf16[512,1024]{0,1:T(8,128)(2,1)}, bf16[512,1024]{0,1:T(8,128)(2,1)}, u32[]{:S(2)}, u32[]{:S(2)}) %collective-permute-start.6) | collective-permute-done | bytes 1048608 | tf_op jit(solution)/shard_map/ppermute | solution.py:375
  82.6 10.6 %shard_map.87 = (f32[2,1024,1024]{2,1,0:T(8,128)}, bf16[2,1024,1024]{2,1,0:T(8,128)(2,1)}) custom-call(s32[1]{0:T(128)} %bitcast.flag, f32[2,1024,1024]{2,1,0:T(8,128)} %anchor.7, bf16[512,1024]{1,0:T(8,128)(2,1)} %copy-done.7, bf16[512,1024]{1,0:T(8,128)(2,1)} %copy-done.6, bf16[1024,512]{1,0:T(8,128)(2,1)} %bitcast.54, f32[2,1024,1024]{2,1,0:T(8,128)} %bitcast.51, ...), custom_call_target="tpu_custom_call" | custom-call | flops 3221225472 | bytes 29360128 | tf_op jit(solution)/shard_map/pallas_call | solution.py:180
  93.2 13.8 %shard_map.90 = (bf16[2,1024,1024]{2,1,0:T(8,128)(2,1)}, bf16[2,1024,1024]{2,1,0:T(8,128)(2,1)}) custom-call(s32[1]{0:T(128)} %bitcast.flag, f32[2,1024,1024]{2,1,0:T(8,128)} %anchor.7, bf16[512,1024]{1,0:T(8,128)(2,1)} %copy-done.12, bf16[512,1024]{1,0:T(8,128)(2,1)} %copy-done.5, bf16[1024,512]{1,0:T(8,128)(2,1)} %bitcast.15.refs_3_.inputs_t, ...), custom_call_target="tpu_custom_call" | custom-call | flops 3221225472 | bytes 29360128 | tf_op jit(solution)/shard_map/pallas_call | solution.py:180
  116.7 5.6 %shard_map.91 = (bf16[512,1024]{1,0:T(8,128)(2,1)S(1)}, bf16[512,1024]{1,0:T(8,128)(2,1)S(1)}, bf16[128,1024]{1,0:T(8,128)(2,1)S(1)}, bf16[128,1024]{1,0:T(8,128...) custom-call(s32[1]{0:T(128)} %bitcast.flag, bf16[512,1024]{1,0:T(8,128)(2,1)S(1)} %copy-done.3, ...), custom_call_target="tpu_custom_call" | custom-call | flops 2147483648 | bytes 16777216 | tf_op jit(solution)/shard_map/pallas_call | solution.py:105
  151.6 14.1 %shard_map.92 = (f32[2,1024,1024]{2,1,0:T(8,128)}, bf16[2,1024,1024]{2,1,0:T(8,128)(2,1)}, bf16[2,1024,1024]{2,1,0:T(8,128)(2,1)}) custom-call(s32[1]{0:T(128)} %bitcast.flag, bf16[2,1024,1024]{2,1,0:T(8,128)(2,1)} %get-tuple-element.59.refs_0_.weights.refs_1_, bf16[512,1024]{1,0:T(8,128)(2,1)} %copy-done.9, bf16[512,1024]{1,0:T(8,128)(2,1)} %copy-done.8, ...), custom_call_target="tpu_custom_call" | custom-call | flops 3221225472 | bytes 29360128 | tf_op jit(solution)/shard_map/pallas_call | solution.py:180
  166.7 13.5 %collective-permute-done.11.refs_0_ = bf16[2,1024,1024]{2,1,0:T(8,128)(2,1)} collective-permute-done((bf16[2,1024,1024]{2,1,0:T(8,128)(2,1)}, bf16[2,1024,1024]{2,1,0:T(8,128)(2,1)}, u32[]{:S(2)}, u32[]{:S(2)}) %collective-permute-start.11) | collective-permute-done | bytes 4194336 | tf_op jit(solution)/shard_map/ppermute | solution.py:375
  180.3 9.6 %collective-permute-start.19 = (bf16[2,1024,1024]{2,1,0:T(8,128)(2,1)}, bf16[2,1024,1024]{2,1,0:T(8,128)(2,1)}, u32[]{:S(2)}, u32[]{:S(2)}) collective-permute-start(bf16[2,1024,1024]{2,1,0:T(8,128)(2,1)} %shard_map.94), channel_id=1, source_target_pairs={{0,4},{8,12},{16,20},{24,28},{1,5},{9,13},{17,21},{25,29},{2,6},{1... | collective-permute-start | bytes 12582920 | tf_op jit(solution)/shard_map/ppermute | solution.py:375
  195.0 9.4 %shard_map.95 = (bf16[512,1024]{1,0:T(8,128)(2,1)S(1)}, bf16[512,1024]{1,0:T(8,128)(2,1)S(1)}, bf16[2,1024,1024]{2,1,0:T(8,128)(2,1)}) custom-call(s32[1]{0:T(128)} %bitcast.flag, bf16[512,1024]{1,0:T(8,128)(2,1)S(1)} %copy.38.inputs, f32[2,1024,1024]{2,1,0:T(8,128)} %anchor.7, bf16[2,1024,1024]{2,1,0:T(8,128)(2,1)} %collective-permute-done.10.refs_4_.refs_1_.refs_0_, ...), custom_call_target="tpu_custom_call" | custom-call | flops 1073741824 | bytes 16777216 | tf_op jit(solution)/shard_map/pallas_call | solution.py:105
  206.4 10.1 %shard_map.96.refs_0_ = bf16[2,1024,1024]{2,1,0:T(8,128)(2,1)} custom-call(s32[1]{0:T(128)} %bitcast.flag, bf16[2,1024,1024]{2,1,0:T(8,128)(2,1)} %get-tuple-element.67.weights.refs_1_, bf16[512,1024]{1,0:T(8,128)(2,1)} %copy-done.14, bf16[512,1024]{1,0:T(8,128)(2,1)} %copy-done.13, bf16[1024,512]{1,0:T(8,128)(2,1)} %bitcast.53, ...), custom_call_target="tpu_custom_call" | custom-call | flops 3221225472 | bytes 29360128 | tf_op jit(solution)/shard_map/pallas_call | solution.py:180
  216.5 25.9 %collective-permute-done.20.refs_2_ = bf16[2,1024,1024]{2,1,0:T(8,128)(2,1)} collective-permute-done((bf16[2,1024,1024]{2,1,0:T(8,128)(2,1)}, bf16[2,1024,1024]{2,1,0:T(8,128)(2,1)}, u32[]{:S(2)}, u32[]{:S(2)}) %collective-permute-start.20) | collective-permute-done | bytes 4194336 | tf_op jit(solution)/shard_map/ppermute | solution.py:375
  242.4 8.8 %shard_map.97 = (bf16[512,1024]{1,0:T(8,128)(2,1)S(1)}, bf16[512,1024]{1,0:T(8,128)(2,1)S(1)}, bf16[128,1024]{1,0:T(8,128)(2,1)S(1)}, bf16[128,1024]{1,0:T(8,128...) custom-call(s32[1]{0:T(128)} %bitcast.flag, ...), custom_call_target="tpu_custom_call" | custom-call | flops 2147483648 | bytes 16777216 | tf_op jit(solution)/shard_map/pallas_call | solution.py:105
  276.8 13.3 %shard_map.98 = (f32[2,1024,1024]{2,1,0:T(8,128)}, bf16[1024,1024]{1,0:T(8,128)(2,1)}, bf16[1024,1024]{1,0:T(8,128)(2,1)}) custom-call(s32[1]{0:T(128)} %bitcast.flag, bf16[2,1024,1024]{2,1,0:T(8,128)(2,1)} %get-tuple-element.70.weights, bf16[512,1024]{1,0:T(8,128)(2,1)} %copy-done.11, bf16[512,1024]{1,0:T(8,128)(2,1)} %copy-done.10, ...), custom_call_target="tpu_custom_call" | custom-call | flops 3221225472 | bytes 29360128 | tf_op jit(solution)/shard_map/pallas_call | solution.py:180
  302.7 8.0 %collective-permute-done.30 = bf16[256,1024]{1,0:T(8,128)(2,1)} collective-permute-done((bf16[256,1024]{1,0:T(8,128)(2,1)S(1)}, bf16[256,1024]{1,0:T(8,128)(2,1)}, u32[]{:S(2)}, u32[]{:S(2)}) %collective-permute-start.30) | collective-permute-done | bytes 524320 | tf_op jit(solution)/shard_map/ppermute | solution.py:308
  313.4 5.8 %collective-permute-start.28 = (bf16[256,1024]{1,0:T(8,128)(2,1)S(1)}, bf16[256,1024]{1,0:T(8,128)(2,1)}, u32[]{:S(2)}, u32[]{:S(2)}) collective-permute-start(bf16[256,1024]{1,0:T(8,128)(2,1)S(1)} %get-tuple-element.102), channel_id=1, source_target_pairs={{0,8},{4,12},{24,16},{28,20},{1,9},{5,13},{25,17},{29,21},{2,10},{... | collective-permute-start | bytes 1572872 | tf_op jit(solution)/shard_map/ppermute | solution.py:308
  321.9 11.2 %collective-permute-done.33 = bf16[256,1024]{1,0:T(8,128)(2,1)} collective-permute-done((bf16[256,1024]{1,0:T(8,128)(2,1)S(1)}, bf16[256,1024]{1,0:T(8,128)(2,1)}, u32[]{:S(2)}, u32[]{:S(2)}) %collective-permute-start.33) | collective-permute-done | bytes 524320 | tf_op jit(solution)/shard_map/ppermute | solution.py:308
  343.9 7.3 %collective-permute-done.35 = bf16[256,1024]{1,0:T(8,128)(2,1)S(1)} collective-permute-done((bf16[256,1024]{1,0:T(8,128)(2,1)S(1)}, bf16[256,1024]{1,0:T(8,128)(2,1)S(1)}, u32[]{:S(2)}, u32[]{:S(2)}) %collective-permute-start.35) | collective-permute-done | bytes 524320 | tf_op jit(solution)/shard_map/ppermute | solution.py:308
  365.0 20.0 %collective-permute-done.41 = bf16[256,1024]{1,0:T(8,128)(2,1)S(1)} collective-permute-done((bf16[256,1024]{1,0:T(8,128)(2,1)S(1)}, bf16[256,1024]{1,0:T(8,128)(2,1)S(1)}, u32[]{:S(2)}, u32[]{:S(2)}) %collective-permute-start.41) | collective-permute-done | bytes 524320 | tf_op jit(solution)/shard_map/ppermute | solution.py:308
  396.3 7.2 %collective-permute-done.40 = bf16[256,1024]{1,0:T(8,128)(2,1)S(1)} collective-permute-done((bf16[256,1024]{1,0:T(8,128)(2,1)S(1)}, bf16[256,1024]{1,0:T(8,128)(2,1)S(1)}, u32[]{:S(2)}, u32[]{:S(2)}) %collective-permute-start.40) | collective-permute-done | bytes 524320 | tf_op jit(solution)/shard_map/ppermute | solution.py:308
  413.4 7.2 %collective-permute-done.39 = bf16[256,1024]{1,0:T(8,128)(2,1)S(1)} collective-permute-done((bf16[256,1024]{1,0:T(8,128)(2,1)S(1)}, bf16[256,1024]{1,0:T(8,128)(2,1)S(1)}, u32[]{:S(2)}, u32[]{:S(2)}) %collective-permute-start.39) | collective-permute-done | bytes 524320 | tf_op jit(solution)/shard_map/ppermute | solution.py:308
  424.1 5.1 %shard_map.102 = (f32[2,1024,1024]{2,1,0:T(8,128)}, f32[2,1024,1024]{2,1,0:T(8,128)}, bf16[8,128]{1,0:T(8,128)(2,1)}) custom-call(s32[1]{0:T(128)} %bitcast.flag, f32[2,1024,1024]{2,1,0:T(8,128)} %slow.7, f32[2,1024,1024]{2,1,0:T(8,128)} %anchor.7, bf16[256,1024]{1,0:T(8,128)(2,1)} %copy-done.19, ...), custom_call_target="tpu_custom_call", output_to_operand_aliasing={{0}: (5, {}), {1}: (6, {})} | custom-call | flops 2097152 | bytes 9437184 | tf_op jit(solution)/shard_map/pallas_call | solution.py:285
  (203 shorter events, 173.9 us)
Async XLA Ops:
  12.6 80.6 %collective-permute-start.8 = (bf16[2,1024,1024]{2,1,0:T(8,128)(2,1)}, bf16[2,1024,1024]{2,1,0:T(8,128)(2,1)}, u32[]{:S(2)}, u32[]{:S(2)}) collective-permute-start(bf16[2,1024,1024]{2,1,0:T(8,128)(2,1)} %shard_map.89), channel_id=1, source_target_pairs={{28,0},{0,4},{4,8},{8,12},{12,16},{16,20},{20,24},{24,28},{29,1},{... | collective-permute-start | bytes 12582920 | tf_op jit(solution)/shard_map/ppermute | solution.py:375
  23.8 14.5 %collective-permute-start.1 = (bf16[128,1024]{1,0:T(8,128)(2,1)S(1)}, bf16[128,1024]{1,0:T(8,128)(2,1)}, u32[]{:S(2)}, u32[]{:S(2)}) collective-permute-start(bf16[128,1024]{1,0:T(8,128)(2,1)S(1)} %get-tuple-element.52), channel_id=1, source_target_pairs={{0,2},{1,3},{2,0},{3,1},{4,6},{5,7},{6,4},{7,5},{8,10},{9,11},{10,... | collective-permute-start | bytes 786440 | tf_op jit(solution)/shard_map/ppermute | solution.py:21
  25.3 13.0 %collective-permute-start.2 = (bf16[128,1024]{1,0:T(8,128)(2,1)S(1)}, bf16[128,1024]{1,0:T(8,128)(2,1)}, u32[]{:S(2)}, u32[]{:S(2)}) collective-permute-start(bf16[128,1024]{1,0:T(8,128)(2,1)S(1)} %get-tuple-element.53), channel_id=1, source_target_pairs={{0,3},{1,2},{2,1},{3,0},{4,7},{5,6},{6,5},{7,4},{8,11},{9,10},{10,... | collective-permute-start | bytes 786440 | tf_op jit(solution)/shard_map/ppermute | solution.py:21
  26.7 48.2 %collective-permute-start.6 = (bf16[512,1024]{0,1:T(8,128)(2,1)}, bf16[512,1024]{0,1:T(8,128)(2,1)}, u32[]{:S(2)}, u32[]{:S(2)}) collective-permute-start(bf16[512,1024]{0,1:T(8,128)(2,1)} %copy.33), channel_id=1, source_target_pairs={{28,0},{0,4},{4,8},{8,12},{12,16},{16,20},{20,24},{24,28},{29,1},{... | collective-permute-start | bytes 3145736 | tf_op jit(solution)/shard_map/ppermute | solution.py:375
  40.3 13.0 %collective-permute-start.4 = (bf16[128,1024]{1,0:T(8,128)(2,1)S(1)}, bf16[128,1024]{1,0:T(8,128)(2,1)S(1)}, u32[]{:S(2)}, u32[]{:S(2)}) collective-permute-start(bf16[128,1024]{1,0:T(8,128)(2,1)S(1)} %multiply_convert_fusion.2), channel_id=1, source_target_pairs={{0,2},{1,3},{2,0},{3,1},{4,6},{5,7},{6,4},{7,5},{8,10},{9,11},{10,... | collective-permute-start | bytes 786440 | tf_op jit(solution)/shard_map/ppermute | solution.py:21
  41.8 13.2 %collective-permute-start.5 = (bf16[128,1024]{1,0:T(8,128)(2,1)S(1)}, bf16[128,1024]{1,0:T(8,128)(2,1)S(1)}, u32[]{:S(2)}, u32[]{:S(2)}) collective-permute-start(bf16[128,1024]{1,0:T(8,128)(2,1)S(1)} %multiply_convert_fusion.2), channel_id=1, source_target_pairs={{0,3},{1,2},{2,1},{3,0},{4,7},{5,6},{6,5},{7,4},{8,11},{9,10},{10,... | collective-permute-start | bytes 786440 | tf_op jit(solution)/shard_map/ppermute | solution.py:21
  55.0 38.2 %collective-permute-start.9 = (bf16[512,1024]{1,0:T(8,128)(2,1)S(1)}, bf16[512,1024]{1,0:T(8,128)(2,1)}, u32[]{:S(2)}, u32[]{:S(2)}) collective-permute-start(bf16[512,1024]{1,0:T(8,128)(2,1)S(1)} %pad_maximum_fusion.refs_1_), channel_id=1, source_target_pairs={{28,0},{0,4},{4,8},{8,12},{12,16},{16,20},{20,24},{24,28},{29,1},{... | collective-permute-start | bytes 3145736 | tf_op jit(solution)/shard_map/ppermute | solution.py:375
  107.0 43.6 %collective-permute-start.10 = (bf16[2,1024,1024]{2,1,0:T(8,128)(2,1)}, bf16[2,1024,1024]{2,1,0:T(8,128)(2,1)}, u32[]{:S(2)}, u32[]{:S(2)}) collective-permute-start(bf16[2,1024,1024]{2,1,0:T(8,128)(2,1)} %get-tuple-element.57), channel_id=1, source_target_pairs={{0,4},{8,12},{16,20},{24,28},{1,5},{9,13},{17,21},{25,29},{2,6},{1... | collective-permute-start | bytes 12582920 | tf_op jit(solution)/shard_map/ppermute | solution.py:375
  110.3 69.9 %collective-permute-start.11 = (bf16[2,1024,1024]{2,1,0:T(8,128)(2,1)}, bf16[2,1024,1024]{2,1,0:T(8,128)(2,1)}, u32[]{:S(2)}, u32[]{:S(2)}) collective-permute-start(bf16[2,1024,1024]{2,1,0:T(8,128)(2,1)} %get-tuple-element.58), channel_id=1, source_target_pairs={{24,0},{0,8},{8,16},{16,24},{25,1},{1,9},{9,17},{17,25},{26,2},{2,... | collective-permute-start | bytes 12582920 | tf_op jit(solution)/shard_map/ppermute | solution.py:375
  126.0 9.9 %collective-permute-start.13 = (bf16[128,1024]{1,0:T(8,128)(2,1)S(1)}, bf16[128,1024]{1,0:T(8,128)(2,1)}, u32[]{:S(2)}, u32[]{:S(2)}) collective-permute-start(bf16[128,1024]{1,0:T(8,128)(2,1)S(1)} %get-tuple-element.64), channel_id=1, source_target_pairs={{0,2},{1,3},{2,0},{3,1},{4,6},{5,7},{6,4},{7,5},{8,10},{9,11},{10,... | collective-permute-start | bytes 786440 | tf_op jit(solution)/shard_map/ppermute | solution.py:21
  149.9 15.8 %collective-permute-start.18 = (bf16[512,1024]{1,0:T(8,128)(2,1)S(1)}, bf16[512,1024]{1,0:T(8,128)(2,1)S(1)}, u32[]{:S(2)}, u32[]{:S(2)}) collective-permute-start(bf16[512,1024]{1,0:T(8,128)(2,1)S(1)} %pad_maximum_fusion.1.refs_2_), channel_id=1, source_target_pairs={{28,4},{4,12},{12,20},{20,28},{29,5},{5,13},{13,21},{21,29},{30,6}... | collective-permute-start | bytes 3145736 | tf_op jit(solution)/shard_map/ppermute | solution.py:375
  180.3 14.7 %collective-permute-start.19 = (bf16[2,1024,1024]{2,1,0:T(8,128)(2,1)}, bf16[2,1024,1024]{2,1,0:T(8,128)(2,1)}, u32[]{:S(2)}, u32[]{:S(2)}) collective-permute-start(bf16[2,1024,1024]{2,1,0:T(8,128)(2,1)} %shard_map.94), channel_id=1, source_target_pairs={{0,4},{8,12},{16,20},{24,28},{1,5},{9,13},{17,21},{25,29},{2,6},{1... | collective-permute-start | bytes 12582920 | tf_op jit(solution)/shard_map/ppermute | solution.py:375
  189.9 52.5 %collective-permute-start.20 = (bf16[2,1024,1024]{2,1,0:T(8,128)(2,1)}, bf16[2,1024,1024]{2,1,0:T(8,128)(2,1)}, u32[]{:S(2)}, u32[]{:S(2)}) collective-permute-start(bf16[2,1024,1024]{2,1,0:T(8,128)(2,1)} %shard_map.93.refs_1_), channel_id=1, source_target_pairs={{24,0},{0,8},{8,16},{16,24},{25,1},{1,9},{9,17},{17,25},{26,2},{2,... | collective-permute-start | bytes 12582920 | tf_op jit(solution)/shard_map/ppermute | solution.py:375
  297.2 13.5 %collective-permute-start.30 = (bf16[256,1024]{1,0:T(8,128)(2,1)S(1)}, bf16[256,1024]{1,0:T(8,128)(2,1)}, u32[]{:S(2)}, u32[]{:S(2)}) collective-permute-start(bf16[256,1024]{1,0:T(8,128)(2,1)S(1)} %get-tuple-element.106), channel_id=1, source_target_pairs={{0,8},{4,12},{24,16},{28,20},{1,9},{5,13},{25,17},{29,21},{2,10},{... | collective-permute-start | bytes 1572872 | tf_op jit(solution)/shard_map/ppermute | solution.py:308
  299.3 22.7 %collective-permute-start.32 = (bf16[256,1024]{1,0:T(8,128)(2,1)S(1)}, bf16[256,1024]{1,0:T(8,128)(2,1)S(1)}, u32[]{:S(2)}, u32[]{:S(2)}) collective-permute-start(bf16[256,1024]{1,0:T(8,128)(2,1)S(1)} %get-tuple-element.103), channel_id=1, source_target_pairs={{0,8},{4,12},{24,16},{28,20},{1,9},{5,13},{25,17},{29,21},{2,10},{... | collective-permute-start | bytes 1572872 | tf_op jit(solution)/shard_map/ppermute | solution.py:308
  300.6 32.6 %collective-permute-start.33 = (bf16[256,1024]{1,0:T(8,128)(2,1)S(1)}, bf16[256,1024]{1,0:T(8,128)(2,1)}, u32[]{:S(2)}, u32[]{:S(2)}) collective-permute-start(bf16[256,1024]{1,0:T(8,128)(2,1)S(1)} %get-tuple-element.107), channel_id=1, source_target_pairs={{0,8},{4,12},{24,16},{28,20},{1,9},{5,13},{25,17},{29,21},{2,10},{... | collective-permute-start | bytes 1572872 | tf_op jit(solution)/shard_map/ppermute | solution.py:308
  312.0 21.2 %collective-permute-start.31 = (bf16[256,1024]{1,0:T(8,128)(2,1)S(1)}, bf16[256,1024]{1,0:T(8,128)(2,1)}, u32[]{:S(2)}, u32[]{:S(2)}) collective-permute-start(bf16[256,1024]{1,0:T(8,128)(2,1)S(1)} %fusion.1), channel_id=1, source_target_pairs={{8,16},{12,20},{16,8},{20,12},{9,17},{13,21},{17,9},{21,13},{10,18... | collective-permute-start | bytes 1572872 | tf_op jit(solution)/shard_map/ppermute | solution.py:308
  313.4 30.5 %collective-permute-start.28 = (bf16[256,1024]{1,0:T(8,128)(2,1)S(1)}, bf16[256,1024]{1,0:T(8,128)(2,1)}, u32[]{:S(2)}, u32[]{:S(2)}) collective-permute-start(bf16[256,1024]{1,0:T(8,128)(2,1)S(1)} %get-tuple-element.102), channel_id=1, source_target_pairs={{0,8},{4,12},{24,16},{28,20},{1,9},{5,13},{25,17},{29,21},{2,10},{... | collective-permute-start | bytes 1572872 | tf_op jit(solution)/shard_map/ppermute | solution.py:308
  336.1 15.1 %collective-permute-start.35 = (bf16[256,1024]{1,0:T(8,128)(2,1)S(1)}, bf16[256,1024]{1,0:T(8,128)(2,1)S(1)}, u32[]{:S(2)}, u32[]{:S(2)}) collective-permute-start(bf16[256,1024]{1,0:T(8,128)(2,1)S(1)} %get-tuple-element.99), channel_id=1, source_target_pairs={{8,0},{12,4},{16,24},{20,28},{9,1},{13,5},{17,25},{21,29},{10,2},{... | collective-permute-start | bytes 1572872 | tf_op jit(solution)/shard_map/ppermute | solution.py:308
  337.4 13.8 %collective-permute-start.36 = (bf16[256,1024]{1,0:T(8,128)(2,1)S(1)}, bf16[256,1024]{1,0:T(8,128)(2,1)S(1)}, u32[]{:S(2)}, u32[]{:S(2)}) collective-permute-start(bf16[256,1024]{1,0:T(8,128)(2,1)S(1)} %get-tuple-element.100), channel_id=1, source_target_pairs={{8,16},{12,20},{16,8},{20,12},{9,17},{13,21},{17,9},{21,13},{10,18... | collective-permute-start | bytes 1572872 | tf_op jit(solution)/shard_map/ppermute | solution.py:308
  338.1 14.7 %collective-permute-start.37 = (bf16[256,1024]{1,0:T(8,128)(2,1)}, bf16[256,1024]{1,0:T(8,128)(2,1)}, u32[]{:S(2)}, u32[]{:S(2)}) collective-permute-start(bf16[256,1024]{1,0:T(8,128)(2,1)} %get-tuple-element.101), channel_id=1, source_target_pairs={{8,16},{12,20},{16,8},{20,12},{9,17},{13,21},{17,9},{21,13},{10,18... | collective-permute-start | bytes 1572872 | tf_op jit(solution)/shard_map/ppermute | solution.py:308
  356.6 28.3 %collective-permute-start.41 = (bf16[256,1024]{1,0:T(8,128)(2,1)S(1)}, bf16[256,1024]{1,0:T(8,128)(2,1)S(1)}, u32[]{:S(2)}, u32[]{:S(2)}) collective-permute-start(bf16[256,1024]{1,0:T(8,128)(2,1)S(1)} %get-tuple-element.97), channel_id=1, source_target_pairs={{8,0},{12,4},{16,24},{20,28},{9,1},{13,5},{17,25},{21,29},{10,2},{... | collective-permute-start | bytes 1572872 | tf_op jit(solution)/shard_map/ppermute | solution.py:308
  387.4 16.2 %collective-permute-start.40 = (bf16[256,1024]{1,0:T(8,128)(2,1)S(1)}, bf16[256,1024]{1,0:T(8,128)(2,1)S(1)}, u32[]{:S(2)}, u32[]{:S(2)}) collective-permute-start(bf16[256,1024]{1,0:T(8,128)(2,1)S(1)} %get-tuple-element.96), channel_id=1, source_target_pairs={{8,0},{12,4},{16,24},{20,28},{9,1},{13,5},{17,25},{21,29},{10,2},{... | collective-permute-start | bytes 1572872 | tf_op jit(solution)/shard_map/ppermute | solution.py:308
  404.4 16.2 %collective-permute-start.39 = (bf16[256,1024]{1,0:T(8,128)(2,1)S(1)}, bf16[256,1024]{1,0:T(8,128)(2,1)S(1)}, u32[]{:S(2)}, u32[]{:S(2)}) collective-permute-start(bf16[256,1024]{1,0:T(8,128)(2,1)S(1)} %get-tuple-element.94), channel_id=1, source_target_pairs={{8,0},{12,4},{16,24},{20,28},{9,1},{13,5},{17,25},{21,29},{10,2},{... | collective-permute-start | bytes 1572872 | tf_op jit(solution)/shard_map/ppermute | solution.py:308
  (61 other events, 327.3 us)
